TPU v7x, 32 devices: a whole 2x2x4 slice. The times are simulated.
32 devices in a mesh: seq: 16 (over z, y, x), tp: 2 (over core).
Axes of the slice: x: 2, y: 2, z: 4, core: 2. Of those that a mesh axis runs over, the one named last changes fastest.
Arguments:
- stream: float32 [2048, 2048], P('seq'), may hold values from -6 to 6
- doc_ids: int32 [2048], P('seq'), may hold values from 0 to 4, as said below
- project: bfloat16 [2048, 3, 2048], P('seq', None, 'tp'), may hold values from -0.125 to 0.125
- project_bias: float32 [3, 2048], P(None, 'tp'), may hold values from -3 to 3
- combine: bfloat16 [2048, 2048], P('seq', 'tp'), may hold values from -0.125 to 0.125
- combine_bias: float32 [2048], replicated, may hold values from -3 to 3
- expand: bfloat16 [2048, 8192], P('seq', 'tp'), may hold values from -0.125 to 0.125
- expand_bias: float32 [8192], P('tp'), may hold values from -3 to 3
- shrink: bfloat16 [2048, 8192], P('seq', 'tp'), may hold values from -0.0625 to 0.0625
- shrink_bias: float32 [2048], replicated, may hold values from -3 to 3
- first_gain: float32 [2048], replicated, may hold values from 0.25 to 1.75
- first_bias: float32 [2048], replicated, may hold values from -2 to 2
- inner_gain: float32 [2048], P('tp'), may hold values from 0.25 to 1.75
- inner_bias: float32 [2048], P('tp'), may hold values from -2 to 2
- second_gain: float32 [2048], replicated, may hold values from 0.25 to 1.75
- second_bias: float32 [2048], replicated, may hold values from -2 to 2
- hidden_gain: float32 [8192], P('tp'), may hold values from 0.25 to 1.75
- hidden_bias: float32 [8192], P('tp'), may hold values from -2 to 2
- out_grad: float32 [2048, 2048], P('seq'), may hold values from -18 to 18
Outputs:
- output: float32 [2048, 2048], P('seq')
- stream_grad: float32 [2048, 2048], P('seq')
- project_grad: float32 [2048, 3, 2048], P('seq', None, 'tp')
- project_bias_grad: float32 [3, 2048], P(None, 'tp')
- combine_grad: float32 [2048, 2048], P('seq', 'tp')
- combine_bias_grad: float32 [2048], replicated
- expand_grad: float32 [2048, 8192], P('seq', 'tp')
- expand_bias_grad: float32 [8192], P('tp')
- shrink_grad: float32 [2048, 8192], P('seq', 'tp')
- shrink_bias_grad: float32 [2048], replicated
- first_gain_grad: float32 [2048], replicated
- first_bias_grad: float32 [2048], replicated
- inner_gain_grad: float32 [2048], P('tp')
- inner_bias_grad: float32 [2048], P('tp')
- second_gain_grad: float32 [2048], replicated
- second_bias_grad: float32 [2048], replicated
- hidden_gain_grad: float32 [8192], P('tp')
- hidden_bias_grad: float32 [8192], P('tp')
Inputs may be any that keep to these rules, and one draw needn't show every extreme that they name: `doc_ids`: never falling along the stream; every number of 0 to 4 occurs; document 2 begins within the first 128 tokens and ends within the last 128.
All inputs are finite; a program needn't handle non-finite values.
Results may differ from a plain program's by a relative error of at most 0.015.
Values may be sent and summed in bfloat16 or wider, within the bound.
No kernel may reach another device: no remote copies, remote signals or barrier semaphores. Data moves between devices by JAX's collectives and lax.ppermute only.
A program may use at most 320 MiB of HBM per device.

v0:
```python
from functools import partial
import math

import jax
import jax.numpy as jnp
from jax import lax
from jax.sharding import PartitionSpec as P

D = 2048
HDIM = 64
FF = 8192
DOCS = 5
SCALE_BASE = 512


EPSILON = 1e-05
NEGATIVE = -1e30
CONTRACT_LAST = (((1,), (1,)), ((), ()))
CONTRACT_FIRST = (((0,), (0,)), ((), ()))


def doubled(values_in):
    return jnp.concatenate([values_in, values_in], axis=-1)


def tables(positions, center):
    half_dim = HDIM // 2
    column = jnp.arange(half_dim, dtype=jnp.float32)
    frequency = jnp.exp(column * (-2.0 * math.log(10000.0) / HDIM))
    base_ratio = (2.0 * column + 0.4 * HDIM) / (1.4 * HDIM)
    location = positions.astype(jnp.float32)
    phase_angle = location[:, None] * frequency[None, :]
    exponent = ((location - center) / SCALE_BASE)[:, None] * jnp.log(base_ratio)[None, :]
    return (
        doubled(jnp.cos(phase_angle)),
        doubled(jnp.sin(phase_angle)),
        doubled(jnp.exp(exponent)),
    )


def turn_pairs(values, cosine, sine_table):
    half_dim = values.shape[-1] // 2
    swapped = jnp.concatenate([-values[..., half_dim:], values[..., :half_dim]], axis=-1)
    return values * cosine[:, None, :] + swapped * sine_table[:, None, :]


def place_query(values, cosine, sine_table, growth):
    return turn_pairs(values, cosine, sine_table) * growth[:, None, :] * HDIM ** (-0.5)


def place_key(values, cosine, sine_table, growth):
    return turn_pairs(values, cosine, sine_table) / growth[:, None, :]


def norm_full(values, gain_vector, shift_vector):
    average = jnp.mean(values, axis=-1, keepdims=True)
    inv_scale = lax.rsqrt(
        jnp.mean(values * values, axis=-1, keepdims=True) - average * average + EPSILON
    )
    normed = (values - average) * inv_scale
    return (normed * gain_vector + shift_vector, normed, inv_scale)


def norm_full_back(incoming, normed, inv_scale, gain_vector):
    scaled_grad = incoming * gain_vector
    first_mean = jnp.mean(scaled_grad, axis=-1, keepdims=True)
    cross_mean = jnp.mean(scaled_grad * normed, axis=-1, keepdims=True)
    return inv_scale * (scaled_grad - first_mean - normed * cross_mean)


def split_sums(first_term, second_term):
    return lax.psum((first_term, second_term), "tp")


def norm_split(values, gain_vector, shift_vector, full_width):
    totals, squares = split_sums(
        jnp.sum(values, axis=-1, keepdims=True), jnp.sum(values * values, axis=-1, keepdims=True)
    )
    average = totals / full_width
    inv_scale = lax.rsqrt(squares / full_width - average * average + EPSILON)
    normed = (values - average) * inv_scale
    return (normed * gain_vector + shift_vector, normed, inv_scale)


def norm_split_back(incoming, normed, inv_scale, gain_vector, full_width):
    scaled_grad = incoming * gain_vector
    totals, crossed = split_sums(
        jnp.sum(scaled_grad, axis=-1, keepdims=True),
        jnp.sum(scaled_grad * normed, axis=-1, keepdims=True),
    )
    return inv_scale * (scaled_grad - totals / full_width - normed * (crossed / full_width))


def branch_total(values):
    return lax.psum(values, "tp")


def doc_of(token_rows, starts):
    return jnp.sum((token_rows[:, None] >= starts[None, 1:]).astype(jnp.int32), axis=1)


def keep_state(state_in):
    return state_in


def gelu_exact(values):
    return jax.nn.gelu(values, approximate=False)


def shards(
    stream,
    doc_ids,
    project,
    project_bias,
    combine,
    combine_bias,
    expand,
    expand_bias,
    shrink,
    shrink_bias,
    first_gain,
    first_bias,
    inner_gain,
    inner_bias,
    second_gain,
    second_bias,
    hidden_gain,
    hidden_bias,
    out_grad,
):
    local_count = stream.shape[0]
    head_width = project.shape[2]
    head_count = head_width // HDIM
    token_rows = lax.axis_index("seq") * local_count + jnp.arange(local_count, dtype=jnp.int32)
    center = lax.axis_size("seq") * local_count // 2
    member = (doc_ids[:, None] == jnp.arange(DOCS, dtype=jnp.int32)[None, :]).astype(jnp.int32)
    counts = lax.psum(jnp.sum(member, axis=0), "seq")
    starts = jnp.cumsum(counts) - counts
    positions = token_rows - jnp.sum(member * starts[None, :], axis=1)
    cosine, sine_table, growth = tables(positions, center)
    first_row = token_rows[0]
    last_row = token_rows[local_count - 1]
    first_doc = doc_ids[0]
    last_doc = doc_ids[local_count - 1]
    full_project, full_combine, full_expand, full_shrink = (
        lax.all_gather(project, "seq", axis=0, tiled=True),
        lax.all_gather(combine, "seq", axis=0, tiled=True),
        lax.all_gather(expand, "seq", axis=0, tiled=True),
        lax.all_gather(shrink, "seq", axis=0, tiled=True),
    )
    first_out, first_normed, first_scale = norm_full(stream, first_gain, first_bias)
    normed_in = first_out.astype(jnp.bfloat16)
    triple = (
        jnp.einsum("td,dch->tch", normed_in, full_project, preferred_element_type=jnp.float32)
        + project_bias[None]
    )
    head_shape = (local_count, head_count, HDIM)
    query_raw = triple[:, 0].reshape(head_shape)
    key_raw = triple[:, 1].reshape(head_shape)
    queries = place_query(query_raw, cosine, sine_table, growth).astype(jnp.bfloat16)
    keyed = place_key(key_raw, cosine, sine_table, growth).astype(jnp.bfloat16)
    valued = triple[:, 2].reshape(head_shape).astype(jnp.bfloat16)
    start_state = (
        jnp.full((head_count, local_count), NEGATIVE, jnp.float32),
        jnp.zeros((head_count, local_count), jnp.float32),
        jnp.zeros((head_count, local_count, HDIM), jnp.float32),
    )
    key_part = lax.all_gather(keyed.reshape(local_count, head_width), "seq", axis=0, tiled=True)
    value_part = lax.all_gather(valued.reshape(local_count, head_width), "seq", axis=0, tiled=True)
    piece_rows = key_part.shape[0]
    key_rows = jnp.arange(piece_rows, dtype=jnp.int32)
    key_docs = doc_of(key_rows, starts)
    skipped = (jnp.int32(0) > last_row) | (key_docs[piece_rows - 1] < first_doc)

    def attend_compute(state):
        running_max, running_sum, summed = state
        key_block = key_part.reshape(piece_rows, head_count, HDIM)
        value_block = value_part.reshape(piece_rows, head_count, HDIM)
        allowed = (
            (key_rows[None, :] <= token_rows[:, None]) & (key_docs[None, :] == doc_ids[:, None])
        )[None]
        scores = jnp.einsum("qhd,khd->hqk", queries, key_block, preferred_element_type=jnp.float32)
        scores = jnp.where(allowed, scores, NEGATIVE)
        newest = jnp.maximum(running_max, jnp.max(scores, axis=-1))
        weights_raw = jnp.where(allowed, jnp.exp(scores - newest[..., None]), 0.0)
        running_sum = jnp.sum(weights_raw, axis=-1)
        summed = jnp.einsum(
            "hqk,khd->hqd",
            weights_raw.astype(jnp.bfloat16),
            value_block,
            preferred_element_type=jnp.float32,
        )
        return (newest, running_sum, summed)

    running_max, running_sum, summed = lax.cond(skipped, keep_state, attend_compute, start_state)
    mixture = jnp.transpose(summed / running_sum[..., None], (1, 0, 2)).reshape(
        local_count, head_width
    )
    log_total = running_max + jnp.log(running_sum)
    inner_out, inner_normed, inner_scale = norm_split(mixture, inner_gain, inner_bias, D)
    combined_in = inner_out.astype(jnp.bfloat16)
    middle = (
        stream
        + branch_total(
            lax.dot_general(
                combined_in, full_combine, CONTRACT_LAST, preferred_element_type=jnp.float32
            )
        )
        + combine_bias
    )
    second_out, second_normed, second_scale = norm_full(middle, second_gain, second_bias)
    expand_in = second_out.astype(jnp.bfloat16)
    raised = jnp.dot(expand_in, full_expand, preferred_element_type=jnp.float32) + expand_bias
    active, gelu_back = jax.vjp(gelu_exact, raised)
    hidden_out, hidden_normed, hidden_scale = norm_split(active, hidden_gain, hidden_bias, FF)
    shrink_in = hidden_out.astype(jnp.bfloat16)
    output = (
        middle
        + branch_total(
            lax.dot_general(
                shrink_in, full_shrink, CONTRACT_LAST, preferred_element_type=jnp.float32
            )
        )
        + shrink_bias
    )
    back_project, back_combine, back_expand, back_shrink = (
        lax.all_gather(project, "seq", axis=0, tiled=True),
        lax.all_gather(combine, "seq", axis=0, tiled=True),
        lax.all_gather(expand, "seq", axis=0, tiled=True),
        lax.all_gather(shrink, "seq", axis=0, tiled=True),
    )
    shrink_bias_grad = jnp.sum(out_grad, axis=0)
    low_out = out_grad.astype(jnp.bfloat16)
    shrink_term = lax.dot_general(
        low_out, shrink_in, CONTRACT_FIRST, preferred_element_type=jnp.float32
    )
    hidden_grad = jnp.dot(low_out, back_shrink, preferred_element_type=jnp.float32)
    hidden_gain_grad = jnp.sum(hidden_grad * hidden_normed, axis=0)
    hidden_bias_grad = jnp.sum(hidden_grad, axis=0)
    active_grad = norm_split_back(hidden_grad, hidden_normed, hidden_scale, hidden_gain, FF)
    (raised_grad,) = gelu_back(active_grad)
    expand_bias_grad = jnp.sum(raised_grad, axis=0)
    low_raised = raised_grad.astype(jnp.bfloat16)
    expand_term = lax.dot_general(
        expand_in, low_raised, CONTRACT_FIRST, preferred_element_type=jnp.float32
    )
    second_grad = branch_total(
        lax.dot_general(low_raised, back_expand, CONTRACT_LAST, preferred_element_type=jnp.float32)
    )
    second_gain_grad = jnp.sum(second_grad * second_normed, axis=0)
    second_bias_grad = jnp.sum(second_grad, axis=0)
    middle_grad = out_grad + norm_full_back(second_grad, second_normed, second_scale, second_gain)
    combine_bias_grad = jnp.sum(middle_grad, axis=0)
    low_middle = middle_grad.astype(jnp.bfloat16)
    combine_term = lax.dot_general(
        low_middle, combined_in, CONTRACT_FIRST, preferred_element_type=jnp.float32
    )
    inner_grad = jnp.dot(low_middle, back_combine, preferred_element_type=jnp.float32)
    inner_gain_grad = jnp.sum(inner_grad * inner_normed, axis=0)
    inner_bias_grad = jnp.sum(inner_grad, axis=0)
    mixture_grad = norm_split_back(inner_grad, inner_normed, inner_scale, inner_gain, D)
    low_mixture = mixture_grad.astype(jnp.bfloat16)
    low_mixture3 = low_mixture.reshape(head_shape)
    delta = jnp.sum(low_mixture3.astype(jnp.float32) * mixture.reshape(head_shape), axis=-1)
    delta_heads = delta.T
    zero_heads = jnp.zeros(head_shape, jnp.float32)
    query_key_part = lax.all_gather(
        keyed.reshape(local_count, head_width), "seq", axis=0, tiled=True
    )
    query_value_part = lax.all_gather(
        valued.reshape(local_count, head_width), "seq", axis=0, tiled=True
    )
    query_piece_rows = query_key_part.shape[0]
    query_key_rows = jnp.arange(query_piece_rows, dtype=jnp.int32)
    query_key_docs = doc_of(query_key_rows, starts)
    skipped = (jnp.int32(0) > last_row) | (query_key_docs[query_piece_rows - 1] < first_doc)

    def query_compute(gathered):
        key_block = query_key_part.reshape(query_piece_rows, head_count, HDIM)
        value_block = query_value_part.reshape(query_piece_rows, head_count, HDIM)
        allowed = (
            (query_key_rows[None, :] <= token_rows[:, None])
            & (query_key_docs[None, :] == doc_ids[:, None])
        )[None]
        scores = jnp.einsum("qhd,khd->hqk", queries, key_block, preferred_element_type=jnp.float32)
        probability = jnp.where(allowed, jnp.exp(scores - log_total[..., None]), 0.0)
        pushes = jnp.einsum(
            "qhd,khd->hqk", low_mixture3, value_block, preferred_element_type=jnp.float32
        )
        dscore = (probability * (pushes - delta_heads[..., None])).astype(jnp.bfloat16)
        return jnp.einsum("hqk,khd->qhd", dscore, key_block, preferred_element_type=jnp.float32)

    query_grad3 = lax.cond(skipped, keep_state, query_compute, zero_heads)
    query_part = lax.all_gather(
        queries.astype(jnp.float32).reshape(local_count, head_width), "seq", axis=0, tiled=True
    )
    pull_part = lax.all_gather(low_mixture.astype(jnp.float32), "seq", axis=0, tiled=True)
    total_part = lax.all_gather(log_total.T, "seq", axis=0, tiled=True)
    delta_part = lax.all_gather(delta, "seq", axis=0, tiled=True)
    key_piece_rows = query_part.shape[0]
    query_rows = jnp.arange(key_piece_rows, dtype=jnp.int32)
    query_docs = doc_of(query_rows, starts)
    skipped = (query_rows[key_piece_rows - 1] < first_row) | (query_docs[0] > last_doc)

    def key_compute(state):
        query_block = query_part.astype(jnp.bfloat16).reshape(key_piece_rows, head_count, HDIM)
        pull_block = pull_part.astype(jnp.bfloat16).reshape(key_piece_rows, head_count, HDIM)
        allowed = (
            (token_rows[None, :] <= query_rows[:, None]) & (doc_ids[None, :] == query_docs[:, None])
        )[None]
        scores = jnp.einsum("qhd,khd->hqk", query_block, keyed, preferred_element_type=jnp.float32)
        probability = jnp.where(allowed, jnp.exp(scores - total_part.T[..., None]), 0.0)
        pushes = jnp.einsum("qhd,khd->hqk", pull_block, valued, preferred_element_type=jnp.float32)
        dscore = (probability * (pushes - delta_part.T[..., None])).astype(jnp.bfloat16)
        key_acc = jnp.einsum(
            "hqk,qhd->khd", dscore, query_block, preferred_element_type=jnp.float32
        )
        value_acc = jnp.einsum(
            "hqk,qhd->khd",
            probability.astype(jnp.bfloat16),
            pull_block,
            preferred_element_type=jnp.float32,
        )
        return (key_acc, value_acc)

    key_grad3, value_grad3 = lax.cond(skipped, keep_state, key_compute, (zero_heads, zero_heads))
    _, query_back = jax.vjp(
        partial(place_query, cosine=cosine, sine_table=sine_table, growth=growth), query_raw
    )
    _, key_back = jax.vjp(
        partial(place_key, cosine=cosine, sine_table=sine_table, growth=growth), key_raw
    )
    (query_grad,) = query_back(query_grad3)
    (key_grad,) = key_back(key_grad3)
    triple_grad = jnp.stack(
        [
            query_grad.reshape(local_count, head_width),
            key_grad.reshape(local_count, head_width),
            value_grad3.reshape(local_count, head_width),
        ],
        axis=1,
    )
    project_bias_grad = jnp.sum(triple_grad, axis=0)
    low_triple = triple_grad.astype(jnp.bfloat16)
    project_term = jnp.einsum(
        "td,tch->dch", normed_in, low_triple, preferred_element_type=jnp.float32
    )
    first_grad = branch_total(
        jnp.einsum("tch,dch->td", low_triple, back_project, preferred_element_type=jnp.float32)
    )
    first_gain_grad = jnp.sum(first_grad * first_normed, axis=0)
    first_bias_grad = jnp.sum(first_grad, axis=0)
    stream_grad = middle_grad + norm_full_back(first_grad, first_normed, first_scale, first_gain)
    project_grad, combine_grad, expand_grad, shrink_grad = (
        lax.psum_scatter(project_term, "seq", scatter_dimension=0, tiled=True),
        lax.psum_scatter(combine_term, "seq", scatter_dimension=0, tiled=True),
        lax.psum_scatter(expand_term, "seq", scatter_dimension=0, tiled=True),
        lax.psum_scatter(shrink_term, "seq", scatter_dimension=0, tiled=True),
    )
    (
        first_gain_grad,
        first_bias_grad,
        project_bias_grad,
        inner_gain_grad,
        inner_bias_grad,
        combine_bias_grad,
        second_gain_grad,
        second_bias_grad,
        expand_bias_grad,
        hidden_gain_grad,
        hidden_bias_grad,
        shrink_bias_grad,
    ) = lax.psum(
        (
            first_gain_grad,
            first_bias_grad,
            project_bias_grad,
            inner_gain_grad,
            inner_bias_grad,
            combine_bias_grad,
            second_gain_grad,
            second_bias_grad,
            expand_bias_grad,
            hidden_gain_grad,
            hidden_bias_grad,
            shrink_bias_grad,
        ),
        "seq",
    )
    return (
        output,
        stream_grad,
        project_grad,
        project_bias_grad,
        combine_grad,
        combine_bias_grad,
        expand_grad,
        expand_bias_grad,
        shrink_grad,
        shrink_bias_grad,
        first_gain_grad,
        first_bias_grad,
        inner_gain_grad,
        inner_bias_grad,
        second_gain_grad,
        second_bias_grad,
        hidden_gain_grad,
        hidden_bias_grad,
    )


def solution(mesh):
    return jax.shard_map(
        shards,
        mesh=mesh,
        in_specs=(
            P("seq", None),
            P("seq"),
            P("seq", None, "tp"),
            P(None, "tp"),
            P("seq", "tp"),
            P(),
            P("seq", "tp"),
            P("tp"),
            P("seq", "tp"),
            P(),
            P(),
            P(),
            P("tp"),
            P("tp"),
            P(),
            P(),
            P("tp"),
            P("tp"),
            P("seq", None),
        ),
        out_specs=(
            P("seq", None),
            P("seq", None),
            P("seq", None, "tp"),
            P(None, "tp"),
            P("seq", "tp"),
            P(),
            P("seq", "tp"),
            P("tp"),
            P("seq", "tp"),
            P(),
            P(),
            P(),
            P("tp"),
            P("tp"),
            P(),
            P(),
            P("tp"),
            P("tp"),
        ),
        check_vma=False,
    )
```

profile of v0, /device:TPU:1, one launch (start us, length us, event | category | flops | bytes accessed | tf_op | source)
XLA Modules:
  0.0 3362.1 jit_solution(15419482670065295772)
XLA Ops:
  24.1 140.3 %all-gather.10.cloned.1.call-done = bf16[2048,3,1024]{2,0,1:T(8,128)(2,1)} async-done(((bf16[128,3,1024]{2,0,1:T(8,128)(2,1)}), bf16[2048,3,1024]{2,0,1:T(8,128)(2,1)}) %all-gather.10.cloned.1.call-update) | async-done | bytes 12582928 | tf_op jit(solution)/shard_map/all_gather | solution.py:146
  192.2 65.7 %all-gather.12.cloned.1.call-done = bf16[2048,1024]{1,0:T(8,128)(2,1)} async-done(((bf16[128,1024]{1,0:T(8,128)(2,1)}), bf16[2048,1024]{1,0:T(8,128)(2,1)}) %all-gather.12.cloned.1.call-update) | async-done | bytes 4194320 | tf_op jit(solution)/shard_map/all_gather | solution.py:168
  257.9 77.5 %all-gather.24.cloned.1.call-done = bf16[2048,1,1024]{2,0,1:T(8,128)(2,1)} async-done(((bf16[128,1,1024]{2,0,1:T(8,128)(2,1)}), bf16[2048,1,1024]{2,0,1:T(8,128)(2,1)}) %all-gather.24.cloned.1.call-update) | async-done | bytes 4194320 | tf_op jit(solution)/shard_map/all_gather | solution.py:169
  335.4 33.8 %conditional.3 = (f32[16,128]{1,0:T(8,128)S(1)}, f32[16,128]{1,0:T(8,128)S(1)}, f32[16,128,64]{1,2,0:T(8,128)S(1)}, f32[16,128]{1,0:T(8,128)S(1)}) conditional(s32[]{:T(128)} %bitcast.15, (s32[2048]{0:T(1024)S(1)}, s32[128]{0:T(128)}, s32[2048]{0:T(1024)}, s32[128]{0:T(128)S(1)}, bf16[2048,1024]{1,0:T(8,128)(2,1)}, ...), branch_computations={%region_7.10_spmd, %region_10.11_spmd} | conditional | flops 1116469248 | bytes 144524352 | solution.py:195
  374.5 38.2 %all-gather.14.cloned.1.call-done = bf16[2048,1024]{1,0:T(8,128)(2,1)} async-done(((bf16[128,1024]{1,0:T(8,128)(2,1)}), bf16[2048,1024]{1,0:T(8,128)(2,1)}) %all-gather.14.cloned.1.call-update) | async-done | bytes 4194320 | tf_op jit(solution)/shard_map/all_gather | solution.py:147
  418.9 18.6 all-reduce.15.cloned.1.call-done
  440.5 192.1 %all-gather.16.cloned.1.call-done = bf16[2048,4096]{1,0:T(8,128)(2,1)} async-done(((bf16[128,4096]{1,0:T(8,128)(2,1)}), bf16[2048,4096]{1,0:T(8,128)(2,1)}) %all-gather.16.cloned.1.call-update) | async-done | bytes 16777232 | tf_op jit(solution)/shard_map/all_gather | solution.py:148
  632.5 12.9 fusion.63
  650.5 175.0 %all-gather.18.cloned.1.call-done = bf16[2048,4096]{1,0:T(8,128)(2,1)} async-done(((bf16[128,4096]{1,0:T(8,128)(2,1)}), bf16[2048,4096]{1,0:T(8,128)(2,1)}) %all-gather.18.cloned.1.call-update) | async-done | bytes 16777232 | tf_op jit(solution)/shard_map/all_gather | solution.py:149
  861.7 17.2 all-reduce.17.cloned.1.call-done
  896.7 37.4 %all_gather.43 = f32[2048,16]{0,1:T(8,128)} all-gather(f32[128,16]{0,1:T(8,128)S(1)} %bitcast.160), channel_id=1, replica_groups=mesh['seq'=16,'tp'=2] {'seq'}, dimensions={0}, use_global_device_ids=true | all-gather | bytes 139264 | tf_op jit(solution)/shard_map/all_gather | solution.py:298
  950.7 40.7 %conditional.4 = (f32[128,16,64]{0,2,1:T(8,128)}) conditional(s32[]{:T(128)} %bitcast.15, (s32[2048]{0:T(1024)}, s32[128]{0:T(128)}, s32[2048]{0:T(1024)}, s32[128]{0:T(128)}, bf16[2048,1024]{1,0:T(8,128)(2,1)}, /*index=5*/bf16[128,16,64]{0,2,1:T(8,128)(2,1)S(1)}, f32[16,128]{1,0:T(8,128)}, bf16[2048,1024]{1,0:T(8,128)(2,1)}, ...), branch_computations={%region_35.36_spmd, %region_36.37_spmd} | conditional | flops 1632370688 | bytes 65604700 | solution.py:293
  975.9 15.5 fusion.11
  991.4 33.2 all_gather.45
  1024.6 13.6 all-gather.22.cloned.1.call-done
  1038.8 56.7 %conditional.5 = (f32[128,16,64]{0,2,1:T(8,128)}, f32[128,1,1024]{2,0,1:T(8,128)}) conditional(s32[]{:T(128)} %bitcast.45, (s32[128]{0:T(128)}, s32[2048]{0:T(1024)}, s32[128]{0:T(128)}, s32[2048]{0:T(1024)}, bf16[2048,1024]{1,0:T(8,128)(2,1)}, /*index=5*/bf16[128,16,64]{0,2,1:T(8,128)(2,1)}, f32[2048,16]{0,1:T(8,128)}, ...), branch_computations={%region_37.38_spmd, %region_38.39_spmd} | conditional | flops 2181824512 | bytes 175820112 | solution.py:326
  1066.7 16.4 multiply_convert_fusion.12
  1113.4 15.5 convolution_bitcast_fusion
  1154.4 14.5 fusion.44
  1173.4 646.9 %reduce-scatter.11.cloned.1.call-done = f32[128,4096]{0,1:T(8,128)} async-done(((f32[2048,4096]{0,1:T(8,128)}), f32[128,4096]{0,1:T(8,128)}) %reduce-scatter.11.cloned.1.call-update) | async-done | bytes 2097168 | tf_op jit(solution)/shard_map/reduce_scatter | solution.py:358
  1823.2 120.9 %all-reduce.19.cloned.1.call-done = (f32[3,1024]{1,0:T(4,128)}, f32[2048]{0:T(1024)}, f32[4096]{0:T(1024)}, f32[2048]{0:T(1024)}, f32[2048]{0:T(1024)}, /*index=...) async-done(((f32[3,1024]{1,0:T(4,128)}, f32[2048]{0:T(1024)}, f32[4096]{0:T(1024)}, ...) | async-done | bytes 118800 | tf_op jit(solution)/shard_map/psum | solution.py:373
  1944.2 181.2 %reduce-scatter.7.cloned.1.call-done = f32[128,1024]{1,0:T(8,128)} async-done(((f32[2048,1024]{1,0:T(8,128)}), f32[128,1024]{1,0:T(8,128)}) %reduce-scatter.7.cloned.1.call-update) | async-done | bytes 524304 | tf_op jit(solution)/shard_map/reduce_scatter | solution.py:356
  2125.4 521.9 %reduce-scatter.5.cloned.1.call-done = f32[128,3,1024]{2,0,1:T(8,128)} async-done(((f32[2048,3,1024]{2,0,1:T(8,128)}), f32[128,3,1024]{2,0,1:T(8,128)}) %reduce-scatter.5.cloned.1.call-update) | async-done | bytes 1572880 | tf_op jit(solution)/shard_map/reduce_scatter | solution.py:355
  2647.3 692.1 %reduce-scatter.9.cloned.1.call-done = f32[128,4096]{1,0:T(8,128)} async-done(((f32[2048,4096]{1,0:T(8,128)}), f32[128,4096]{1,0:T(8,128)}) %reduce-scatter.9.cloned.1.call-update) | async-done | bytes 2097168 | tf_op jit(solution)/shard_map/reduce_scatter | solution.py:357
  (288 shorter events, 295.7 us)
Async XLA Ops:
  7.2 157.2 %all-gather.10.cloned.1.call-start = ((), (), s32[]{:S(2)}) async-start(), calls=%async_computation.4 | async-start | bytes 13369344 | tf_op jit(solution)/shard_map/all_gather | solution.py:146
  7.9 250.0 %all-gather.12.cloned.1.call-start = ((), (), s32[]{:S(2)}) async-start(), calls=%async_computation.5 | async-start | bytes 4456448 | tf_op jit(solution)/shard_map/all_gather | solution.py:168
  21.7 142.7 %copy-start.26 = (f32[3,1024]{1,0:T(4,128)S(1)}, f32[3,1024]{1,0:T(4,128)}, u32[]{:S(2)}) copy-start(f32[3,1024]{1,0:T(4,128)} %param.28) | copy-start | bytes 36868
  21.7 142.7 %copy-start.27 = (f32[2048]{0:T(1024)S(1)}, f32[2048]{0:T(1024)}, u32[]{:S(2)}) copy-start(f32[2048]{0:T(1024)} %param.35) | copy-start | bytes 24580
  21.7 142.7 %copy-start.36 = (f32[2048]{0:T(1024)S(1)}, f32[2048]{0:T(1024)}, u32[]{:S(2)}) copy-start(f32[2048]{0:T(1024)} %param.36) | copy-start | bytes 24580
  24.0 146.9 %copy-start.50 = (f32[128]{0:T(128)}, f32[128]{0:T(128)S(1)}, u32[]{:S(2)}) copy-start(f32[128]{0:T(128)S(1)} %get-tuple-element.352) | copy-start | bytes 1540
  24.0 146.9 %copy-start.52 = (f32[128]{0:T(128)}, f32[128]{0:T(128)S(1)}, u32[]{:S(2)}) copy-start(f32[128]{0:T(128)S(1)} %get-tuple-element.353) | copy-start | bytes 1540
  184.3 151.1 %all-gather.24.cloned.1.call-start = ((), (), s32[]{:S(2)}) async-start(), calls=%async_computation.17 | async-start | bytes 4456448 | tf_op jit(solution)/shard_map/all_gather | solution.py:169
  185.1 227.6 %all-gather.14.cloned.1.call-start = ((), (), s32[]{:S(2)}) async-start(), calls=%async_computation.6 | async-start | bytes 4456448 | tf_op jit(solution)/shard_map/all_gather | solution.py:147
  185.7 251.8 %all-reduce.15.cloned.1.call-start = ((), (), s32[]{:S(2)}) async-start(), calls=%async_computation.7 | async-start | bytes 2097152 | tf_op jit(solution)/shard_map/psum | solution.py:95
  369.2 48.3 %copy-start.30 = (f32[16,128]{1,0:T(8,128)}, f32[16,128]{1,0:T(8,128)S(1)}, u32[]{:S(2)}) copy-start(f32[16,128]{1,0:T(8,128)S(1)} %get-tuple-element.114) | copy-start | bytes 24580
  369.4 48.1 %copy-start.13 = (f32[16,128,64]{1,2,0:T(8,128)}, f32[16,128,64]{1,2,0:T(8,128)S(1)}, u32[]{:S(2)}) copy-start(f32[16,128,64]{1,2,0:T(8,128)S(1)} %get-tuple-element.308) | copy-start | bytes 1572868
  417.6 215.0 %all-gather.16.cloned.1.call-start = ((), (), s32[]{:S(2)}) async-start(), calls=%async_computation.8 | async-start | bytes 17825792 | tf_op jit(solution)/shard_map/all_gather | solution.py:148
  418.1 407.4 %all-gather.18.cloned.1.call-start = ((), (), s32[]{:S(2)}) async-start(), calls=%async_computation.9 | async-start | bytes 17825792 | tf_op jit(solution)/shard_map/all_gather | solution.py:149
  418.9 460.1 %all-reduce.17.cloned.1.call-start = ((), (), s32[]{:S(2)}) async-start(), calls=%async_computation.10 | async-start | bytes 2097152 | tf_op jit(solution)/shard_map/psum | solution.py:95
  632.5 193.0 %copy-start.22 = (f32[4096]{0:T(1024)S(1)}, f32[4096]{0:T(1024)}, u32[]{:S(2)}) copy-start(f32[4096]{0:T(1024)} %param.41) | copy-start | bytes 49156
  860.9 163.6 %all-gather.20.cloned.1.call-start = ((), (), s32[]{:S(2)}) async-start(), calls=%async_computation.11 | async-start | bytes 4456448 | tf_op jit(solution)/shard_map/all_gather | solution.py:294
  861.7 176.5 %all-gather.22.cloned.1.call-start = ((), (), s32[]{:S(2)}) async-start(), calls=%async_computation.12 | async-start | bytes 4456448 | tf_op jit(solution)/shard_map/all_gather | solution.py:297
  893.4 240.3 %all-reduce.21.cloned.1.call-start = ((), (), s32[]{:S(2)}) async-start(), calls=%async_computation.19 | async-start | bytes 4194304 | tf_op jit(solution)/shard_map/psum | solution.py:95
  1112.7 707.7 %reduce-scatter.11.cloned.1.call-start = ((), (), s32[]{:S(2)}) async-start(), calls=%async_computation.16 | async-start | bytes 35651584 | tf_op jit(solution)/shard_map/reduce_scatter | solution.py:358
  1129.0 815.1 %all-reduce.19.cloned.1.call-start = ((), (), s32[]{:S(2)}) async-start(), calls=%async_computation.18 | async-start | bytes 245760 | tf_op jit(solution)/shard_map/psum | solution.py:373
  1136.0 989.4 %reduce-scatter.7.cloned.1.call-start = ((), (), s32[]{:S(2)}) async-start(), calls=%async_computation.14 | async-start | bytes 8912896 | tf_op jit(solution)/shard_map/reduce_scatter | solution.py:356
  1140.8 1506.5 %reduce-scatter.5.cloned.1.call-start = ((), (), s32[]{:S(2)}) async-start(), calls=%async_computation.13 | async-start | bytes 26738688 | tf_op jit(solution)/shard_map/reduce_scatter | solution.py:355
  1153.2 2186.2 %reduce-scatter.9.cloned.1.call-start = ((), (), s32[]{:S(2)}) async-start(), calls=%async_computation.15 | async-start | bytes 35651584 | tf_op jit(solution)/shard_map/reduce_scatter | solution.py:357
  (61 other events, 522.8 us)
Sparse Core Ops, SparseCore 0:
  10.8 153.5 all-gather.9
  184.4 73.4 all-gather.11
  260.7 74.6 all-gather.23
  338.0 74.6 all-gather.13
  417.7 19.7 all-reduce.14
  440.5 191.9 all-gather.15
  635.7 189.8 all-gather.17
  861.1 17.8 all-reduce.16
  881.7 76.3 all-gather.19
  961.3 76.8 all-gather.21
  1112.8 20.8 all-reduce.20
  1136.0 684.2 reduce-scatter.10
  1829.6 114.4 all-reduce.18
  1946.9 178.4 reduce-scatter.6
  2128.1 519.1 reduce-scatter.4
  2650.1 689.2 reduce-scatter.8
where the time goes:
time: 3380 us; the launch traced here: 3360 us
  waiting for transfers between devices  2910 us (86%)
  matrix products  196 us (6%)
  blocking collectives  97.7 us (3%)
  local copies, waits for them, and re-layouts  89 us (3%)
  other arithmetic  52.6 us (2%)
    reduce_scatter x1, waiting for transfers between devices, shards(): lax.psum_scatter(expand_term, 'seq', scatter_dimension=0, tiled=True)  692 us
    reduce_scatter x1, waiting for transfers between devices, shards(): lax.psum_scatter(shrink_term, 'seq', scatter_dimension=0, tiled=True)  647 us
    reduce_scatter x1, waiting for transfers between devices, shards(): lax.psum_scatter(project_term, 'seq', scatter_dimension=0, tiled=True)  522 us
    all_gather x1, waiting for transfers between devices, shards(): lax.all_gather(expand, 'seq', axis=0, tiled=True)  192 us
    reduce_scatter x1, waiting for transfers between devices, shards(): lax.psum_scatter(combine_term, 'seq', scatter_dimension=0, tiled=True)  181 us
    all_gather x1, waiting for transfers between devices, shards(): lax.all_gather(shrink, 'seq', axis=0, tiled=True)  175 us
    all_gather x1, waiting for transfers between devices, shards(): lax.all_gather(project, 'seq', axis=0, tiled=True)  140 us
    psum x1, waiting for transfers between devices, shards(): lax.psum((first_gain_grad, first_bias_grad, project_bias_grad, inner_gain...  121 us
  transfers between devices with their start and end apart: 16, of which 15 were waited for; matrix products, arithmetic and copies ran while one was open for 6% of the time, Pallas kernels for 0%

commit v1 on v0

--- a/solution.py
+++ b/solution.py
@@ -4,6 +4,8 @@
 import jax
 import jax.numpy as jnp
 from jax import lax
+from jax.experimental import pallas as pl
+from jax.experimental.pallas import tpu as pltpu
 from jax.sharding import PartitionSpec as P
 
 D = 2048
@@ -409,9 +411,545 @@
     )
 
 
+BF = jnp.bfloat16
+F32 = jnp.float32
+GRID = (4, 2, 2)
+SEQ = 16
+ALIGNED = (((0,), (0,)), ((), ()))
+PLAIN = (((1,), (0,)), ((), ()))
+HOPS = {
+    "x": [(i, i ^ 1) for i in range(SEQ)],
+    "y": [(i, i ^ 2) for i in range(SEQ)],
+    "z": [(i, (i + 4) % SEQ) for i in range(SEQ)],
+    "back": [((i + 4) % SEQ, i) for i in range(SEQ)],
+    "far": [(i, (i + 8) % SEQ) for i in range(SEQ)],
+}
+
+
+def fits_heads(mesh):
+    return mesh.shape["seq"] == SEQ and mesh.shape["tp"] == 2
+
+
+def hop(values, way):
+    if way == "t":
+        return lax.ppermute(values, "tp", [(0, 1), (1, 0)])
+    return lax.ppermute(values, "seq", HOPS[way])
+
+
+def gather_along(values, way, axis):
+    parts = [values]
+    for _ in range(3 if way == "z" else 1):
+        parts.append(hop(parts[-1], way))
+    return jnp.stack(parts, axis=axis)
+
+
+def gather_zxy(values):
+    return gather_along(gather_along(gather_along(values, "z", 0), "x", 1), "y", 1)
+
+
+def gather_yxz(values):
+    return gather_along(gather_along(gather_along(values, "y", 0), "x", 1), "z", 0)
+
+
+def add_low(first, second):
+    return (first.astype(F32) + second.astype(F32)).astype(BF)
+
+
+def fold(values, way, axis, add=add_low):
+    def part(i):
+        return lax.index_in_dim(values, i, axis, keepdims=False)
+
+    if way != "z":
+        return add(part(0), hop(part(1), way))
+    total = part(3)
+    for i in (2, 1):
+        total = add(part(i), hop(total, "back"))
+    return add(part(0), hop(total, "back"))
+
+
+def add_wide(first, second):
+    return first.astype(F32) + second.astype(F32)
+
+
+def scatter_yxz(values):
+    return fold(fold(fold(values, "y", 1), "x", 1), "z", 0, add_wide)
+
+
+def scatter_zxy(values):
+    return fold(fold(fold(values, "z", 0), "x", 1), "y", 0, add_wide)
+
+
+def gather_rows(own):
+    half = own.shape[1] // 2
+    mine = [gather_zxy(own[:, :half]), gather_yxz(own[:, half:])]
+    mine = [piece.reshape(-1, half) for piece in mine]
+    return mine + [hop(piece, "t") for piece in mine]
+
+
+def scatter_rows(pieces):
+    first = add_low(pieces[0], hop(pieces[2], "t"))
+    second = add_low(pieces[1], hop(pieces[3], "t"))
+    shape = GRID + (-1, first.shape[1])
+    return jnp.concatenate(
+        [scatter_yxz(first.reshape(shape)), scatter_zxy(second.reshape(shape))], axis=1
+    )
+
+
+def swap_by(flag, values, axis):
+    return jnp.where(flag == 0, values, jnp.flip(values, axis))
+
+
+def own_half(side, values, axis=-1):
+    left, right = jnp.split(values, 2, axis=axis)
+    return jnp.where(side == 0, left, right)
+
+
+def join_halves(side, mine, other, axis=-1):
+    return jnp.concatenate(
+        [jnp.where(side == 0, mine, other), jnp.where(side == 0, other, mine)], axis=axis
+    )
+
+
+def turn_halves(side, values, axis=0):
+    left, right = jnp.split(values, 2, axis=axis)
+    return jnp.concatenate(
+        [jnp.where(side == 0, left, right), jnp.where(side == 0, right, left)], axis=axis
+    )
+
+
+def token_sum(values):
+    shape = values.shape
+    values = (values + hop(values, "t")).reshape((shape[0],) + GRID + (-1,))
+    values = values + jnp.flip(hop(values, "x"), 3)
+    values = values + jnp.flip(hop(values, "y"), 2)
+    values = values + jnp.roll(hop(values, "z"), 1, 1)
+    values = values + jnp.roll(hop(values, "far"), 2, 1)
+    return values.reshape(shape)
+
+
+def seq_sum(values):
+    for way in ("x", "y", "z", "far"):
+        values = values + hop(values, way)
+    return values
+
+
+def pair_sum(values):
+    return values + hop(values, "t")
+
+
+def dot(first, second, dims):
+    return lax.dot_general(first, second, dims, preferred_element_type=F32)
+
+
+BLOCK = 512
+KERNEL_BYTES = 48 * 1024 * 1024
+
+
+def attend_kernel(
+    order_ref, raw_ref, bias_ref, cosine_ref, sine_ref, growth_ref, begin_ref,
+    kept_ref, mixture_ref, log_ref, wide,
+):
+    tokens = raw_ref.shape[1]
+    half = HDIM // 2
+    rows = tokens // SEQ
+    for block in range(SEQ):
+        place = pl.ds(pl.multiple_of(order_ref[block] * rows, rows), rows)
+        wide[:, block * rows : (block + 1) * rows] = raw_ref[:, place] + bias_ref[...]
+    cosine, sine, growth = cosine_ref[...], sine_ref[...], growth_ref[...]
+    first, second = wide[0:half, :], wide[half:HDIM, :]
+    scaled = growth * HDIM ** (-0.5)
+    kept_ref[0:half, :] = ((first * cosine - second * sine) * scaled).astype(BF)
+    kept_ref[half:HDIM, :] = ((second * cosine + first * sine) * scaled).astype(BF)
+    first, second = wide[HDIM : HDIM + half, :], wide[HDIM + half : 2 * HDIM, :]
+    kept_ref[HDIM : HDIM + half, :] = ((first * cosine - second * sine) / growth).astype(BF)
+    kept_ref[HDIM + half : 2 * HDIM, :] = ((second * cosine + first * sine) / growth).astype(BF)
+    kept_ref[2 * HDIM :, :] = wide[2 * HDIM :, :].astype(BF)
+    key_rows = lax.broadcasted_iota(jnp.int32, (BLOCK, BLOCK), 0)
+    query_rows = lax.broadcasted_iota(jnp.int32, (BLOCK, BLOCK), 1)
+    for i in range(tokens // BLOCK):
+        columns = slice(i * BLOCK, (i + 1) * BLOCK)
+        queries = kept_ref[0:HDIM, columns]
+        begin = begin_ref[:, columns]
+        largest = jnp.full((1, BLOCK), NEGATIVE, F32)
+        total = jnp.zeros((1, BLOCK), F32)
+        summed = jnp.zeros((HDIM, BLOCK), F32)
+        for j in range(i, -1, -1):
+            place = slice(j * BLOCK, (j + 1) * BLOCK)
+            scores = dot(kept_ref[HDIM : 2 * HDIM, place], queries, ALIGNED)
+            allowed = key_rows + j * BLOCK >= begin
+            if j == i:
+                allowed = allowed & (key_rows <= query_rows)
+            scores = jnp.where(allowed, scores, NEGATIVE)
+            newest = jnp.maximum(largest, jnp.max(scores, axis=0, keepdims=True))
+            weights = jnp.exp(scores - newest)
+            shrunk = jnp.exp(largest - newest)
+            total = total * shrunk + jnp.sum(weights, axis=0, keepdims=True)
+            summed = summed * shrunk + dot(
+                kept_ref[2 * HDIM :, place], weights.astype(BF), PLAIN
+            )
+            largest = newest
+        mixture = summed / total
+        for block in range(BLOCK // rows):
+            mixture_ref[i * (BLOCK // rows) + block] = mixture[:, block * rows : (block + 1) * rows]
+        log_ref[:, columns] = largest + jnp.log(total)
+
+
+def retreat_kernel(
+    order_ref, kept_ref, pull_ref, mixture_ref, log_ref, cosine_ref, sine_ref, growth_ref, begin_ref,
+    low_ref, bias_ref, pulls, delta, query_sum, key_sum, value_sum,
+):
+    tokens = kept_ref.shape[1]
+    half = HDIM // 2
+    rows = tokens // SEQ
+    for block in range(SEQ):
+        place = slice(block * rows, (block + 1) * rows)
+        pulls[:, place] = pull_ref[block]
+        delta[:, place] = jnp.sum(
+            pull_ref[block].astype(F32) * mixture_ref[block], axis=0, keepdims=True
+        )
+    key_rows = lax.broadcasted_iota(jnp.int32, (BLOCK, BLOCK), 0)
+    query_rows = lax.broadcasted_iota(jnp.int32, (BLOCK, BLOCK), 1)
+    for i in range(tokens // BLOCK):
+        columns = slice(i * BLOCK, (i + 1) * BLOCK)
+        queries = kept_ref[0:HDIM, columns]
+        pull = pulls[:, columns]
+        begin = begin_ref[:, columns]
+        logs = log_ref[:, columns]
+        offset = delta[:, columns]
+        query_part = jnp.zeros((HDIM, BLOCK), F32)
+        for j in range(i + 1):
+            place = slice(j * BLOCK, (j + 1) * BLOCK)
+            keys = kept_ref[HDIM : 2 * HDIM, place]
+            scores = dot(keys, queries, ALIGNED)
+            allowed = key_rows + j * BLOCK >= begin
+            if j == i:
+                allowed = allowed & (key_rows <= query_rows)
+            chance = jnp.where(allowed, jnp.exp(scores - logs), 0.0)
+            pushes = dot(kept_ref[2 * HDIM :, place], pull, ALIGNED)
+            dscore = (chance * (pushes - offset)).astype(BF)
+            query_part = query_part + dot(keys, dscore, PLAIN)
+            key_part = dot(queries, dscore, CONTRACT_LAST)
+            value_part = dot(pull, chance.astype(BF), CONTRACT_LAST)
+            if j == i:
+                key_sum[:, place] = key_part
+                value_sum[:, place] = value_part
+            else:
+                key_sum[:, place] += key_part
+                value_sum[:, place] += value_part
+        query_sum[:, columns] = query_part
+    cosine, sine, growth = cosine_ref[...], sine_ref[...], growth_ref[...]
+    scaled = growth * HDIM ** (-0.5)
+    first, second = query_sum[0:half, :] * scaled, query_sum[half:, :] * scaled
+    pieces = [first * cosine + second * sine, second * cosine - first * sine]
+    first, second = key_sum[0:half, :] / growth, key_sum[half:, :] / growth
+    pieces += [first * cosine + second * sine, second * cosine - first * sine]
+    pieces += [value_sum[0:half, :], value_sum[half:, :]]
+    for index, piece in enumerate(pieces):
+        lanes = slice(index * half, (index + 1) * half)
+        bias_ref[lanes, :] = jnp.sum(piece, axis=1, keepdims=True)
+        low = piece.astype(BF)
+        for block in range(SEQ):
+            place = pl.ds(pl.multiple_of(order_ref[block] * rows, rows), rows)
+            low_ref[lanes, place] = low[:, block * rows : (block + 1) * rows]
+
+
+def whole(count):
+    return [pl.BlockSpec(memory_space=pltpu.VMEM) for _ in range(count)]
+
+
+def attend(order, raw, bias, cosine, sine, growth, begin):
+    tokens = raw.shape[1]
+    return pl.pallas_call(
+        attend_kernel,
+        out_shape=(
+            jax.ShapeDtypeStruct((3 * HDIM, tokens), BF),
+            jax.ShapeDtypeStruct((SEQ, HDIM, tokens // SEQ), F32),
+            jax.ShapeDtypeStruct((1, tokens), F32),
+        ),
+        in_specs=[pl.BlockSpec(memory_space=pltpu.SMEM)] + whole(6),
+        out_specs=tuple(whole(3)),
+        scratch_shapes=[pltpu.VMEM((3 * HDIM, tokens), F32)],
+        compiler_params=pltpu.CompilerParams(vmem_limit_bytes=KERNEL_BYTES),
+        cost_estimate=pl.CostEstimate(
+            flops=2 * tokens * tokens * HDIM, bytes_accessed=8 * 192 * tokens,
+            transcendentals=tokens * tokens // 2,
+        ),
+    )(order, raw, bias, cosine, sine, growth, begin)
+
+
+def retreat(order, kept, pull, mixture, logs, cosine, sine, growth, begin):
+    tokens = kept.shape[1]
+    return pl.pallas_call(
+        retreat_kernel,
+        out_shape=(
+            jax.ShapeDtypeStruct((3 * HDIM, tokens), BF),
+            jax.ShapeDtypeStruct((3 * HDIM, 1), F32),
+        ),
+        in_specs=[pl.BlockSpec(memory_space=pltpu.SMEM)] + whole(8),
+        out_specs=tuple(whole(2)),
+        scratch_shapes=[
+            pltpu.VMEM((HDIM, tokens), BF),
+            pltpu.VMEM((1, tokens), F32),
+            pltpu.VMEM((HDIM, tokens), F32),
+            pltpu.VMEM((HDIM, tokens), F32),
+            pltpu.VMEM((HDIM, tokens), F32),
+        ],
+        compiler_params=pltpu.CompilerParams(vmem_limit_bytes=KERNEL_BYTES),
+        cost_estimate=pl.CostEstimate(
+            flops=5 * tokens * tokens * HDIM, bytes_accessed=8 * 192 * tokens,
+            transcendentals=tokens * tokens // 2,
+        ),
+    )(order, kept, pull, mixture, logs, cosine, sine, growth, begin)
+
+
+def to_owners(values):
+    return lax.all_to_all(values, "seq", split_axis=0, concat_axis=0, tiled=True)
+
+
+def column_owners(weights, rows, side):
+    width = weights.shape[1] // SEQ
+    moved = to_owners(jnp.transpose(weights.reshape(rows, SEQ, width), (1, 0, 2)))
+    return turn_halves(side, moved.reshape(SEQ * rows, width))
+
+
+def row_owners(pieces, rows, side):
+    full = turn_halves(side, jnp.concatenate(pieces, axis=0).astype(BF))
+    width = full.shape[1]
+    moved = to_owners(full.reshape(SEQ, rows, width))
+    return jnp.transpose(moved, (1, 0, 2)).reshape(rows, SEQ * width).astype(F32)
+
+
+def head_shards(
+    stream,
+    doc_ids,
+    project,
+    project_bias,
+    combine,
+    combine_bias,
+    expand,
+    expand_bias,
+    shrink,
+    shrink_bias,
+    first_gain,
+    first_bias,
+    inner_gain,
+    inner_bias,
+    second_gain,
+    second_bias,
+    hidden_gain,
+    hidden_bias,
+    out_grad,
+):
+    rows = stream.shape[0]
+    tokens = SEQ * rows
+    head_width = project.shape[2]
+    width = expand.shape[1] // SEQ
+    spot = lax.axis_index("seq")
+    side = lax.axis_index("tp")
+    spot_z, spot_y, spot_x = spot // 4, (spot // 2) % 2, spot % 2
+    blocks = jnp.arange(SEQ, dtype=jnp.int32)
+    order = (
+        ((spot_z - blocks // 4) % 4) * 4 + (spot_y ^ ((blocks // 2) % 2)) * 2 + (spot_x ^ (blocks % 2))
+    )
+
+    def mine(values, axis=-1):
+        return own_half(side, values, axis)
+
+    def my_units(vector, size):
+        return lax.dynamic_slice_in_dim(vector, spot * size, size, axis=-1)
+
+    first_out, first_normed, first_scale = norm_full(stream, first_gain, first_bias)
+    normed_pieces = gather_rows(mine(first_out.astype(BF)))
+    docs_near = gather_zxy(doc_ids[None, :]).reshape(SEQ, rows)
+    project_moved = to_owners(
+        jnp.transpose(project.reshape(rows, 3, SEQ, HDIM), (2, 1, 3, 0)).reshape(SEQ, 3 * HDIM, rows)
+    )
+    project_mine = turn_halves(
+        side, jnp.transpose(project_moved, (1, 0, 2)).reshape(3 * HDIM, tokens), axis=1
+    )
+    project_pieces = jnp.split(project_mine, 4, axis=1)
+
+    docs = docs_near[order].reshape(tokens)
+    member = (docs[:, None] == jnp.arange(DOCS, dtype=jnp.int32)[None, :]).astype(jnp.int32)
+    counts = jnp.sum(member, axis=0)
+    starts = jnp.cumsum(counts) - counts
+    begin = jnp.sum(member * starts[None, :], axis=1)
+    positions = jnp.arange(tokens, dtype=jnp.int32) - begin
+    column = jnp.arange(HDIM // 2, dtype=F32)
+    frequency = jnp.exp(column * (-2.0 * math.log(10000.0) / HDIM))
+    base_ratio = (2.0 * column + 0.4 * HDIM) / (1.4 * HDIM)
+    location = positions.astype(F32)
+    phase_angle = frequency[:, None] * location[None, :]
+    cosine, sine = jnp.cos(phase_angle), jnp.sin(phase_angle)
+    growth = jnp.exp(
+        jnp.log(base_ratio)[:, None] * ((location - tokens // 2) / SCALE_BASE)[None, :]
+    )
+    begin = begin[None, :]
+
+    raw = sum(
+        dot(weights, piece, CONTRACT_LAST)
+        for weights, piece in zip(project_pieces, normed_pieces, strict=True)
+    )
+    head_bias = my_units(project_bias, HDIM).reshape(3 * HDIM, 1)
+    kept, mixture, logs = attend(order, raw, head_bias, cosine, sine, growth, begin)
+
+    spread = to_owners(mixture).reshape(head_width, rows)
+    full_combine = lax.all_gather(combine, "seq", axis=0, tiled=True)
+    sums = pair_sum(jnp.stack([jnp.sum(spread, axis=0), jnp.sum(spread * spread, axis=0)]))
+    average = sums[0:1] / D
+    inner_scale = lax.rsqrt(sums[1:2] / D - average * average + EPSILON)
+    inner_normed = (spread - average) * inner_scale
+    combined_in = (inner_normed * inner_gain[:, None] + inner_bias[:, None]).astype(BF)
+    branch = dot(combined_in, full_combine, (((0,), (1,)), ((), ())))
+    left, right = jnp.split(branch, 2, axis=1)
+    branch = jnp.where(side == 0, left, right) + hop(jnp.where(side == 0, right, left), "t")
+    middle = mine(stream) + branch + mine(combine_bias)
+    sums = pair_sum(jnp.stack([jnp.sum(middle, axis=1), jnp.sum(middle * middle, axis=1)]))
+    average = (sums[0] / D)[:, None]
+    second_scale = lax.rsqrt((sums[1] / D)[:, None] - average * average + EPSILON)
+    second_normed = (middle - average) * second_scale
+    gain_half, bias_half = mine(second_gain), mine(second_bias)
+    expand_pieces = gather_rows((second_normed * gain_half + bias_half).astype(BF))
+
+    out_grad_mine = mine(out_grad)
+    low_out_pieces = gather_rows(out_grad_mine.astype(BF))
+    expand_mine = jnp.split(column_owners(expand, rows, side), 4, axis=0)
+    shrink_mine = jnp.split(column_owners(shrink, rows, side), 4, axis=0)
+    unit_gain, unit_bias = my_units(hidden_gain, width), my_units(hidden_bias, width)
+    hidden_grad = sum(
+        dot(piece, weights, PLAIN)
+        for piece, weights in zip(low_out_pieces, shrink_mine, strict=True)
+    )
+    raised = sum(
+        dot(piece, weights, PLAIN)
+        for piece, weights in zip(expand_pieces, expand_mine, strict=True)
+    ) + my_units(expand_bias, width)
+    active, gelu_back = jax.vjp(gelu_exact, raised)
+    scaled_grad = hidden_grad * unit_gain
+    sums = token_sum(
+        jnp.stack(
+            [
+                jnp.sum(active, axis=1),
+                jnp.sum(active * active, axis=1),
+                jnp.sum(scaled_grad, axis=1),
+                jnp.sum(scaled_grad * active, axis=1),
+            ]
+        )
+    )
+    average = (sums[0] / FF)[:, None]
+    hidden_scale = lax.rsqrt((sums[1] / FF)[:, None] - average * average + EPSILON)
+    hidden_normed = (active - average) * hidden_scale
+    shrink_in = (hidden_normed * unit_gain + unit_bias).astype(BF)
+    grad_mean = (sums[2] / FF)[:, None]
+    cross_mean = hidden_scale * ((sums[3] / FF)[:, None] - average * grad_mean)
+    active_grad = hidden_scale * (scaled_grad - grad_mean - hidden_normed * cross_mean)
+    (raised_grad,) = gelu_back(active_grad)
+    low_raised = raised_grad.astype(BF)
+    second_grad = scatter_rows(
+        [dot(low_raised, weights, CONTRACT_LAST).astype(BF) for weights in expand_mine]
+    )
+    output_sum = scatter_rows(
+        [dot(shrink_in, weights, CONTRACT_LAST).astype(BF) for weights in shrink_mine]
+    )
+    output = middle + output_sum + mine(shrink_bias)
+    shrink_grad = row_owners(
+        [dot(piece, shrink_in, CONTRACT_FIRST) for piece in low_out_pieces], rows, side
+    )
+    expand_grad = row_owners(
+        [dot(piece, low_raised, CONTRACT_FIRST) for piece in expand_pieces], rows, side
+    )
+    unit_sums = jnp.stack(
+        [
+            jnp.sum(hidden_grad * hidden_normed, axis=0),
+            jnp.sum(hidden_grad, axis=0),
+            jnp.sum(raised_grad, axis=0),
+        ]
+    )
+
+    scaled = second_grad * gain_half
+    sums = pair_sum(jnp.stack([jnp.sum(scaled, axis=1), jnp.sum(scaled * second_normed, axis=1)]))
+    middle_grad = out_grad_mine + second_scale * (
+        scaled - (sums[0] / D)[:, None] - second_normed * (sums[1] / D)[:, None]
+    )
+    low_middle = middle_grad.astype(BF)
+    low_middle = join_halves(side, low_middle, hop(low_middle, "t"))
+    inner_grad = dot(full_combine, low_middle, (((0,), (1,)), ((), ())))
+    scaled = inner_grad * inner_gain[:, None]
+    sums = pair_sum(jnp.stack([jnp.sum(scaled, axis=0), jnp.sum(scaled * inner_normed, axis=0)]))
+    mixture_grad = inner_scale * (scaled - sums[0:1] / D - inner_normed * (sums[1:2] / D))
+    pull = to_owners(mixture_grad.astype(BF).reshape(SEQ, HDIM, rows))
+    combine_term = dot(low_middle, combined_in, (((0,), (1,)), ((), ()))).astype(BF)
+    combine_grad = lax.psum_scatter(
+        combine_term, "seq", scatter_dimension=0, tiled=True
+    ).astype(F32)
+
+    low_triple, head_sums = retreat(
+        order, kept, pull, mixture, logs, cosine, sine, growth, begin
+    )
+    first_grad = scatter_rows(
+        [dot(low_triple, weights, CONTRACT_FIRST).astype(BF) for weights in project_pieces]
+    )
+    term = turn_halves(
+        side,
+        jnp.concatenate([dot(low_triple, piece, PLAIN) for piece in normed_pieces], axis=1),
+        axis=1,
+    ).astype(BF)
+    moved = to_owners(jnp.transpose(term.reshape(3 * HDIM, SEQ, rows), (1, 0, 2)))
+    project_grad = jnp.transpose(moved.reshape(SEQ, 3, HDIM, rows), (3, 1, 0, 2)).reshape(
+        rows, 3, head_width
+    ).astype(F32)
+    normed_half = mine(first_normed)
+    scaled = first_grad * mine(first_gain)
+    sums = pair_sum(jnp.stack([jnp.sum(scaled, axis=1), jnp.sum(scaled * normed_half, axis=1)]))
+    stream_grad = middle_grad + first_scale * (
+        scaled - (sums[0] / D)[:, None] - normed_half * (sums[1] / D)[:, None]
+    )
+
+    early = seq_sum(
+        jnp.stack(
+            [
+                jnp.sum(out_grad_mine, axis=0),
+                jnp.sum(second_grad * second_normed, axis=0),
+                jnp.sum(second_grad, axis=0),
+                jnp.sum(middle_grad, axis=0),
+                jnp.sum(inner_grad * inner_normed, axis=1),
+                jnp.sum(inner_grad, axis=1),
+            ]
+        )
+    )
+    late = seq_sum(jnp.stack([jnp.sum(first_grad * normed_half, axis=0), jnp.sum(first_grad, axis=0)]))
+    halves = jnp.concatenate([early[:4], late])
+    halves = join_halves(side, halves, hop(halves, "t"))
+    unit_sums = gather_zxy(unit_sums).reshape(SEQ, 3, width)[order]
+    unit_sums = jnp.transpose(unit_sums, (1, 0, 2)).reshape(3, SEQ * width)
+    head_sums = gather_zxy(head_sums.reshape(3, HDIM)).reshape(SEQ, 3, HDIM)[order]
+    project_bias_grad = jnp.transpose(head_sums, (1, 0, 2)).reshape(3, head_width)
+    return (
+        join_halves(side, output, hop(output, "t")),
+        join_halves(side, stream_grad, hop(stream_grad, "t")),
+        project_grad,
+        project_bias_grad,
+        combine_grad,
+        halves[3],
+        expand_grad,
+        unit_sums[2],
+        shrink_grad,
+        halves[0],
+        halves[4],
+        halves[5],
+        early[4],
+        early[5],
+        halves[1],
+        halves[2],
+        unit_sums[0],
+        unit_sums[1],
+    )
+
+
 def solution(mesh):
+    plan = head_shards if fits_heads(mesh) else shards
     return jax.shard_map(
-        shards,
+        plan,
         mesh=mesh,
         in_specs=(
             P("seq", None),

time: 3380 us -> 769 us (0.23)
  waiting for transfers between devices: 2910 us -> 303 us
  starting transfers between devices: 0.94 us -> 228 us
  matrix products: 196 us -> 81.1 us
  blocking collectives: 97.7 us -> 0 us
    reduce_scatter x4 -> x1, waiting for transfers between devices: 2040 us -> 0.01 us  [head_shards(): lax.psum_scatter(combine_term, 'seq', scatter_dimension=0, tiled=True)]
    all_gather x8 -> x1, waiting for transfers between devices: 703 us -> 0.02 us  [head_shards(): full_combine = lax.all_gather(combine, 'seq', axis=0, tiled=True)]
    ppermute x0 -> x110, waiting for transfers between devices: none -> 288 us  [the longest x87 286 us: hop(): return lax.ppermute(values, 'seq', HOPS[way])]
    ppermute x0 -> x110, starting transfers between devices: none -> 183 us  [the longest x87 142 us: hop(): return lax.ppermute(values, 'seq', HOPS[way])]
    psum x4 -> x0, waiting for transfers between devices: 158 us -> none  [the longest x1 121 us: shards(): lax.psum((first_gain_grad, first_bias_grad, project_bias_grad, inner_gain...]
    dot_general x20 -> x39, matrix products: 196 us -> 81.1 us  [dot(): return lax.dot_general(first, second, dims, preferred_element_type=F32)]
    all_gather x2 -> x0, blocking collectives: 70.5 us -> none  [the longest x1 37.4 us: shards(): total_part = lax.all_gather(log_total.T, 'seq', axis=0, tiled=True)]
    all_to_all x0 -> x8, starting transfers between devices: none -> 44.7 us  [to_owners(): lax.all_to_all(values, 'seq', split_axis=0, concat_axis=0, tiled=True)]
  transfers between devices with their start and end apart: 16 -> 120, of which waited for: 15 -> 51; matrix products, arithmetic and copies ran while one was open for 6% -> 21% of each run, Pallas kernels for 0% -> 2%
where the time goes in v1:
time: 769 us; the launch traced here: 759 us
  waiting for transfers between devices  303 us (39%)
  starting transfers between devices  228 us (30%)
  matrix products  81.1 us (11%)
  other arithmetic  58.2 us (8%)
  local copies, waits for them, and re-layouts  56.2 us (7%)
  between operations  16.3 us (2%)
  Pallas kernels  15.5 us (2%)
    ppermute x87, waiting for transfers between devices, hop(): return lax.ppermute(values, 'seq', HOPS[way])  286 us
    ppermute x87, starting transfers between devices, hop(): return lax.ppermute(values, 'seq', HOPS[way])  142 us
    dot_general x39, matrix products, dot(): return lax.dot_general(first, second, dims, preferred_element_type=F32)  81.1 us
    all_to_all x8, starting transfers between devices, to_owners(): lax.all_to_all(values, 'seq', split_axis=0, concat_axis=0, tiled=True)  44.7 us
    ppermute x23, starting transfers between devices, hop(): return lax.ppermute(values, 'tp', [(0, 1), (1, 0)])  40.8 us
    another operation x28, other arithmetic, gather_along(): return jnp.stack(parts, axis=axis)  20.3 us
  transfers between devices with their start and end apart: 120, of which 51 were waited for; matrix products, arithmetic and copies ran while one was open for 21% of the time, Pallas kernels for 2%

profile of v1, /device:TPU:1, one launch (start us, length us, event | category | flops | bytes accessed | tf_op | source)
XLA Modules:
  0.0 758.9 jit_solution(6962352474333175397)
XLA Ops:
  23.7 9.2 %collective-permute-done.5 = bf16[128,512]{1,0:T(8,128)(2,1)S(1)} collective-permute-done((bf16[128,512]{1,0:T(8,128)(2,1)S(1)}, bf16[128,512]{1,0:T(8,128)(2,1)S(1)}, u32[]{:S(2)}, u32[]{:S(2)}) %collective-permute-start.5) | collective-permute-done | bytes 131104 | tf_op jit(solution)/shard_map/ppermute | solution.py:436
  34.3 8.6 %collective-permute-done.12 = s32[1,128]{1,0:T(1,128)S(1)} collective-permute-done((s32[1,128]{1,0:T(1,128)S(1)}, s32[1,128]{1,0:T(1,128)S(1)}, u32[]{:S(2)}, u32[]{:S(2)}) %collective-permute-start.12) | collective-permute-done | bytes 544 | tf_op jit(solution)/shard_map/ppermute | solution.py:436
  58.7 19.9 %collective-permute-done.2 = bf16[128,512]{1,0:T(8,128)(2,1)S(1)} collective-permute-done((bf16[128,512]{1,0:T(8,128)(2,1)S(1)}, bf16[128,512]{1,0:T(8,128)(2,1)S(1)}, u32[]{:S(2)}, u32[]{:S(2)}) %collective-permute-start.2) | collective-permute-done | bytes 131104 | tf_op jit(solution)/shard_map/ppermute | solution.py:436
  81.9 22.1 %collective-permute-done.3 = bf16[4,128,512]{2,1,0:T(8,128)(2,1)} collective-permute-done((bf16[4,128,512]{2,1,0:T(8,128)(2,1)S(1)}, bf16[4,128,512]{2,1,0:T(8,128)(2,1)}, u32[]{:S(2)}, u32[]{:S(2)}) %collective-permute-start.3) | collective-permute-done | bytes 524320 | tf_op jit(solution)/shard_map/ppermute | solution.py:436
  107.6 19.6 %collective-permute-done.9 = bf16[2,2,128,512]{3,2,0,1:T(8,128)(2,1)S(1)} collective-permute-done((bf16[2,2,128,512]{3,2,0,1:T(8,128)(2,1)}, bf16[2,2,128,512]{3,2,0,1:T(8,128)(2,1)S(1)}, u32[]{:S(2)}, u32[]{:S(2)}) %collective-permute-start.9) | collective-permute-done | bytes 524320 | tf_op jit(solution)/shard_map/ppermute | solution.py:436
  157.1 9.4 %all-to-all-done.1 = f32[16,64,128]{2,1,0:T(8,128)S(1)} async-done(((f32[16,64,128]{2,1,0:T(8,128)}), f32[16,64,128]{2,1,0:T(8,128)S(1)}, u32[]{:S(2)}, u32[]{:S(2)}) %all-to-all-start.1) | async-done | bytes 524320 | tf_op jit(solution)/shard_map/all_to_all | solution.py:706
  185.5 9.8 %collective-permute-done.32 = bf16[128,512]{1,0:T(8,128)(2,1)S(1)} collective-permute-done((bf16[128,512]{1,0:T(8,128)(2,1)S(1)}, bf16[128,512]{1,0:T(8,128)(2,1)S(1)}, u32[]{:S(2)}, u32[]{:S(2)}) %collective-permute-start.32) | collective-permute-done | bytes 131104 | tf_op jit(solution)/shard_map/ppermute | solution.py:436
  229.4 9.3 %collective-permute-done.26 = bf16[2,128,512]{2,1,0:T(8,128)(2,1)S(1)} collective-permute-done((bf16[2,128,512]{2,1,0:T(8,128)(2,1)S(1)}, bf16[2,128,512]{2,1,0:T(8,128)(2,1)S(1)}, u32[]{:S(2)}, u32[]{:S(2)}) %collective-permute-start.26) | collective-permute-done | bytes 262176 | tf_op jit(solution)/shard_map/ppermute | solution.py:436
  242.0 8.6 %collective-permute-done.20 = bf16[128,512]{1,0:T(8,128)(2,1)S(1)} collective-permute-done((bf16[128,512]{1,0:T(8,128)(2,1)}, bf16[128,512]{1,0:T(8,128)(2,1)S(1)}, u32[]{:S(2)}, u32[]{:S(2)}) %collective-permute-start.20) | collective-permute-done | bytes 131104 | tf_op jit(solution)/shard_map/ppermute | solution.py:436
  250.6 12.1 %collective-permute-start.21 = (bf16[128,512]{1,0:T(8,128)(2,1)S(1)}, bf16[128,512]{1,0:T(8,128)(2,1)S(1)}, u32[]{:S(2)}, u32[]{:S(2)}) collective-permute-start(bf16[128,512]{1,0:T(8,128)(2,1)S(1)} %collective-permute-done.20), channel_id=1, source_target_pairs={{0,8},{2,10},{4,12},{6,14},{8,16},{10,18},{12,20},{14,22},{16,24},... | collective-permute-start | bytes 393224 | tf_op jit(solution)/shard_map/ppermute | solution.py:436
  267.5 9.1 %collective-permute-start.22 = (bf16[128,512]{1,0:T(8,128)(2,1)S(1)}, bf16[128,512]{1,0:T(8,128)(2,1)S(1)}, u32[]{:S(2)}, u32[]{:S(2)}) collective-permute-start(bf16[128,512]{1,0:T(8,128)(2,1)S(1)} %collective-permute-done.21), channel_id=1, source_target_pairs={{0,8},{2,10},{4,12},{6,14},{8,16},{10,18},{12,20},{14,22},{16,24},... | collective-permute-start | bytes 393224 | tf_op jit(solution)/shard_map/ppermute | solution.py:436
  343.4 9.5 %multiply_reduce_fusion.3 = (f32[2048]{0:T(1024)S(1)}, f32[2048]{0:T(1024)S(1)}, f32[2048]{0:T(1024)S(1)}, f32[2048]{0:T(1024)S(1)}, f32[2048,256]{0,1:T(8,128)}, /*index=5*/f32[2048,256]{0,1:T(8,128)}, f32[2048,256]{0,1:T(8,128)}) fusion(f32[256]{0:T(256)S(1)} %dynamic_slice.14, f32[2048,256]{0,1:T(8,128)S(1)} %fusion.2, f32[2048,256]{0,1:T(8,128)S(1)} %fusion.121, ...), kind=kOutput, calls=%fused_computation.68 | convolution fusion | flops 575135744 | bytes 14976000 | tf_op jit(solution)/shard_map/dot_general | solution.py:541
  445.0 9.6 %collective-permute-done.69 = bf16[2,2,128,512]{3,2,0,1:T(8,128)(2,1)S(1)} collective-permute-done((bf16[2,2,128,512]{3,2,0,1:T(8,128)(2,1)S(1)}, bf16[2,2,128,512]{3,2,0,1:T(8,128)(2,1)S(1)}, u32[]{:S(2)}, u32[]{:S(2)}) %collective-permute-start.69) | collective-permute-done | bytes 524320 | tf_op jit(solution)/shard_map/ppermute | solution.py:436
  457.9 7.9 %collective-permute-done.57 = bf16[2,2,128,512]{3,2,0,1:T(8,128)(2,1)S(1)} collective-permute-done((bf16[2,2,128,512]{3,2,0,1:T(8,128)(2,1)S(1)}, bf16[2,2,128,512]{3,2,0,1:T(8,128)(2,1)S(1)}, u32[]{:S(2)}, u32[]{:S(2)}) %collective-permute-start.57) | collective-permute-done | bytes 524320 | tf_op jit(solution)/shard_map/ppermute | solution.py:436
  467.5 8.3 %collective-permute-done.63 = bf16[4,2,128,512]{3,2,0,1:T(8,128)(2,1)S(1)} collective-permute-done((bf16[4,2,128,512]{3,2,0,1:T(8,128)(2,1)S(1)}, bf16[4,2,128,512]{3,2,0,1:T(8,128)(2,1)S(1)}, u32[]{:S(2)}, u32[]{:S(2)}) %collective-permute-start.63) | collective-permute-done | bytes 1048608 | tf_op jit(solution)/shard_map/ppermute | solution.py:436
  479.0 9.3 %collective-permute-done.58 = bf16[2,2,128,512]{3,2,0,1:T(8,128)(2,1)S(1)} collective-permute-done((bf16[2,2,128,512]{3,2,0,1:T(8,128)(2,1)S(1)}, bf16[2,2,128,512]{3,2,0,1:T(8,128)(2,1)S(1)}, u32[]{:S(2)}, u32[]{:S(2)}) %collective-permute-start.58) | collective-permute-done | bytes 524320 | tf_op jit(solution)/shard_map/ppermute | solution.py:436
  491.4 8.1 %collective-permute-done.71 = bf16[2,2,128,512]{3,2,0,1:T(8,128)(2,1)S(1)} collective-permute-done((bf16[2,2,128,512]{3,2,0,1:T(8,128)(2,1)S(1)}, bf16[2,2,128,512]{3,2,0,1:T(8,128)(2,1)S(1)}, u32[]{:S(2)}, u32[]{:S(2)}) %collective-permute-start.71) | collective-permute-done | bytes 524320 | tf_op jit(solution)/shard_map/ppermute | solution.py:436
  518.0 8.7 %collective-permute-done.67 = f32[128,512]{1,0:T(8,128)S(1)} collective-permute-done((f32[128,512]{1,0:T(8,128)S(1)}, f32[128,512]{1,0:T(8,128)S(1)}, u32[]{:S(2)}, u32[]{:S(2)}) %collective-permute-start.67) | collective-permute-done | bytes 262176 | tf_op jit(solution)/shard_map/ppermute | solution.py:436
  527.1 7.9 %collective-permute-start.74 = (f32[2,128]{1,0:T(2,128)S(1)}, f32[2,128]{1,0:T(2,128)S(1)}, u32[]{:S(2)}, u32[]{:S(2)}) collective-permute-start(f32[2,128]{1,0:T(2,128)S(1)} %pad_maximum_fusion.50), channel_id=1, source_target_pairs={{0,1},{1,0},{2,3},{3,2},{4,5},{5,4},{6,7},{7,6},{8,9},{9,8},{10,11... | collective-permute-start | bytes 3080 | tf_op jit(solution)/shard_map/ppermute | solution.py:435
  587.8 9.3 %shard_map.323 = (bf16[192,2048]{1,0:T(8,128)(2,1)S(1)}, f32[192,1]{1,0:T(8,128)S(1)}) custom-call(s32[16]{0:T(128)S(1)} %fusion.49.order_ref, bf16[192,2048]{1,0:T(8,128)(2,1)S(1)} %get-tuple-element.24.kept_ref, bf16[16,64,128]{2,1,0:T(8,128)(2,1)S(1)} %all-to-all-done.4.pull_ref, f32[16,64,128]{2,1,0:T(8,128)} %get-tuple-element.23.mixture_ref, ...), custom_call_target="tpu_custom_call" | custom-call | flops 1342177280 | bytes 3145728 | tf_op jit(solution)/shard_map/pallas_call | solution.py:682
  621.3 20.2 %collective-permute-done.84 = bf16[2,2,128,512]{3,2,0,1:T(8,128)(2,1)S(1)} collective-permute-done((bf16[2,2,128,512]{3,2,0,1:T(8,128)(2,1)S(1)}, bf16[2,2,128,512]{3,2,0,1:T(8,128)(2,1)S(1)}, u32[]{:S(2)}, u32[]{:S(2)}) %collective-permute-start.84) | collective-permute-done | bytes 524320 | tf_op jit(solution)/shard_map/ppermute | solution.py:436
  644.9 15.7 %collective-permute-done.78 = bf16[4,2,128,512]{3,2,0,1:T(8,128)(2,1)S(1)} collective-permute-done((bf16[4,2,128,512]{3,2,0,1:T(8,128)(2,1)S(1)}, bf16[4,2,128,512]{3,2,0,1:T(8,128)(2,1)S(1)}, u32[]{:S(2)}, u32[]{:S(2)}) %collective-permute-start.78) | collective-permute-done | bytes 1048608 | tf_op jit(solution)/shard_map/ppermute | solution.py:436
  675.6 16.3 %collective-permute-done.79 = bf16[4,128,512]{2,1,0:T(8,128)(2,1)} collective-permute-done((bf16[4,128,512]{2,1,0:T(8,128)(2,1)}, bf16[4,128,512]{2,1,0:T(8,128)(2,1)}, u32[]{:S(2)}, u32[]{:S(2)}) %collective-permute-start.79) | collective-permute-done | bytes 524320 | tf_op jit(solution)/shard_map/ppermute | solution.py:436
  707.1 11.2 %collective-permute-done.81 = f32[128,512]{1,0:T(8,128)S(1)} collective-permute-done((f32[128,512]{1,0:T(8,128)S(1)}, f32[128,512]{1,0:T(8,128)S(1)}, u32[]{:S(2)}, u32[]{:S(2)}) %collective-permute-start.81) | collective-permute-done | bytes 262176 | tf_op jit(solution)/shard_map/ppermute | solution.py:436
  (608 shorter events, 463.0 us)
Async XLA Ops:
  7.2 168.6 %all-gather.2.cloned.1.call-start = ((), (), s32[]{:S(2)}) async-start(), calls=%async_computation.9 | async-start | bytes 4456448 | tf_op jit(solution)/shard_map/all_gather | solution.py:797
  12.0 36.1 %collective-permute-start = (bf16[128,512]{1,0:T(8,128)(2,1)S(1)}, bf16[128,512]{1,0:T(8,128)(2,1)}, u32[]{:S(2)}, u32[]{:S(2)}) collective-permute-start(bf16[128,512]{1,0:T(8,128)(2,1)S(1)} %get-tuple-element.198), channel_id=1, source_target_pairs={{0,8},{2,10},{4,12},{6,14},{8,16},{10,18},{12,20},{14,22},{16,24},... | collective-permute-start | bytes 393224 | tf_op jit(solution)/shard_map/ppermute | solution.py:436
  15.5 117.5 %all-to-all-start = ((bf16[16,192,128]{2,1,0:T(8,128)(2,1)}), bf16[16,192,128]{2,1,0:T(8,128)(2,1)S(1)}, u32[]{:S(2)}, u32[]{:S(2)}) async-start(bf16[16,192,128]{2,1,0:T(8,128)(2,1)} %bitcast.2), calls=%async_computation | async-start | bytes 1572864 | tf_op jit(solution)/shard_map/all_to_all | solution.py:706
  49.9 31.5 %collective-permute-start.7 = (bf16[2,2,128,512]{3,2,0,1:T(8,128)(2,1)S(1)}, bf16[2,2,128,512]{3,2,0,1:T(8,128)(2,1)}, u32[]{:S(2)}, u32[]{:S(2)}) collective-permute-start(bf16[2,2,128,512]{3,2,0,1:T(8,128)(2,1)S(1)} %get-tuple-element.182), channel_id=1, source_target_pairs={{0,8},{2,10},{4,12},{6,14},{8,16},{10,18},{12,20},{14,22},{16,24},... | collective-permute-start | bytes 1572872 | tf_op jit(solution)/shard_map/ppermute | solution.py:436
  166.5 46.7 %all-to-all-start.2 = ((bf16[16,128,256]{1,2,0:T(8,128)(2,1)}), bf16[16,128,256]{1,2,0:T(8,128)(2,1)}, u32[]{:S(2)}, u32[]{:S(2)}) async-start(bf16[16,128,256]{1,2,0:T(8,128)(2,1)} %bitcast.499), calls=%async_computation.2 | async-start | bytes 2097152 | tf_op jit(solution)/shard_map/all_to_all | solution.py:706
  213.2 75.0 %all-to-all-start.3 = ((bf16[16,128,256]{1,2,0:T(8,128)(2,1)}), bf16[16,128,256]{1,2,0:T(8,128)(2,1)}, u32[]{:S(2)}, u32[]{:S(2)}) async-start(bf16[16,128,256]{1,2,0:T(8,128)(2,1)} %bitcast.498), calls=%async_computation.3 | async-start | bytes 2097152 | tf_op jit(solution)/shard_map/all_to_all | solution.py:706
  224.2 38.5 %collective-permute-start.35 = (bf16[4,128,512]{2,1,0:T(8,128)(2,1)S(1)}, bf16[4,128,512]{2,1,0:T(8,128)(2,1)S(1)}, u32[]{:S(2)}, u32[]{:S(2)}) collective-permute-start(bf16[4,128,512]{2,1,0:T(8,128)(2,1)S(1)} %get-tuple-element.176), channel_id=1, source_target_pairs={{0,2},{2,0},{4,6},{6,4},{8,10},{10,8},{12,14},{14,12},{16,18},{18,... | collective-permute-start | bytes 1572872 | tf_op jit(solution)/shard_map/ppermute | solution.py:436
  227.2 49.4 %collective-permute-start.41 = (bf16[2,2,128,512]{3,2,0,1:T(8,128)(2,1)}, bf16[2,2,128,512]{3,2,0,1:T(8,128)(2,1)}, u32[]{:S(2)}, u32[]{:S(2)}) collective-permute-start(bf16[2,2,128,512]{3,2,0,1:T(8,128)(2,1)} %collective-permute-done.40), channel_id=1, source_target_pairs={{0,8},{2,10},{4,12},{6,14},{8,16},{10,18},{12,20},{14,22},{16,24},... | collective-permute-start | bytes 1572872 | tf_op jit(solution)/shard_map/ppermute | solution.py:436
  239.7 46.3 %collective-permute-start.27 = (bf16[2,2,128,512]{3,2,0,1:T(8,128)(2,1)}, bf16[2,2,128,512]{3,2,0,1:T(8,128)(2,1)}, u32[]{:S(2)}, u32[]{:S(2)}) collective-permute-start(bf16[2,2,128,512]{3,2,0,1:T(8,128)(2,1)} %get-tuple-element.170), channel_id=1, source_target_pairs={{0,8},{2,10},{4,12},{6,14},{8,16},{10,18},{12,20},{14,22},{16,24},... | collective-permute-start | bytes 1572872 | tf_op jit(solution)/shard_map/ppermute | solution.py:436
  265.8 45.3 %collective-permute-start.36 = (bf16[4,2,128,512]{3,2,0,1:T(8,128)(2,1)}, bf16[4,2,128,512]{3,2,0,1:T(8,128)(2,1)}, u32[]{:S(2)}, u32[]{:S(2)}) collective-permute-start(bf16[4,2,128,512]{3,2,0,1:T(8,128)(2,1)} %get-tuple-element.153), channel_id=1, source_target_pairs={{0,4},{2,6},{4,0},{6,2},{8,12},{10,14},{12,8},{14,10},{16,20},{18,... | collective-permute-start | bytes 3145736 | tf_op jit(solution)/shard_map/ppermute | solution.py:436
  279.9 53.9 %collective-permute-start.43 = (bf16[2048,512]{1,0:T(8,128)(2,1)}, bf16[2048,512]{1,0:T(8,128)(2,1)}, u32[]{:S(2)}, u32[]{:S(2)}) collective-permute-start(bf16[2048,512]{1,0:T(8,128)(2,1)} %bitcast.92), channel_id=1, source_target_pairs={{0,1},{1,0},{2,3},{3,2},{4,5},{5,4},{6,7},{7,6},{8,9},{9,8},{10,11... | collective-permute-start | bytes 6291464 | tf_op jit(solution)/shard_map/ppermute | solution.py:435
  392.7 145.2 %all-to-all-start.7 = ((bf16[16,128,256]{2,1,0:T(8,128)(2,1)}), bf16[16,128,256]{2,1,0:T(8,128)(2,1)}, u32[]{:S(2)}, u32[]{:S(2)}) async-start(bf16[16,128,256]{2,1,0:T(8,128)(2,1)} %bitcast.496), calls=%async_computation.8 | async-start | bytes 2097152 | tf_op jit(solution)/shard_map/all_to_all | solution.py:706
  399.6 32.4 %collective-permute-start.49 = (bf16[2048,512]{1,0:T(8,128)(2,1)}, bf16[2048,512]{1,0:T(8,128)(2,1)S(1)}, u32[]{:S(2)}, u32[]{:S(2)}) collective-permute-start(bf16[2048,512]{1,0:T(8,128)(2,1)} %convolution_convert_fusion.11), channel_id=1, source_target_pairs={{0,1},{1,0},{2,3},{3,2},{4,5},{5,4},{6,7},{7,6},{8,9},{9,8},{10,11... | collective-permute-start | bytes 6291464 | tf_op jit(solution)/shard_map/ppermute | solution.py:435
  404.5 28.8 %collective-permute-start.55 = (bf16[2048,512]{1,0:T(8,128)(2,1)}, bf16[2048,512]{1,0:T(8,128)(2,1)S(1)}, u32[]{:S(2)}, u32[]{:S(2)}) collective-permute-start(bf16[2048,512]{1,0:T(8,128)(2,1)} %convolution_convert_fusion.9), channel_id=1, source_target_pairs={{0,1},{1,0},{2,3},{3,2},{4,5},{5,4},{6,7},{7,6},{8,9},{9,8},{10,11... | collective-permute-start | bytes 6291464 | tf_op jit(solution)/shard_map/ppermute | solution.py:435
  406.3 30.9 %collective-permute-start.62 = (bf16[2048,512]{1,0:T(8,128)(2,1)S(1)}, bf16[2048,512]{1,0:T(8,128)(2,1)S(1)}, u32[]{:S(2)}, u32[]{:S(2)}) collective-permute-start(bf16[2048,512]{1,0:T(8,128)(2,1)S(1)} %convolution_convert_fusion.7), channel_id=1, source_target_pairs={{0,1},{1,0},{2,3},{3,2},{4,5},{5,4},{6,7},{7,6},{8,9},{9,8},{10,11... | collective-permute-start | bytes 6291464 | tf_op jit(solution)/shard_map/ppermute | solution.py:435
  430.7 106.6 %collective-permute-start.109 = (f32[4,2,3,256]{3,1,0,2:T(2,128)S(1)}, f32[4,2,3,256]{3,1,0,2:T(2,128)S(1)}, u32[]{:S(2)}, u32[]{:S(2)}) collective-permute-start(f32[4,2,3,256]{3,1,0,2:T(2,128)S(1)} %get-tuple-element.221), channel_id=1, source_target_pairs={{0,4},{2,6},{4,0},{6,2},{8,12},{10,14},{12,8},{14,10},{16,20},{18,... | collective-permute-start | bytes 73736 | tf_op jit(solution)/shard_map/ppermute | solution.py:436
  438.5 37.3 %collective-permute-start.63 = (bf16[4,2,128,512]{3,2,0,1:T(8,128)(2,1)S(1)}, bf16[4,2,128,512]{3,2,0,1:T(8,128)(2,1)S(1)}, u32[]{:S(2)}, u32[]{:S(2)}) collective-permute-start(bf16[4,2,128,512]{3,2,0,1:T(8,128)(2,1)S(1)} %bitcast.531), channel_id=1, source_target_pairs={{0,4},{2,6},{4,0},{6,2},{8,12},{10,14},{12,8},{14,10},{16,20},{18,... | collective-permute-start | bytes 3145736 | tf_op jit(solution)/shard_map/ppermute | solution.py:436
  538.0 28.9 %all-to-all-start.6 = ((bf16[16,128,256]{2,1,0:T(8,128)(2,1)}), bf16[16,128,256]{2,1,0:T(8,128)(2,1)}, u32[]{:S(2)}, u32[]{:S(2)}) async-start(bf16[16,128,256]{2,1,0:T(8,128)(2,1)} %bitcast.497), calls=%async_computation.7 | async-start | bytes 2097152 | tf_op jit(solution)/shard_map/all_to_all | solution.py:706
  574.3 175.8 %reduce-scatter.2.cloned.1.call-start = ((), (), s32[]{:S(2)}) async-start(), calls=%async_computation.10 | async-start | bytes 4456448 | tf_op jit(solution)/shard_map/reduce_scatter | solution.py:882
  604.9 58.4 %collective-permute-start.91 = (f32[3,64]{1,0:T(4,128)S(1)}, f32[3,64]{1,0:T(4,128)S(1)}, u32[]{:S(2)}, u32[]{:S(2)}) collective-permute-start(f32[3,64]{1,0:T(4,128)S(1)} %reshape.643), channel_id=1, source_target_pairs={{0,8},{2,10},{4,12},{6,14},{8,16},{10,18},{12,20},{14,22},{16,24},... | collective-permute-start | bytes 2312 | tf_op jit(solution)/shard_map/ppermute | solution.py:436
  614.4 46.2 %collective-permute-start.78 = (bf16[4,2,128,512]{3,2,0,1:T(8,128)(2,1)S(1)}, bf16[4,2,128,512]{3,2,0,1:T(8,128)(2,1)S(1)}, u32[]{:S(2)}, u32[]{:S(2)}) collective-permute-start(bf16[4,2,128,512]{3,2,0,1:T(8,128)(2,1)S(1)} %bitcast.532), channel_id=1, source_target_pairs={{0,4},{2,6},{4,0},{6,2},{8,12},{10,14},{12,8},{14,10},{16,20},{18,... | collective-permute-start | bytes 3145736 | tf_op jit(solution)/shard_map/ppermute | solution.py:436
  661.7 30.1 %collective-permute-start.79 = (bf16[4,128,512]{2,1,0:T(8,128)(2,1)}, bf16[4,128,512]{2,1,0:T(8,128)(2,1)}, u32[]{:S(2)}, u32[]{:S(2)}) collective-permute-start(bf16[4,128,512]{2,1,0:T(8,128)(2,1)} %slice_bitcast_fusion), channel_id=1, source_target_pairs={{0,2},{2,0},{4,6},{6,4},{8,10},{10,8},{12,14},{14,12},{16,18},{18,... | collective-permute-start | bytes 1572872 | tf_op jit(solution)/shard_map/ppermute | solution.py:436
  665.5 27.7 %collective-permute-start.86 = (bf16[2,2,128,512]{3,2,0,1:T(8,128)(2,1)}, bf16[2,2,128,512]{3,2,0,1:T(8,128)(2,1)}, u32[]{:S(2)}, u32[]{:S(2)}) collective-permute-start(bf16[2,2,128,512]{3,2,0,1:T(8,128)(2,1)} %fusion.17), channel_id=1, source_target_pairs={{8,0},{10,2},{12,4},{14,6},{16,8},{18,10},{20,12},{22,14},{24,16},... | collective-permute-start | bytes 1572872 | tf_op jit(solution)/shard_map/ppermute | solution.py:436
  670.6 75.8 %all-to-all-start.5 = ((bf16[16,192,128]{2,1,0:T(8,128)(2,1)}), bf16[16,192,128]{2,1,0:T(8,128)(2,1)S(1)}, u32[]{:S(2)}, u32[]{:S(2)}) async-start(bf16[16,192,128]{2,1,0:T(8,128)(2,1)} %maximum_bitcast_fusion), calls=%async_computation.5 | async-start | bytes 1572864 | tf_op jit(solution)/shard_map/all_to_all | solution.py:706
  (152 other events, 1776.9 us)
Sparse Core Ops, SparseCore 0:
  10.8 105.3 all-gather.1
  587.8 109.0 reduce-scatter.1

commit v2 on v1

--- a/solution.py
+++ b/solution.py
@@ -420,10 +420,12 @@
 HOPS = {
     "x": [(i, i ^ 1) for i in range(SEQ)],
     "y": [(i, i ^ 2) for i in range(SEQ)],
-    "z": [(i, (i + 4) % SEQ) for i in range(SEQ)],
-    "back": [((i + 4) % SEQ, i) for i in range(SEQ)],
-    "far": [(i, (i + 8) % SEQ) for i in range(SEQ)],
+    "xy": [(i, i ^ 3) for i in range(SEQ)],
+    "z1": [(i, (i + 4) % SEQ) for i in range(SEQ)],
+    "z2": [(i, (i + 8) % SEQ) for i in range(SEQ)],
+    "z3": [(i, (i + 12) % SEQ) for i in range(SEQ)],
 }
+COLUMN = ("z1", "z2", "z3")
 
 
 def fits_heads(mesh):
@@ -436,63 +438,71 @@
     return lax.ppermute(values, "seq", HOPS[way])
 
 
+def after(first, *later):
+    return lax.optimization_barrier((first,) + later)
+
+
 def gather_along(values, way, axis):
-    parts = [values]
-    for _ in range(3 if way == "z" else 1):
-        parts.append(hop(parts[-1], way))
-    return jnp.stack(parts, axis=axis)
-
-
-def gather_zxy(values):
-    return gather_along(gather_along(gather_along(values, "z", 0), "x", 1), "y", 1)
-
-
-def gather_yxz(values):
-    return gather_along(gather_along(gather_along(values, "y", 0), "x", 1), "z", 0)
+    return jnp.stack([values, hop(values, way)], axis=axis)
+
+
+def gather_column(own):
+    return jnp.stack([own] + [hop(own, way) for way in COLUMN])
+
+
+def gather_plane(column, midway=None):
+    half = column.shape[2] // 2
+    left = gather_along(column[:, :, :half], "x", 1)
+    right = gather_along(column[:, :, half:], "y", 1)
+    done = None
+    if midway is not None:
+        left, right, done = midway(left, right)
+    mine = [gather_along(left, "y", 1), gather_along(right, "x", 2)]
+    mine = [piece.reshape(-1, half) for piece in mine]
+    if midway is not None:
+        mine[0], mine[1], *done = after(mine[0], mine[1], *done)
+    return mine + [hop(piece, "t") for piece in mine], done
+
+
+def gather_small(values):
+    return gather_along(gather_along(gather_column(values), "x", 1), "y", 1)
 
 
 def add_low(first, second):
     return (first.astype(F32) + second.astype(F32)).astype(BF)
 
 
-def fold(values, way, axis, add=add_low):
-    def part(i):
-        return lax.index_in_dim(values, i, axis, keepdims=False)
-
-    if way != "z":
-        return add(part(0), hop(part(1), way))
-    total = part(3)
-    for i in (2, 1):
-        total = add(part(i), hop(total, "back"))
-    return add(part(0), hop(total, "back"))
-
-
-def add_wide(first, second):
-    return first.astype(F32) + second.astype(F32)
-
-
-def scatter_yxz(values):
-    return fold(fold(fold(values, "y", 1), "x", 1), "z", 0, add_wide)
-
-
-def scatter_zxy(values):
-    return fold(fold(fold(values, "z", 0), "x", 1), "y", 0, add_wide)
-
-
-def gather_rows(own):
-    half = own.shape[1] // 2
-    mine = [gather_zxy(own[:, :half]), gather_yxz(own[:, half:])]
-    mine = [piece.reshape(-1, half) for piece in mine]
-    return mine + [hop(piece, "t") for piece in mine]
-
-
-def scatter_rows(pieces):
-    first = add_low(pieces[0], hop(pieces[2], "t"))
-    second = add_low(pieces[1], hop(pieces[3], "t"))
-    shape = GRID + (-1, first.shape[1])
-    return jnp.concatenate(
-        [scatter_yxz(first.reshape(shape)), scatter_zxy(second.reshape(shape))], axis=1
-    )
+def fold(values, way, axis):
+    near = lax.index_in_dim(values, 0, axis, keepdims=False)
+    far = lax.index_in_dim(values, 1, axis, keepdims=False)
+    return add_low(near, hop(far, way))
+
+
+def scatter_pair(low, own, others):
+    return [
+        (dot(low, weights, own[0]) + hop(other, "t").astype(F32)).astype(BF)
+        for weights, other in zip(own[1], others, strict=True)
+    ]
+
+
+def scatter_wide(pair):
+    shape = GRID + (-1, pair[0].shape[1])
+    return [fold(pair[0].reshape(shape), "y", 1), fold(pair[1].reshape(shape), "x", 2)]
+
+
+def scatter_narrow(halves):
+    return jnp.concatenate([fold(halves[0], "x", 1), fold(halves[1], "y", 1)], axis=2)
+
+
+def scatter_plane(pair):
+    return scatter_narrow(scatter_wide(pair))
+
+
+def scatter_column(slabs):
+    total = slabs[0].astype(F32)
+    for i in range(1, 4):
+        total = total + lax.optimization_barrier(hop(slabs[i], COLUMN[3 - i])).astype(F32)
+    return total
 
 
 def swap_by(flag, values, axis):
@@ -520,17 +530,15 @@
 def token_sum(values):
     shape = values.shape
     values = (values + hop(values, "t")).reshape((shape[0],) + GRID + (-1,))
-    values = values + jnp.flip(hop(values, "x"), 3)
-    values = values + jnp.flip(hop(values, "y"), 2)
-    values = values + jnp.roll(hop(values, "z"), 1, 1)
-    values = values + jnp.roll(hop(values, "far"), 2, 1)
-    return values.reshape(shape)
+    moved = [jnp.flip(hop(values, "x"), 3), jnp.flip(hop(values, "y"), 2)]
+    values = values + moved[0] + moved[1] + jnp.flip(hop(values, "xy"), (2, 3))
+    moved = [jnp.roll(hop(values, COLUMN[i]), i + 1, 1) for i in range(3)]
+    return (values + moved[0] + moved[1] + moved[2]).reshape(shape)
 
 
 def seq_sum(values):
-    for way in ("x", "y", "z", "far"):
-        values = values + hop(values, way)
-    return values
+    values = values + hop(values, "x") + hop(values, "y") + hop(values, "xy")
+    return values + hop(values, "z1") + hop(values, "z2") + hop(values, "z3")
 
 
 def pair_sum(values):
@@ -542,19 +550,37 @@
 
 
 BLOCK = 512
+CHUNK = 256
 KERNEL_BYTES = 48 * 1024 * 1024
 
 
 def attend_kernel(
-    order_ref, raw_ref, bias_ref, cosine_ref, sine_ref, growth_ref, begin_ref,
-    kept_ref, mixture_ref, log_ref, wide,
+    order_ref, first_ref, second_ref, third_ref, fourth_ref, weights_ref, bias_ref,
+    cosine_ref, sine_ref, growth_ref, begin_ref, kept_ref, mixture_ref, log_ref, wide,
 ):
-    tokens = raw_ref.shape[1]
+    step = pl.program_id(0)
+    part = first_ref.shape[1]
+    rows = mixture_ref.shape[2]
+    raw = bias_ref[...]
+    for index, piece in enumerate((first_ref, second_ref, third_ref, fourth_ref)):
+        raw = raw + dot(
+            weights_ref[:, index * part : (index + 1) * part], piece[...], CONTRACT_LAST
+        )
+    for block in range(CHUNK // rows):
+        place = order_ref[step * (CHUNK // rows) + block] * rows
+        wide[:, pl.ds(pl.multiple_of(place, rows), rows)] = raw[:, block * rows : (block + 1) * rows]
+
+    @pl.when(step == pl.num_programs(0) - 1)
+    def _():
+        attend_head(
+            cosine_ref, sine_ref, growth_ref, begin_ref, kept_ref, mixture_ref, log_ref, wide
+        )
+
+
+def attend_head(cosine_ref, sine_ref, growth_ref, begin_ref, kept_ref, mixture_ref, log_ref, wide):
+    tokens = wide.shape[1]
     half = HDIM // 2
     rows = tokens // SEQ
-    for block in range(SEQ):
-        place = pl.ds(pl.multiple_of(order_ref[block] * rows, rows), rows)
-        wide[:, block * rows : (block + 1) * rows] = raw_ref[:, place] + bias_ref[...]
     cosine, sine, growth = cosine_ref[...], sine_ref[...], growth_ref[...]
     first, second = wide[0:half, :], wide[half:HDIM, :]
     scaled = growth * HDIM ** (-0.5)
@@ -657,24 +683,35 @@
     return [pl.BlockSpec(memory_space=pltpu.VMEM) for _ in range(count)]
 
 
-def attend(order, raw, bias, cosine, sine, growth, begin):
-    tokens = raw.shape[1]
+def attend(order, pieces, weights, bias, cosine, sine, growth, begin):
+    tokens, part = pieces[0].shape
+    depth = weights.shape[1]
+    table = still((HDIM // 2, tokens))
     return pl.pallas_call(
         attend_kernel,
+        grid_spec=pltpu.PrefetchScalarGridSpec(
+            num_scalar_prefetch=1,
+            grid=(tokens // CHUNK,),
+            in_specs=[pl.BlockSpec((CHUNK, part), lambda i, order: (i, 0)) for _ in pieces]
+            + [still((3 * HDIM, depth)), still((3 * HDIM, 1)), table, table, table, still((1, tokens))],
+            out_specs=(
+                still((3 * HDIM, tokens)),
+                still((SEQ, HDIM, tokens // SEQ)),
+                still((1, tokens)),
+            ),
+            scratch_shapes=[pltpu.VMEM((3 * HDIM, tokens), F32)],
+        ),
         out_shape=(
             jax.ShapeDtypeStruct((3 * HDIM, tokens), BF),
             jax.ShapeDtypeStruct((SEQ, HDIM, tokens // SEQ), F32),
             jax.ShapeDtypeStruct((1, tokens), F32),
         ),
-        in_specs=[pl.BlockSpec(memory_space=pltpu.SMEM)] + whole(6),
-        out_specs=tuple(whole(3)),
-        scratch_shapes=[pltpu.VMEM((3 * HDIM, tokens), F32)],
         compiler_params=pltpu.CompilerParams(vmem_limit_bytes=KERNEL_BYTES),
         cost_estimate=pl.CostEstimate(
-            flops=2 * tokens * tokens * HDIM, bytes_accessed=8 * 192 * tokens,
+            flops=2 * tokens * tokens * HDIM, bytes_accessed=2 * tokens * depth,
             transcendentals=tokens * tokens // 2,
         ),
-    )(order, raw, bias, cosine, sine, growth, begin)
+    )(order, *pieces, weights, bias, cosine, sine, growth, begin)
 
 
 def retreat(order, kept, pull, mixture, logs, cosine, sine, growth, begin):
@@ -702,21 +739,117 @@
     )(order, kept, pull, mixture, logs, cosine, sine, growth, begin)
 
 
+def enter_kernel(
+    first_ref, second_ref, third_ref, fourth_ref, grad_ref, expand_ref, shift_ref, gain_ref,
+    active_ref, slope_ref, stats_ref,
+):
+    part = first_ref.shape[1]
+    raised = shift_ref[...]
+    for index, piece in enumerate((first_ref, second_ref, third_ref, fourth_ref)):
+        raised = raised + dot(piece[...], expand_ref[index * part : (index + 1) * part, :], PLAIN)
+    chance = 0.5 * (1.0 + lax.erf(raised * math.sqrt(0.5)))
+    active = raised * chance
+    active_ref[...] = active
+    slope_ref[...] = chance + raised * jnp.exp(raised * raised * -0.5) * (1.0 / math.sqrt(2.0 * math.pi))
+    scaled = grad_ref[...] * gain_ref[...]
+    lane = lax.broadcasted_iota(jnp.int32, (CHUNK, 128), 1)
+    columns = jnp.zeros((CHUNK, 128), F32)
+    for index, values in enumerate((active, active * active, scaled, scaled * active)):
+        columns = jnp.where(lane == index, jnp.sum(values, axis=1, keepdims=True), columns)
+    stats_ref[...] = columns.T[0:8, :]
+
+
+def leave_kernel(
+    active_ref, slope_ref, grad_ref, stats_ref, expand_ref, gain_ref, shift_ref,
+    shrunk_ref, low_ref, first_ref, second_ref, sums_ref,
+):
+    @pl.when(pl.program_id(0) == 0)
+    def _():
+        sums_ref[...] = jnp.zeros_like(sums_ref)
+
+    columns = jnp.concatenate([stats_ref[...], jnp.zeros((120, CHUNK), F32)], axis=0).T
+    average, scale, grad_mean, cross_mean = (columns[:, i : i + 1] for i in range(4))
+    hidden_grad = grad_ref[...]
+    normed = (active_ref[...] - average) * scale
+    shrunk_ref[...] = (normed * gain_ref[...] + shift_ref[...]).astype(BF)
+    raised_grad = (
+        scale * (hidden_grad * gain_ref[...] - grad_mean - normed * cross_mean) * slope_ref[...]
+    )
+    low = raised_grad.astype(BF)
+    low_ref[...] = low
+    sums_ref[0:1, :] += jnp.sum(hidden_grad * normed, axis=0, keepdims=True)
+    sums_ref[1:2, :] += jnp.sum(hidden_grad, axis=0, keepdims=True)
+    sums_ref[2:3, :] += jnp.sum(raised_grad, axis=0, keepdims=True)
+    part = first_ref.shape[1]
+    for index, out_ref in enumerate((first_ref, second_ref)):
+        out_ref[...] = dot(
+            low, expand_ref[index * part : (index + 1) * part, :], CONTRACT_LAST
+        ).astype(BF)
+
+
+def still(shape):
+    return pl.BlockSpec(shape, lambda *_: (0,) * len(shape))
+
+
+def enter(pieces, grad, expand_mine, shift, gain):
+    tokens, part = pieces[0].shape
+    depth, units = expand_mine.shape
+    block = pl.BlockSpec((CHUNK, units), lambda i: (i, 0))
+    wide = jax.ShapeDtypeStruct((tokens, units), F32)
+    return pl.pallas_call(
+        enter_kernel,
+        grid=(tokens // CHUNK,),
+        in_specs=[pl.BlockSpec((CHUNK, part), lambda i: (i, 0)) for _ in pieces]
+        + [block, still((depth, units)), still((1, units)), still((1, units))],
+        out_specs=(block, block, pl.BlockSpec((8, CHUNK), lambda i: (0, i))),
+        out_shape=(wide, wide, jax.ShapeDtypeStruct((8, tokens), F32)),
+        compiler_params=pltpu.CompilerParams(vmem_limit_bytes=KERNEL_BYTES),
+        cost_estimate=pl.CostEstimate(
+            flops=2 * tokens * depth * units, bytes_accessed=6 * tokens * depth, transcendentals=0
+        ),
+    )(*pieces, grad, expand_mine, shift, gain)
+
+
+def leave(active, slope, grad, stats, expand_other, gain, shift):
+    tokens, units = active.shape
+    depth = expand_other.shape[0]
+    block = pl.BlockSpec((CHUNK, units), lambda i: (i, 0))
+    piece = pl.BlockSpec((CHUNK, depth // 2), lambda i: (i, 0))
+    low = jax.ShapeDtypeStruct((tokens, units), BF)
+    partial_sum = jax.ShapeDtypeStruct((tokens, depth // 2), BF)
+    return pl.pallas_call(
+        leave_kernel,
+        grid=(tokens // CHUNK,),
+        in_specs=[block, block, block, pl.BlockSpec((8, CHUNK), lambda i: (0, i))]
+        + [still((depth, units)), still((1, units)), still((1, units))],
+        out_specs=(block, block, piece, piece, still((8, units))),
+        out_shape=(low, low) + (partial_sum,) * 2 + (jax.ShapeDtypeStruct((8, units), F32),),
+        compiler_params=pltpu.CompilerParams(vmem_limit_bytes=KERNEL_BYTES),
+        cost_estimate=pl.CostEstimate(
+            flops=2 * tokens * depth * units, bytes_accessed=6 * tokens * depth, transcendentals=0
+        ),
+    )(active, slope, grad, stats, expand_other, gain, shift)
+
+
 def to_owners(values):
     return lax.all_to_all(values, "seq", split_axis=0, concat_axis=0, tiled=True)
 
 
-def column_owners(weights, rows, side):
-    width = weights.shape[1] // SEQ
-    moved = to_owners(jnp.transpose(weights.reshape(rows, SEQ, width), (1, 0, 2)))
-    return turn_halves(side, moved.reshape(SEQ * rows, width))
-
-
-def row_owners(pieces, rows, side):
-    full = turn_halves(side, jnp.concatenate(pieces, axis=0).astype(BF))
-    width = full.shape[1]
-    moved = to_owners(full.reshape(SEQ, rows, width))
-    return jnp.transpose(moved, (1, 0, 2)).reshape(rows, SEQ * width).astype(F32)
+def by_owner(weights, rows):
+    return jnp.transpose(weights.reshape(rows, SEQ, -1), (1, 0, 2))
+
+
+def columns_of(moved, side):
+    return turn_halves(side, moved.reshape(-1, moved.shape[2]))
+
+
+def by_row_owner(pieces, side):
+    full = turn_halves(side, jnp.concatenate(pieces, axis=0))
+    return full.reshape(SEQ, -1, full.shape[1])
+
+
+def rows_of(moved):
+    return jnp.transpose(moved, (1, 0, 2)).reshape(moved.shape[1], -1).astype(F32)
 
 
 def head_shards(
@@ -759,11 +892,19 @@
         return lax.dynamic_slice_in_dim(vector, spot * size, size, axis=-1)
 
     first_out, first_normed, first_scale = norm_full(stream, first_gain, first_bias)
-    normed_pieces = gather_rows(mine(first_out.astype(BF)))
-    docs_near = gather_zxy(doc_ids[None, :]).reshape(SEQ, rows)
-    project_moved = to_owners(
-        jnp.transpose(project.reshape(rows, 3, SEQ, HDIM), (2, 1, 3, 0)).reshape(SEQ, 3 * HDIM, rows)
-    )
+    normed_column = gather_column(mine(first_out.astype(BF)))
+    docs_near = gather_small(doc_ids[None, :]).reshape(SEQ, rows)
+    full_combine = lax.all_gather(combine, "seq", axis=0, tiled=True)
+    out_grad_mine = mine(out_grad)
+    low_out = lax.all_gather(out_grad_mine.astype(BF), "seq", axis=0, tiled=True)
+    normed_column, project_own = after(
+        normed_column,
+        jnp.transpose(project.reshape(rows, 3, SEQ, HDIM), (2, 1, 3, 0)).reshape(
+            SEQ, 3 * HDIM, rows
+        ),
+    )
+    normed_pieces, _ = gather_plane(normed_column)
+    project_moved = to_owners(project_own)
     project_mine = turn_halves(
         side, jnp.transpose(project_moved, (1, 0, 2)).reshape(3 * HDIM, tokens), axis=1
     )
@@ -786,15 +927,12 @@
     )
     begin = begin[None, :]
 
-    raw = sum(
-        dot(weights, piece, CONTRACT_LAST)
-        for weights, piece in zip(project_pieces, normed_pieces, strict=True)
-    )
     head_bias = my_units(project_bias, HDIM).reshape(3 * HDIM, 1)
-    kept, mixture, logs = attend(order, raw, head_bias, cosine, sine, growth, begin)
+    kept, mixture, logs = attend(
+        order, normed_pieces, project_mine, head_bias, cosine, sine, growth, begin
+    )
 
     spread = to_owners(mixture).reshape(head_width, rows)
-    full_combine = lax.all_gather(combine, "seq", axis=0, tiled=True)
     sums = pair_sum(jnp.stack([jnp.sum(spread, axis=0), jnp.sum(spread * spread, axis=0)]))
     average = sums[0:1] / D
     inner_scale = lax.rsqrt(sums[1:2] / D - average * average + EPSILON)
@@ -809,62 +947,62 @@
     second_scale = lax.rsqrt((sums[1] / D)[:, None] - average * average + EPSILON)
     second_normed = (middle - average) * second_scale
     gain_half, bias_half = mine(second_gain), mine(second_bias)
-    expand_pieces = gather_rows((second_normed * gain_half + bias_half).astype(BF))
-
-    out_grad_mine = mine(out_grad)
-    low_out_pieces = gather_rows(out_grad_mine.astype(BF))
-    expand_mine = jnp.split(column_owners(expand, rows, side), 4, axis=0)
-    shrink_mine = jnp.split(column_owners(shrink, rows, side), 4, axis=0)
-    unit_gain, unit_bias = my_units(hidden_gain, width), my_units(hidden_bias, width)
-    hidden_grad = sum(
-        dot(piece, weights, PLAIN)
-        for piece, weights in zip(low_out_pieces, shrink_mine, strict=True)
-    )
-    raised = sum(
-        dot(piece, weights, PLAIN)
-        for piece, weights in zip(expand_pieces, expand_mine, strict=True)
-    ) + my_units(expand_bias, width)
-    active, gelu_back = jax.vjp(gelu_exact, raised)
-    scaled_grad = hidden_grad * unit_gain
-    sums = token_sum(
-        jnp.stack(
-            [
-                jnp.sum(active, axis=1),
-                jnp.sum(active * active, axis=1),
-                jnp.sum(scaled_grad, axis=1),
-                jnp.sum(scaled_grad * active, axis=1),
-            ]
+    expand_column = gather_column((second_normed * gain_half + bias_half).astype(BF))
+    expand_column, expand_own = after(expand_column, by_owner(expand, rows))
+    expand_moved = to_owners(expand_own)
+
+    def pull_back(left, right):
+        left, right, units, shrink_own, near = after(
+            left, right, expand_moved, by_owner(shrink, rows), low_out
         )
-    )
-    average = (sums[0] / FF)[:, None]
-    hidden_scale = lax.rsqrt((sums[1] / FF)[:, None] - average * average + EPSILON)
-    hidden_normed = (active - average) * hidden_scale
-    shrink_in = (hidden_normed * unit_gain + unit_bias).astype(BF)
-    grad_mean = (sums[2] / FF)[:, None]
-    cross_mean = hidden_scale * ((sums[3] / FF)[:, None] - average * grad_mean)
-    active_grad = hidden_scale * (scaled_grad - grad_mean - hidden_normed * cross_mean)
-    (raised_grad,) = gelu_back(active_grad)
-    low_raised = raised_grad.astype(BF)
-    second_grad = scatter_rows(
-        [dot(low_raised, weights, CONTRACT_LAST).astype(BF) for weights in expand_mine]
-    )
-    output_sum = scatter_rows(
-        [dot(shrink_in, weights, CONTRACT_LAST).astype(BF) for weights in shrink_mine]
-    )
-    output = middle + output_sum + mine(shrink_bias)
-    shrink_grad = row_owners(
-        [dot(piece, shrink_in, CONTRACT_FIRST) for piece in low_out_pieces], rows, side
-    )
-    expand_grad = row_owners(
-        [dot(piece, low_raised, CONTRACT_FIRST) for piece in expand_pieces], rows, side
-    )
-    unit_sums = jnp.stack(
-        [
-            jnp.sum(hidden_grad * hidden_normed, axis=0),
-            jnp.sum(hidden_grad, axis=0),
-            jnp.sum(raised_grad, axis=0),
-        ]
-    )
+        shrink_mine = columns_of(to_owners(shrink_own), side)
+        low = [near, hop(near, "t")]
+        grad = sum(
+            dot(piece, part, PLAIN)
+            for piece, part in zip(low, jnp.split(shrink_mine, 2, axis=0), strict=True)
+        )
+        grad = grad.reshape(SEQ, rows, width)[order].reshape(tokens, width)
+        return left, right, (low[0], low[1], grad, shrink_mine, columns_of(units, side))
+
+    expand_pieces, midway = gather_plane(expand_column, pull_back)
+    low_out, (hidden_grad, shrink_mine, expand_mine) = midway[:2], midway[2:]
+
+    unit_gain, unit_bias = my_units(hidden_gain, width)[None, :], my_units(hidden_bias, width)[None, :]
+    active, slope, sums = enter(
+        expand_pieces, hidden_grad, expand_mine, my_units(expand_bias, width)[None, :], unit_gain
+    )
+    sums, combined_late = after(token_sum(sums[0:4]), combined_in.T)
+    full_combined = lax.all_gather(combined_late, "seq", axis=0, tiled=True)
+    average = sums[0:1] / FF
+    hidden_scale = lax.rsqrt(sums[1:2] / FF - average * average + EPSILON)
+    grad_mean = sums[2:3] / FF
+    cross_mean = hidden_scale * (sums[3:4] / FF - average * grad_mean)
+    stats = jnp.concatenate(
+        [average, hidden_scale, grad_mean, cross_mean, jnp.zeros((4, tokens), F32)]
+    )
+    expand_parts = jnp.split(expand_mine, 4, axis=0)
+    left = leave(
+        active, slope, hidden_grad, stats, expand_mine[expand_mine.shape[0] // 2 :], unit_gain, unit_bias
+    )
+    pair, shrink_in, low_raised = after(
+        scatter_pair(left[1], (CONTRACT_LAST, expand_parts[:2]), left[2:4]), left[0], left[1]
+    )
+    shrink_far = shrink_in.reshape(SEQ, rows, width)[order].reshape(tokens, width)
+    shrink_term = by_row_owner(
+        [dot(piece, shrink_far, CONTRACT_FIRST).astype(BF) for piece in low_out], side
+    )
+    slabs, shrink_moved = after(scatter_plane(pair), to_owners(shrink_term))
+    shrink_grad = rows_of(shrink_moved)
+    second_grad = scatter_column(slabs)
+    expand_term = by_row_owner(
+        [dot(piece, low_raised, CONTRACT_FIRST).astype(BF) for piece in expand_pieces], side
+    )
+    shrink_parts = jnp.split(shrink_mine, 4, axis=0)
+    others = [dot(shrink_in, weights, CONTRACT_LAST).astype(BF) for weights in shrink_parts[2:]]
+    output_pair = scatter_pair(shrink_in, (CONTRACT_LAST, shrink_parts[:2]), others)
+    second_grad, expand_term, output_pair = after(second_grad, expand_term, output_pair)
+    expand_moved = to_owners(expand_term)
+    output_halves = scatter_wide(output_pair)
 
     scaled = second_grad * gain_half
     sums = pair_sum(jnp.stack([jnp.sum(scaled, axis=1), jnp.sum(scaled * second_normed, axis=1)]))
@@ -877,24 +1015,34 @@
     scaled = inner_grad * inner_gain[:, None]
     sums = pair_sum(jnp.stack([jnp.sum(scaled, axis=0), jnp.sum(scaled * inner_normed, axis=0)]))
     mixture_grad = inner_scale * (scaled - sums[0:1] / D - inner_normed * (sums[1:2] / D))
-    pull = to_owners(mixture_grad.astype(BF).reshape(SEQ, HDIM, rows))
-    combine_term = dot(low_middle, combined_in, (((0,), (1,)), ((), ()))).astype(BF)
-    combine_grad = lax.psum_scatter(
-        combine_term, "seq", scatter_dimension=0, tiled=True
-    ).astype(F32)
+    mixture_grad, expand_moved, output_halves, full_combined = after(
+        mixture_grad.astype(BF).reshape(SEQ, HDIM, rows), expand_moved, output_halves, full_combined
+    )
+    expand_grad = rows_of(expand_moved)
+    pull, low_middle, output_slabs = after(
+        to_owners(mixture_grad), low_middle, scatter_narrow(output_halves)
+    )
+    output = middle + scatter_column(output_slabs) + mine(shrink_bias)
+    moved = to_owners(by_owner(low_middle, rows))
 
     low_triple, head_sums = retreat(
         order, kept, pull, mixture, logs, cosine, sine, growth, begin
     )
-    first_grad = scatter_rows(
-        [dot(low_triple, weights, CONTRACT_FIRST).astype(BF) for weights in project_pieces]
-    )
+    others = [dot(low_triple, weights, CONTRACT_FIRST).astype(BF) for weights in project_pieces[2:]]
+    others, moved, output = after(others, moved, output)
+    combine_grad = dot(moved.reshape(tokens, -1), full_combined, CONTRACT_FIRST)
+    pair = scatter_pair(low_triple, (CONTRACT_FIRST, project_pieces[:2]), others)
     term = turn_halves(
         side,
-        jnp.concatenate([dot(low_triple, piece, PLAIN) for piece in normed_pieces], axis=1),
+        jnp.concatenate(
+            [dot(low_triple, piece, PLAIN).astype(BF) for piece in normed_pieces], axis=1
+        ),
         axis=1,
-    ).astype(BF)
+    )
+    pair[0], term = after(pair[0], term)
     moved = to_owners(jnp.transpose(term.reshape(3 * HDIM, SEQ, rows), (1, 0, 2)))
+    slabs, moved = after(scatter_plane(pair), moved)
+    first_grad = scatter_column(slabs)
     project_grad = jnp.transpose(moved.reshape(SEQ, 3, HDIM, rows), (3, 1, 0, 2)).reshape(
         rows, 3, head_width
     ).astype(F32)
@@ -905,25 +1053,28 @@
         scaled - (sums[0] / D)[:, None] - normed_half * (sums[1] / D)[:, None]
     )
 
+    unit_sums = lax.dynamic_update_slice(
+        jnp.zeros((3, SEQ * width), F32), left[4][0:3], (0, spot * width)
+    )
+    head_sums = lax.dynamic_update_slice(
+        jnp.zeros((3, head_width), F32), head_sums.reshape(3, HDIM), (0, spot * HDIM)
+    )
+    early = [
+        jnp.sum(out_grad_mine, axis=0),
+        jnp.sum(second_grad * second_normed, axis=0),
+        jnp.sum(second_grad, axis=0),
+        jnp.sum(middle_grad, axis=0),
+        jnp.sum(inner_grad * inner_normed, axis=1),
+        jnp.sum(inner_grad, axis=1),
+    ]
     early = seq_sum(
-        jnp.stack(
-            [
-                jnp.sum(out_grad_mine, axis=0),
-                jnp.sum(second_grad * second_normed, axis=0),
-                jnp.sum(second_grad, axis=0),
-                jnp.sum(middle_grad, axis=0),
-                jnp.sum(inner_grad * inner_normed, axis=1),
-                jnp.sum(inner_grad, axis=1),
-            ]
-        )
+        jnp.concatenate([jnp.stack(early), head_sums, unit_sums.reshape(-1, head_width)])
     )
     late = seq_sum(jnp.stack([jnp.sum(first_grad * normed_half, axis=0), jnp.sum(first_grad, axis=0)]))
-    halves = jnp.concatenate([early[:4], late])
-    halves = join_halves(side, halves, hop(halves, "t"))
-    unit_sums = gather_zxy(unit_sums).reshape(SEQ, 3, width)[order]
-    unit_sums = jnp.transpose(unit_sums, (1, 0, 2)).reshape(3, SEQ * width)
-    head_sums = gather_zxy(head_sums.reshape(3, HDIM)).reshape(SEQ, 3, HDIM)[order]
-    project_bias_grad = jnp.transpose(head_sums, (1, 0, 2)).reshape(3, head_width)
+    halves = join_halves(side, early[:4], hop(early[:4], "t"))
+    late = join_halves(side, late, hop(late, "t"))
+    project_bias_grad = early[6:9]
+    unit_sums = early[9:].reshape(3, SEQ * width)
     return (
         join_halves(side, output, hop(output, "t")),
         join_halves(side, stream_grad, hop(stream_grad, "t")),
@@ -935,8 +1086,8 @@
         unit_sums[2],
         shrink_grad,
         halves[0],
-        halves[4],
-        halves[5],
+        late[0],
+        late[1],
         early[4],
         early[5],
         halves[1],

time: 769 us -> 715 us (0.930)
  starting transfers between devices: 228 us -> 167 us
  blocking collectives: 0 us -> 31 us
  Pallas kernels: 15.5 us -> 38.7 us
  matrix products: 81.1 us -> 58.4 us
  other arithmetic: 58.2 us -> 46.2 us
    ppermute x87 -> x58, starting transfers between devices: 142 us -> 68.1 us  [hop(): return lax.ppermute(values, 'seq', HOPS[way])]
    all_to_all x0 -> x1, blocking collectives: none -> 31 us  [to_owners(): lax.all_to_all(values, 'seq', split_axis=0, concat_axis=0, tiled=True)]
    pallas_call x1 -> x3, Pallas kernels: 6.28 us -> 30 us  [the longest x1 12.4 us: attend(): pl.pallas_call(attend_kernel, grid_spec=pltpu.PrefetchScalarGridSpec(num_...]
    dot_general x39 -> x25, matrix products: 81.1 us -> 58.4 us  [dot(): return lax.dot_general(first, second, dims, preferred_element_type=F32)]
    all_to_all x8, starting transfers between devices: 44.7 us -> 61.1 us  [to_owners(): lax.all_to_all(values, 'seq', split_axis=0, concat_axis=0, tiled=True)]
    split x12 -> x0, local copies, waits for them, and re-layouts: 13.3 us -> none  [the longest x6 7.13 us: head_shards(): expand_mine = jnp.split(column_owners(expand, rows, side), 4, axis=0)]
    another operation x31 -> x16, other arithmetic: 20.5 us -> 8.26 us  [the longest x10 7.62 us: gather_along(): return jnp.stack([values, hop(values, way)], axis=axis)]
    ppermute x23, waiting for transfers between devices: 2.17 us -> 13.9 us  [hop(): return lax.ppermute(values, 'tp', [(0, 1), (1, 0)])]
  transfers between devices with their start and end apart: 120 -> 92, of which waited for: 51 -> 40; matrix products, arithmetic and copies ran while one was open for 21% -> 19% of each run, Pallas kernels for 2% -> 3%
where the time goes in v2:
time: 715 us; the launch traced here: 705 us
  waiting for transfers between devices  299 us (42%)
  starting transfers between devices  167 us (23%)
  matrix products  58.4 us (8%)
  local copies, waits for them, and re-layouts  48.7 us (7%)
  other arithmetic  46.2 us (6%)
  Pallas kernels  38.7 us (5%)
  blocking collectives  31 us (4%)
  between operations  15.8 us (2%)
    ppermute x58, waiting for transfers between devices, hop(): return lax.ppermute(values, 'seq', HOPS[way])  276 us
    ppermute x58, starting transfers between devices, hop(): return lax.ppermute(values, 'seq', HOPS[way])  68.1 us
    all_to_all x8, starting transfers between devices, to_owners(): lax.all_to_all(values, 'seq', split_axis=0, concat_axis=0, tiled=True)  61.1 us
    dot_general x25, matrix products, dot(): return lax.dot_general(first, second, dims, preferred_element_type=F32)  58.4 us
    ppermute x23, starting transfers between devices, hop(): return lax.ppermute(values, 'tp', [(0, 1), (1, 0)])  37.4 us
    all_to_all x1, blocking collectives, to_owners(): lax.all_to_all(values, 'seq', split_axis=0, concat_axis=0, tiled=True)  31 us
  transfers between devices with their start and end apart: 92, of which 40 were waited for; matrix products, arithmetic and copies ran while one was open for 19% of the time, Pallas kernels for 3%

profile of v2, /device:TPU:1, one launch (start us, length us, event | category | flops | bytes accessed | tf_op | source)
XLA Modules:
  0.0 704.8 jit_solution(11738241010424749629)
XLA Ops:
  25.1 15.9 %collective-permute-done.1 = bf16[128,1024]{1,0:T(8,128)(2,1)S(1)} collective-permute-done((bf16[128,1024]{1,0:T(8,128)(2,1)S(1)}, bf16[128,1024]{1,0:T(8,128)(2,1)S(1)}, u32[]{:S(2)}, u32[]{:S(2)}) %collective-permute-start.1) | collective-permute-done | bytes 262176 | tf_op jit(solution)/shard_map/ppermute | solution.py:438
  45.3 11.3 %collective-permute-done.5 = bf16[4,128,512]{2,1,0:T(8,128)(2,1)S(1)} collective-permute-done((bf16[4,128,512]{2,1,0:T(8,128)(2,1)S(1)}, bf16[4,128,512]{2,1,0:T(8,128)(2,1)S(1)}, u32[]{:S(2)}, u32[]{:S(2)}) %collective-permute-start.5) | collective-permute-done | bytes 524320 | tf_op jit(solution)/shard_map/ppermute | solution.py:438
  62.1 14.1 %all-to-all-start = ((bf16[16,192,128]{2,1,0:T(8,128)(2,1)}), bf16[16,192,128]{2,1,0:T(8,128)(2,1)}, u32[]{:S(2)}, u32[]{:S(2)}) async-start(bf16[16,192,128]{2,1,0:T(8,128)(2,1)} %bitcast.6), calls=%async_computation | async-start | bytes 1572864 | tf_op jit(solution)/shard_map/all_to_all | solution.py:835
  76.2 16.4 %collective-permute-done.6 = bf16[4,2,128,512]{3,2,0,1:T(8,128)(2,1)} collective-permute-done((bf16[4,2,128,512]{3,2,0,1:T(8,128)(2,1)S(1)}, bf16[4,2,128,512]{3,2,0,1:T(8,128)(2,1)}, u32[]{:S(2)}, u32[]{:S(2)}) %collective-permute-start.6) | collective-permute-done | bytes 1048608 | tf_op jit(solution)/shard_map/ppermute | solution.py:438
  95.5 11.5 %collective-permute-start.8 = (bf16[2048,512]{1,0:T(8,128)(2,1)}, bf16[2048,512]{1,0:T(8,128)(2,1)}, u32[]{:S(2)}, u32[]{:S(2)}) collective-permute-start(bf16[2048,512]{1,0:T(8,128)(2,1)} %bitcast.16.second_ref), channel_id=1, source_target_pairs={{0,1},{1,0},{2,3},{3,2},{4,5},{5,4},{6,7},{7,6},{8,9},{9,8},{10,11... | collective-permute-start | bytes 6291464 | tf_op jit(solution)/shard_map/ppermute | solution.py:437
  114.0 12.4 %shard_map.322 = (bf16[192,2048]{1,0:T(8,128)(2,1)S(1)}, f32[16,64,128]{2,1,0:T(8,128)S(1)}, f32[1,2048]{1,0:T(1,128)S(1)}) custom-call(s32[16]{0:T(128)S(1)} %fusion.39.order_ref, bf16[2048,512]{1,0:T(8,128)(2,1)S(1)} %bitcast.361, bf16[2048,512]{1,0:T(8,128)(2,1)} %bitcast.16.second_ref, bf16[2048,512]{1,0:T(8,128)(2,1)} %collective-permute-done.7.third_ref, ...), custom_call_target="tpu_custom_call" | custom-call | flops 536870912 | bytes 8388608 | tf_op jit(solution)/shard_map/pallas_call | solution.py:690
  126.4 31.0 %all_to_all.45 = f32[16,64,128]{2,1,0:T(8,128)S(1)} all-to-all(f32[16,64,128]{2,1,0:T(8,128)S(1)} %get-tuple-element.78.mixture_ref), channel_id=1, replica_groups=mesh['seq'=16,'tp'=2] {'seq'}, dimensions={0} | all-to-all | bytes 1048576 | tf_op jit(solution)/shard_map/all_to_all | solution.py:835
  173.8 6.5 collective-permute-done.17
  180.3 20.5 %collective-permute-done.18 = bf16[128,1024]{1,0:T(8,128)(2,1)S(1)} collective-permute-done((bf16[128,1024]{1,0:T(8,128)(2,1)S(1)}, bf16[128,1024]{1,0:T(8,128)(2,1)S(1)}, u32[]{:S(2)}, u32[]{:S(2)}) %collective-permute-start.18) | collective-permute-done | bytes 262176 | tf_op jit(solution)/shard_map/ppermute | solution.py:438
  200.9 18.5 %all-to-all-start.2 = ((bf16[16,128,256]{2,1,0:T(8,128)(2,1)}), bf16[16,128,256]{2,1,0:T(8,128)(2,1)S(1)}, u32[]{:S(2)}, u32[]{:S(2)}) async-start(bf16[16,128,256]{2,1,0:T(8,128)(2,1)} %bitcast.349), calls=%async_computation.2 | async-start | bytes 2097152 | tf_op jit(solution)/shard_map/all_to_all | solution.py:835
  223.3 19.6 %collective-permute-done.21 = bf16[4,128,512]{2,1,0:T(8,128)(2,1)S(1)} collective-permute-done((bf16[4,128,512]{2,1,0:T(8,128)(2,1)S(1)}, bf16[4,128,512]{2,1,0:T(8,128)(2,1)S(1)}, u32[]{:S(2)}, u32[]{:S(2)}) %collective-permute-start.21) | collective-permute-done | bytes 524320 | tf_op jit(solution)/shard_map/ppermute | solution.py:438
  254.4 33.0 %collective-permute-done.23 = bf16[4,2,128,512]{3,2,0,1:T(8,128)(2,1)S(1)} collective-permute-done((bf16[4,2,128,512]{3,2,0,1:T(8,128)(2,1)S(1)}, bf16[4,2,128,512]{3,2,0,1:T(8,128)(2,1)S(1)}, u32[]{:S(2)}, u32[]{:S(2)}) %collective-permute-start.23) | collective-permute-done | bytes 1048608 | tf_op jit(solution)/shard_map/ppermute | solution.py:438
  312.1 8.8 %shard_map.323 = (f32[2048,256]{1,0:T(8,128)S(1)}, f32[2048,256]{1,0:T(8,128)S(1)}, f32[8,2048]{1,0:T(8,128)S(1)}) custom-call(bf16[2048,512]{1,0:T(8,128)(2,1)} %bitcast.373, bf16[2048,512]{1,0:T(8,128)(2,1)} %bitcast.370, bf16[2048,512]{1,0:T(8,128)(2,1)} %collective-permute-done.25.third_ref, bf16[2048,512]{1,0:T(8,128)(2,1)} %collective-permute-done.26.fourth_ref, ...), custom_call_target="tpu_custom_call" | custom-call | flops 2147483648 | bytes 25165824 | tf_op jit(solution)/shard_map/pallas_call | solution.py:799
  339.2 8.9 %shard_map.324 = (bf16[2048,256]{1,0:T(8,128)(2,1)S(1)}, bf16[2048,256]{1,0:T(8,128)(2,1)S(1)}, bf16[2048,512]{1,0:T(8,128)(2,1)}, bf16[2048,512]{1,0:T(8,128)(2,1)}, f32[8,256]{1,0:T(8,128)S(1)}) custom-call(f32[2048,256]{1,0:T(8,128)} %copy-done.5, f32[2048,256]{1,0:T(8,128)} %copy-done.6, f32[2048,256]{1,0:T(8,128)} %bitcast.376, ...), custom_call_target="tpu_custom_call" | custom-call | flops 1073741824 | bytes 12582912 | tf_op jit(solution)/shard_map/pallas_call | solution.py:820
  391.5 29.9 %collective-permute-done.36 = bf16[4,2,128,512]{3,2,0,1:T(8,128)(2,1)S(1)} collective-permute-done((bf16[4,2,128,512]{3,2,0,1:T(8,128)(2,1)S(1)}, bf16[4,2,128,512]{3,2,0,1:T(8,128)(2,1)S(1)}, u32[]{:S(2)}, u32[]{:S(2)}) %collective-permute-start.36) | collective-permute-done | bytes 1048608 | tf_op jit(solution)/shard_map/ppermute | solution.py:438
  431.2 15.6 %collective-permute-done.37 = bf16[4,128,512]{2,1,0:T(8,128)(2,1)S(1)} collective-permute-done((bf16[4,128,512]{2,1,0:T(8,128)(2,1)S(1)}, bf16[4,128,512]{2,1,0:T(8,128)(2,1)S(1)}, u32[]{:S(2)}, u32[]{:S(2)}) %collective-permute-start.37) | collective-permute-done | bytes 524320 | tf_op jit(solution)/shard_map/ppermute | solution.py:438
  459.6 16.7 %collective-permute-done.41 = bf16[128,1024]{1,0:T(8,128)(2,1)S(1)} collective-permute-done((bf16[128,1024]{1,0:T(8,128)(2,1)S(1)}, bf16[128,1024]{1,0:T(8,128)(2,1)S(1)}, u32[]{:S(2)}, u32[]{:S(2)}) %collective-permute-start.41) | collective-permute-done | bytes 262176 | tf_op jit(solution)/shard_map/ppermute | solution.py:438
  495.0 15.2 %collective-permute-done.49 = bf16[4,2,128,512]{3,2,0,1:T(8,128)(2,1)} collective-permute-done((bf16[4,2,128,512]{3,2,0,1:T(8,128)(2,1)}, bf16[4,2,128,512]{3,2,0,1:T(8,128)(2,1)}, u32[]{:S(2)}, u32[]{:S(2)}) %collective-permute-start.49) | collective-permute-done | bytes 1048608 | tf_op jit(solution)/shard_map/ppermute | solution.py:438
  511.8 5.6 collective-permute-done.48
  547.3 8.7 %shard_map.325 = (bf16[192,2048]{1,0:T(8,128)(2,1)S(1)}, f32[192,1]{1,0:T(8,128)S(1)}) custom-call(s32[16]{0:T(128)S(1)} %fusion.39.order_ref, bf16[192,2048]{1,0:T(8,128)(2,1)S(1)} %copy-done.14, bf16[16,64,128]{2,1,0:T(8,128)(2,1)S(1)} %all-to-all-done.6.pull_ref, f32[16,64,128]{2,1,0:T(8,128)S(1)} %copy-done.12, ...), custom_call_target="tpu_custom_call" | custom-call | flops 1342177280 | bytes 3145728 | tf_op jit(solution)/shard_map/pallas_call | solution.py:719
  562.4 8.2 %all-to-all-done.7 = bf16[16,128,128]{2,1,0:T(8,128)(2,1)} async-done(((bf16[16,128,128]{2,1,0:T(8,128)(2,1)}), bf16[16,128,128]{2,1,0:T(8,128)(2,1)}, u32[]{:S(2)}, u32[]{:S(2)}) %all-to-all-start.7) | async-done | bytes 524320 | tf_op jit(solution)/shard_map/all_to_all | solution.py:835
  617.1 16.0 %collective-permute-done.57 = bf16[4,2,128,512]{3,2,0,1:T(8,128)(2,1)} collective-permute-done((bf16[4,2,128,512]{3,2,0,1:T(8,128)(2,1)}, bf16[4,2,128,512]{3,2,0,1:T(8,128)(2,1)}, u32[]{:S(2)}, u32[]{:S(2)}) %collective-permute-start.57) | collective-permute-done | bytes 1048608 | tf_op jit(solution)/shard_map/ppermute | solution.py:438
  643.0 8.2 %collective-permute-done.58 = bf16[4,128,512]{2,1,0:T(8,128)(2,1)S(1)} collective-permute-done((bf16[4,128,512]{2,1,0:T(8,128)(2,1)S(1)}, bf16[4,128,512]{2,1,0:T(8,128)(2,1)S(1)}, u32[]{:S(2)}, u32[]{:S(2)}) %collective-permute-start.58) | collective-permute-done | bytes 524320 | tf_op jit(solution)/shard_map/ppermute | solution.py:438
  657.7 18.4 %collective-permute-done.63 = bf16[128,1024]{1,0:T(8,128)(2,1)S(1)} collective-permute-done((bf16[128,1024]{1,0:T(8,128)(2,1)S(1)}, bf16[128,1024]{1,0:T(8,128)(2,1)S(1)}, u32[]{:S(2)}, u32[]{:S(2)}) %collective-permute-start.63) | collective-permute-done | bytes 262176 | tf_op jit(solution)/shard_map/ppermute | solution.py:438
  (497 shorter events, 318.2 us)
Async XLA Ops:
  7.2 153.7 %all-gather.4.cloned.1.call-start = ((), (), s32[]{:S(2)}) async-start(), calls=%async_computation.9 | async-start | bytes 4456448 | tf_op jit(solution)/shard_map/all_gather | solution.py:897
  7.9 236.2 %all-gather.6.cloned.1.call-start = ((), (), s32[]{:S(2)}) async-start(), calls=%async_computation.10 | async-start | bytes 4456448 | tf_op jit(solution)/shard_map/all_gather | solution.py:899
  8.0 37.0 %collective-permute-start.9 = (s32[1,128]{1,0:T(1,128)}, s32[1,128]{1,0:T(1,128)S(1)}, u32[]{:S(2)}, u32[]{:S(2)}) collective-permute-start(s32[1,128]{1,0:T(1,128)} %bitcast.463), channel_id=1, source_target_pairs={{0,8},{2,10},{4,12},{6,14},{8,16},{10,18},{12,20},{14,22},{16,24},... | collective-permute-start | bytes 1544 | tf_op jit(solution)/shard_map/ppermute | solution.py:438
  10.2 34.8 %collective-permute-start.10 = (s32[1,128]{1,0:T(1,128)}, s32[1,128]{1,0:T(1,128)S(1)}, u32[]{:S(2)}, u32[]{:S(2)}) collective-permute-start(s32[1,128]{1,0:T(1,128)} %bitcast.464), channel_id=1, source_target_pairs={{0,16},{2,18},{4,20},{6,22},{8,24},{10,26},{12,28},{14,30},{16,0},... | collective-permute-start | bytes 1544 | tf_op jit(solution)/shard_map/ppermute | solution.py:438
  56.7 35.8 %collective-permute-start.6 = (bf16[4,2,128,512]{3,2,0,1:T(8,128)(2,1)S(1)}, bf16[4,2,128,512]{3,2,0,1:T(8,128)(2,1)}, u32[]{:S(2)}, u32[]{:S(2)}) collective-permute-start(bf16[4,2,128,512]{3,2,0,1:T(8,128)(2,1)S(1)} %get-tuple-element.252), channel_id=1, source_target_pairs={{0,2},{2,0},{4,6},{6,4},{8,10},{10,8},{12,14},{14,12},{16,18},{18,... | collective-permute-start | bytes 3145736 | tf_op jit(solution)/shard_map/ppermute | solution.py:438
  60.7 46.3 %collective-permute-start.4 = (bf16[4,2,128,512]{3,2,0,1:T(8,128)(2,1)}, bf16[4,2,128,512]{3,2,0,1:T(8,128)(2,1)}, u32[]{:S(2)}, u32[]{:S(2)}) collective-permute-start(bf16[4,2,128,512]{3,2,0,1:T(8,128)(2,1)} %get-tuple-element.258), channel_id=1, source_target_pairs={{0,4},{2,6},{4,0},{6,2},{8,12},{10,14},{12,8},{14,10},{16,20},{18,... | collective-permute-start | bytes 3145736 | tf_op jit(solution)/shard_map/ppermute | solution.py:438
  62.1 47.9 %all-to-all-start = ((bf16[16,192,128]{2,1,0:T(8,128)(2,1)}), bf16[16,192,128]{2,1,0:T(8,128)(2,1)}, u32[]{:S(2)}, u32[]{:S(2)}) async-start(bf16[16,192,128]{2,1,0:T(8,128)(2,1)} %bitcast.6), calls=%async_computation | async-start | bytes 1572864 | tf_op jit(solution)/shard_map/all_to_all | solution.py:835
  200.9 43.2 %all-to-all-start.2 = ((bf16[16,128,256]{2,1,0:T(8,128)(2,1)}), bf16[16,128,256]{2,1,0:T(8,128)(2,1)S(1)}, u32[]{:S(2)}, u32[]{:S(2)}) async-start(bf16[16,128,256]{2,1,0:T(8,128)(2,1)} %bitcast.349), calls=%async_computation.2 | async-start | bytes 2097152 | tf_op jit(solution)/shard_map/all_to_all | solution.py:835
  244.1 51.4 %collective-permute-start.24 = (bf16[2048,1024]{1,0:T(8,128)(2,1)}, bf16[2048,1024]{1,0:T(8,128)(2,1)}, u32[]{:S(2)}, u32[]{:S(2)}) collective-permute-start(bf16[2048,1024]{1,0:T(8,128)(2,1)} %all-gather.6.cloned.1.call-done), channel_id=1, source_target_pairs={{0,1},{1,0},{2,3},{3,2},{4,5},{5,4},{6,7},{7,6},{8,9},{9,8},{10,11... | collective-permute-start | bytes 12582920 | tf_op jit(solution)/shard_map/ppermute | solution.py:437
  246.3 45.2 %all-to-all-start.3 = ((bf16[16,128,256]{2,1,0:T(8,128)(2,1)}), bf16[16,128,256]{2,1,0:T(8,128)(2,1)}, u32[]{:S(2)}, u32[]{:S(2)}) async-start(bf16[16,128,256]{2,1,0:T(8,128)(2,1)} %bitcast.347), calls=%async_computation.3 | async-start | bytes 2097152 | tf_op jit(solution)/shard_map/all_to_all | solution.py:835
  251.6 267.4 %all-gather.8.cloned.1.call-start = ((), (), s32[]{:S(2)}) async-start(), calls=%async_computation.11 | async-start | bytes 4456448 | tf_op jit(solution)/shard_map/all_gather | solution.py:975
  251.7 35.7 %collective-permute-start.23 = (bf16[4,2,128,512]{3,2,0,1:T(8,128)(2,1)S(1)}, bf16[4,2,128,512]{3,2,0,1:T(8,128)(2,1)S(1)}, u32[]{:S(2)}, u32[]{:S(2)}) collective-permute-start(bf16[4,2,128,512]{3,2,0,1:T(8,128)(2,1)S(1)} %pad_maximum_fusion.9), channel_id=1, source_target_pairs={{0,2},{2,0},{4,6},{6,4},{8,10},{10,8},{12,14},{14,12},{16,18},{18,... | collective-permute-start | bytes 3145736 | tf_op jit(solution)/shard_map/ppermute | solution.py:438
  253.0 34.7 %collective-permute-start.22 = (bf16[4,2,128,512]{3,2,0,1:T(8,128)(2,1)}, bf16[4,2,128,512]{3,2,0,1:T(8,128)(2,1)S(1)}, u32[]{:S(2)}, u32[]{:S(2)}) collective-permute-start(bf16[4,2,128,512]{3,2,0,1:T(8,128)(2,1)} %pad_maximum_fusion.8), channel_id=1, source_target_pairs={{0,4},{2,6},{4,0},{6,2},{8,12},{10,14},{12,8},{14,10},{16,20},{18,... | collective-permute-start | bytes 3145736 | tf_op jit(solution)/shard_map/ppermute | solution.py:438
  366.7 86.0 %collective-permute-start.44 = (bf16[2048,512]{1,0:T(8,128)(2,1)}, bf16[2048,512]{1,0:T(8,128)(2,1)}, u32[]{:S(2)}, u32[]{:S(2)}) collective-permute-start(bf16[2048,512]{1,0:T(8,128)(2,1)} %convolution_convert_fusion.2), channel_id=1, source_target_pairs={{0,1},{1,0},{2,3},{3,2},{4,5},{5,4},{6,7},{7,6},{8,9},{9,8},{10,11... | collective-permute-start | bytes 6291464 | tf_op jit(solution)/shard_map/ppermute | solution.py:437
  367.1 88.0 %collective-permute-start.43 = (bf16[2048,512]{1,0:T(8,128)(2,1)}, bf16[2048,512]{1,0:T(8,128)(2,1)}, u32[]{:S(2)}, u32[]{:S(2)}) collective-permute-start(bf16[2048,512]{1,0:T(8,128)(2,1)} %convolution_convert_fusion.3), channel_id=1, source_target_pairs={{0,1},{1,0},{2,3},{3,2},{4,5},{5,4},{6,7},{7,6},{8,9},{9,8},{10,11... | collective-permute-start | bytes 6291464 | tf_op jit(solution)/shard_map/ppermute | solution.py:437
  375.4 71.9 %all-to-all-start.4 = ((bf16[16,128,256]{2,1,0:T(8,128)(2,1)}), bf16[16,128,256]{2,1,0:T(8,128)(2,1)S(1)}, u32[]{:S(2)}, u32[]{:S(2)}) async-start(bf16[16,128,256]{2,1,0:T(8,128)(2,1)} %bitcast.388), calls=%async_computation.4 | async-start | bytes 2097152 | tf_op jit(solution)/shard_map/all_to_all | solution.py:835
  382.7 38.7 %collective-permute-start.36 = (bf16[4,2,128,512]{3,2,0,1:T(8,128)(2,1)S(1)}, bf16[4,2,128,512]{3,2,0,1:T(8,128)(2,1)S(1)}, u32[]{:S(2)}, u32[]{:S(2)}) collective-permute-start(bf16[4,2,128,512]{3,2,0,1:T(8,128)(2,1)S(1)} %bitcast.402), channel_id=1, source_target_pairs={{0,4},{2,6},{4,0},{6,2},{8,12},{10,14},{12,8},{14,10},{16,20},{18,... | collective-permute-start | bytes 3145736 | tf_op jit(solution)/shard_map/ppermute | solution.py:438
  384.5 43.8 %collective-permute-start.38 = (bf16[4,2,128,512]{3,2,0,1:T(8,128)(2,1)S(1)}, bf16[4,2,128,512]{3,2,0,1:T(8,128)(2,1)S(1)}, u32[]{:S(2)}, u32[]{:S(2)}) collective-permute-start(bf16[4,2,128,512]{3,2,0,1:T(8,128)(2,1)S(1)} %bitcast.401), channel_id=1, source_target_pairs={{0,2},{2,0},{4,6},{6,4},{8,10},{10,8},{12,14},{14,12},{16,18},{18,... | collective-permute-start | bytes 3145736 | tf_op jit(solution)/shard_map/ppermute | solution.py:438
  478.8 31.4 %collective-permute-start.49 = (bf16[4,2,128,512]{3,2,0,1:T(8,128)(2,1)}, bf16[4,2,128,512]{3,2,0,1:T(8,128)(2,1)}, u32[]{:S(2)}, u32[]{:S(2)}) collective-permute-start(bf16[4,2,128,512]{3,2,0,1:T(8,128)(2,1)} %bitcast.352), channel_id=1, source_target_pairs={{0,2},{2,0},{4,6},{6,4},{8,10},{10,8},{12,14},{14,12},{16,18},{18,... | collective-permute-start | bytes 3145736 | tf_op jit(solution)/shard_map/ppermute | solution.py:438
  482.7 34.7 %collective-permute-start.48 = (bf16[4,2,128,512]{3,2,0,1:T(8,128)(2,1)}, bf16[4,2,128,512]{3,2,0,1:T(8,128)(2,1)}, u32[]{:S(2)}, u32[]{:S(2)}) collective-permute-start(bf16[4,2,128,512]{3,2,0,1:T(8,128)(2,1)} %bitcast.353), channel_id=1, source_target_pairs={{0,4},{2,6},{4,0},{6,2},{8,12},{10,14},{12,8},{14,10},{16,20},{18,... | collective-permute-start | bytes 3145736 | tf_op jit(solution)/shard_map/ppermute | solution.py:438
  483.8 35.1 %all-to-all-start.5 = ((bf16[16,128,256]{2,1,0:T(8,128)(2,1)}), bf16[16,128,256]{2,1,0:T(8,128)(2,1)}, u32[]{:S(2)}, u32[]{:S(2)}) async-start(bf16[16,128,256]{2,1,0:T(8,128)(2,1)} %bitcast.85), calls=%async_computation.5 | async-start | bytes 2097152 | tf_op jit(solution)/shard_map/all_to_all | solution.py:835
  606.8 31.1 %collective-permute-start.60 = (bf16[4,2,128,512]{3,2,0,1:T(8,128)(2,1)}, bf16[4,2,128,512]{3,2,0,1:T(8,128)(2,1)}, u32[]{:S(2)}, u32[]{:S(2)}) collective-permute-start(bf16[4,2,128,512]{3,2,0,1:T(8,128)(2,1)} %bitcast.350), channel_id=1, source_target_pairs={{0,2},{2,0},{4,6},{6,4},{8,10},{10,8},{12,14},{14,12},{16,18},{18,... | collective-permute-start | bytes 3145736 | tf_op jit(solution)/shard_map/ppermute | solution.py:438
  610.3 44.7 %collective-permute-start.55 = (f32[128,1024]{1,0:T(8,128)}, f32[128,1024]{1,0:T(8,128)}, u32[]{:S(2)}, u32[]{:S(2)}) collective-permute-start(f32[128,1024]{1,0:T(8,128)} %fusion.17), channel_id=1, source_target_pairs={{0,1},{1,0},{2,3},{3,2},{4,5},{5,4},{6,7},{7,6},{8,9},{9,8},{10,11... | collective-permute-start | bytes 1572872 | tf_op jit(solution)/shard_map/ppermute | solution.py:437
  612.0 39.7 %all-to-all-start.8 = ((bf16[16,192,128]{2,1,0:T(8,128)(2,1)}), bf16[16,192,128]{2,1,0:T(8,128)(2,1)}, u32[]{:S(2)}, u32[]{:S(2)}) async-start(bf16[16,192,128]{2,1,0:T(8,128)(2,1)} %bitcast_bitcast_fusion.2), calls=%async_computation.8 | async-start | bytes 1572864 | tf_op jit(solution)/shard_map/all_to_all | solution.py:835
  (124 other events, 1346.5 us)
Sparse Core Ops, SparseCore 0:
  10.8 115.3 all-gather.3
  129.6 89.3 all-gather.5
  351.0 106.3 all-gather.7

commit v3 on v2

--- a/solution.py
+++ b/solution.py
@@ -551,12 +551,13 @@
 
 BLOCK = 512
 CHUNK = 256
+SPARE = 16
 KERNEL_BYTES = 48 * 1024 * 1024
 
 
 def attend_kernel(
     order_ref, first_ref, second_ref, third_ref, fourth_ref, weights_ref, bias_ref,
-    cosine_ref, sine_ref, growth_ref, begin_ref, kept_ref, mixture_ref, log_ref, wide,
+    cosine_ref, sine_ref, growth_ref, begin_ref, kept_ref, mixture_ref, sent_ref, log_ref, wide,
 ):
     step = pl.program_id(0)
     part = first_ref.shape[1]
@@ -573,11 +574,14 @@
     @pl.when(step == pl.num_programs(0) - 1)
     def _():
         attend_head(
-            cosine_ref, sine_ref, growth_ref, begin_ref, kept_ref, mixture_ref, log_ref, wide
+            cosine_ref, sine_ref, growth_ref, begin_ref, kept_ref, mixture_ref, sent_ref, log_ref,
+            wide,
         )
 
 
-def attend_head(cosine_ref, sine_ref, growth_ref, begin_ref, kept_ref, mixture_ref, log_ref, wide):
+def attend_head(
+    cosine_ref, sine_ref, growth_ref, begin_ref, kept_ref, mixture_ref, sent_ref, log_ref, wide
+):
     tokens = wide.shape[1]
     half = HDIM // 2
     rows = tokens // SEQ
@@ -592,6 +596,7 @@
     kept_ref[2 * HDIM :, :] = wide[2 * HDIM :, :].astype(BF)
     key_rows = lax.broadcasted_iota(jnp.int32, (BLOCK, BLOCK), 0)
     query_rows = lax.broadcasted_iota(jnp.int32, (BLOCK, BLOCK), 1)
+    spare = lax.broadcasted_iota(jnp.int32, (SPARE, BLOCK), 0)
     for i in range(tokens // BLOCK):
         columns = slice(i * BLOCK, (i + 1) * BLOCK)
         queries = kept_ref[0:HDIM, columns]
@@ -615,8 +620,15 @@
             )
             largest = newest
         mixture = summed / total
+        average = jnp.mean(mixture, axis=0, keepdims=True)
+        high = average.astype(BF).astype(F32)
+        low = (average - high).astype(BF).astype(F32)
+        tail = jnp.where(spare == 0, high, jnp.where(spare == 1, low, average - high - low))
+        sent = jnp.concatenate([mixture - average, jnp.where(spare < 3, tail, 0.0)], axis=0).astype(BF)
         for block in range(BLOCK // rows):
-            mixture_ref[i * (BLOCK // rows) + block] = mixture[:, block * rows : (block + 1) * rows]
+            place = slice(block * rows, (block + 1) * rows)
+            mixture_ref[i * (BLOCK // rows) + block] = mixture[:, place]
+            sent_ref[i * (BLOCK // rows) + block] = sent[:, place]
         log_ref[:, columns] = largest + jnp.log(total)
 
 
@@ -697,6 +709,7 @@
             out_specs=(
                 still((3 * HDIM, tokens)),
                 still((SEQ, HDIM, tokens // SEQ)),
+                still((SEQ, HDIM + SPARE, tokens // SEQ)),
                 still((1, tokens)),
             ),
             scratch_shapes=[pltpu.VMEM((3 * HDIM, tokens), F32)],
@@ -704,6 +717,7 @@
         out_shape=(
             jax.ShapeDtypeStruct((3 * HDIM, tokens), BF),
             jax.ShapeDtypeStruct((SEQ, HDIM, tokens // SEQ), F32),
+            jax.ShapeDtypeStruct((SEQ, HDIM + SPARE, tokens // SEQ), BF),
             jax.ShapeDtypeStruct((1, tokens), F32),
         ),
         compiler_params=pltpu.CompilerParams(vmem_limit_bytes=KERNEL_BYTES),
@@ -928,11 +942,13 @@
     begin = begin[None, :]
 
     head_bias = my_units(project_bias, HDIM).reshape(3 * HDIM, 1)
-    kept, mixture, logs = attend(
+    kept, mixture, sent, logs = attend(
         order, normed_pieces, project_mine, head_bias, cosine, sine, growth, begin
     )
 
-    spread = to_owners(mixture).reshape(head_width, rows)
+    sent = to_owners(sent).astype(F32)
+    averages = jnp.sum(sent[:, HDIM : HDIM + 3], axis=1, keepdims=True)
+    spread = (sent[:, :HDIM] + averages).reshape(head_width, rows)
     sums = pair_sum(jnp.stack([jnp.sum(spread, axis=0), jnp.sum(spread * spread, axis=0)]))
     average = sums[0:1] / D
     inner_scale = lax.rsqrt(sums[1:2] / D - average * average + EPSILON)
@@ -948,24 +964,24 @@
     second_normed = (middle - average) * second_scale
     gain_half, bias_half = mine(second_gain), mine(second_bias)
     expand_column = gather_column((second_normed * gain_half + bias_half).astype(BF))
-    expand_column, expand_own = after(expand_column, by_owner(expand, rows))
-    expand_moved = to_owners(expand_own)
+    expand_column, shrink_own = after(expand_column, by_owner(shrink, rows))
+    shrink_moved = to_owners(shrink_own)
 
     def pull_back(left, right):
-        left, right, units, shrink_own, near = after(
-            left, right, expand_moved, by_owner(shrink, rows), low_out
-        )
-        shrink_mine = columns_of(to_owners(shrink_own), side)
+        left, right, units, expand_own = after(left, right, shrink_moved, by_owner(expand, rows))
+        _, near = after(left, low_out)
+        shrink_mine = columns_of(units, side)
         low = [near, hop(near, "t")]
         grad = sum(
             dot(piece, part, PLAIN)
             for piece, part in zip(low, jnp.split(shrink_mine, 2, axis=0), strict=True)
         )
         grad = grad.reshape(SEQ, rows, width)[order].reshape(tokens, width)
-        return left, right, (low[0], low[1], grad, shrink_mine, columns_of(units, side))
+        return left, right, (low[0], low[1], grad, shrink_mine, to_owners(expand_own))
 
     expand_pieces, midway = gather_plane(expand_column, pull_back)
-    low_out, (hidden_grad, shrink_mine, expand_mine) = midway[:2], midway[2:]
+    low_out, (hidden_grad, shrink_mine) = midway[:2], midway[2:4]
+    expand_mine = columns_of(midway[4], side)
 
     unit_gain, unit_bias = my_units(hidden_gain, width)[None, :], my_units(hidden_bias, width)[None, :]
     active, slope, sums = enter(
@@ -991,7 +1007,8 @@
     shrink_term = by_row_owner(
         [dot(piece, shrink_far, CONTRACT_FIRST).astype(BF) for piece in low_out], side
     )
-    slabs, shrink_moved = after(scatter_plane(pair), to_owners(shrink_term))
+    halves, shrink_in = after(scatter_wide(pair), shrink_in)
+    slabs, shrink_moved = after(scatter_narrow(halves), to_owners(shrink_term))
     shrink_grad = rows_of(shrink_moved)
     second_grad = scatter_column(slabs)
     expand_term = by_row_owner(

time: 715 us -> 700 us (0.979)
  waiting for transfers between devices: 299 us -> 283 us
    ppermute x58, waiting for transfers between devices: 276 us -> 248 us  [hop(): return lax.ppermute(values, 'seq', HOPS[way])]
    all_to_all x8, waiting for transfers between devices: 8.22 us -> 20.9 us  [to_owners(): lax.all_to_all(values, 'seq', split_axis=0, concat_axis=0, tiled=True)]
    unnamed x123 -> x143, local copies, waits for them, and re-layouts: 14.2 us -> 16.6 us
  transfers between devices with their start and end apart: 92 -> 92, of which waited for: 40 -> 40; matrix products, arithmetic and copies ran while one was open for 19% -> 21% of each run, Pallas kernels for 3% -> 3%
where the time goes in v3:
time: 700 us; the launch traced here: 690 us
  waiting for transfers between devices  283 us (40%)
  starting transfers between devices  169 us (24%)
  matrix products  58.4 us (8%)
  local copies, waits for them, and re-layouts  51.1 us (7%)
  other arithmetic  46.6 us (7%)
  Pallas kernels  38.7 us (6%)
  blocking collectives  27.1 us (4%)
  between operations  15.9 us (2%)
    ppermute x58, waiting for transfers between devices, hop(): return lax.ppermute(values, 'seq', HOPS[way])  248 us
    all_to_all x8, starting transfers between devices, to_owners(): lax.all_to_all(values, 'seq', split_axis=0, concat_axis=0, tiled=True)  65.2 us
    ppermute x58, starting transfers between devices, hop(): return lax.ppermute(values, 'seq', HOPS[way])  63.3 us
    dot_general x25, matrix products, dot(): return lax.dot_general(first, second, dims, preferred_element_type=F32)  58.4 us
    ppermute x23, starting transfers between devices, hop(): return lax.ppermute(values, 'tp', [(0, 1), (1, 0)])  40.3 us
    all_to_all x1, blocking collectives, to_owners(): lax.all_to_all(values, 'seq', split_axis=0, concat_axis=0, tiled=True)  27.1 us
    all_to_all x8, waiting for transfers between devices, to_owners(): lax.all_to_all(values, 'seq', split_axis=0, concat_axis=0, tiled=True)  20.9 us
    unnamed x143, local copies, waits for them, and re-layouts  16.6 us
  transfers between devices with their start and end apart: 92, of which 40 were waited for; matrix products, arithmetic and copies ran while one was open for 21% of the time, Pallas kernels for 3%

profile of v3, /device:TPU:1, one launch (start us, length us, event | category | flops | bytes accessed | tf_op | source)
XLA Modules:
  0.0 690.1 jit_solution(18391560145611948252)
XLA Ops:
  25.1 15.9 %collective-permute-done.1 = bf16[128,1024]{1,0:T(8,128)(2,1)S(1)} collective-permute-done((bf16[128,1024]{1,0:T(8,128)(2,1)S(1)}, bf16[128,1024]{1,0:T(8,128)(2,1)S(1)}, u32[]{:S(2)}, u32[]{:S(2)}) %collective-permute-start.1) | collective-permute-done | bytes 262176 | tf_op jit(solution)/shard_map/ppermute | solution.py:438
  45.3 11.2 %collective-permute-done.5 = bf16[4,128,512]{2,1,0:T(8,128)(2,1)S(1)} collective-permute-done((bf16[4,128,512]{2,1,0:T(8,128)(2,1)S(1)}, bf16[4,128,512]{2,1,0:T(8,128)(2,1)S(1)}, u32[]{:S(2)}, u32[]{:S(2)}) %collective-permute-start.5) | collective-permute-done | bytes 524320 | tf_op jit(solution)/shard_map/ppermute | solution.py:438
  62.8 13.3 %all-to-all-start = ((bf16[16,192,128]{2,1,0:T(8,128)(2,1)}), bf16[16,192,128]{2,1,0:T(8,128)(2,1)}, u32[]{:S(2)}, u32[]{:S(2)}) async-start(bf16[16,192,128]{2,1,0:T(8,128)(2,1)} %bitcast.6), calls=%async_computation | async-start | bytes 1572864 | tf_op jit(solution)/shard_map/all_to_all | solution.py:849
  76.1 17.7 %collective-permute-done.6 = bf16[4,2,128,512]{3,2,0,1:T(8,128)(2,1)} collective-permute-done((bf16[4,2,128,512]{3,2,0,1:T(8,128)(2,1)}, bf16[4,2,128,512]{3,2,0,1:T(8,128)(2,1)}, u32[]{:S(2)}, u32[]{:S(2)}) %collective-permute-start.6) | collective-permute-done | bytes 1048608 | tf_op jit(solution)/shard_map/ppermute | solution.py:438
  96.9 10.4 %collective-permute-start.8 = (bf16[2048,512]{1,0:T(8,128)(2,1)}, bf16[2048,512]{1,0:T(8,128)(2,1)}, u32[]{:S(2)}, u32[]{:S(2)}) collective-permute-start(bf16[2048,512]{1,0:T(8,128)(2,1)} %bitcast.16.second_ref), channel_id=1, source_target_pairs={{0,1},{1,0},{2,3},{3,2},{4,5},{5,4},{6,7},{7,6},{8,9},{9,8},{10,11... | collective-permute-start | bytes 6291464 | tf_op jit(solution)/shard_map/ppermute | solution.py:437
  114.2 12.4 %shard_map.322 = (bf16[192,2048]{1,0:T(8,128)(2,1)S(1)}, f32[16,64,128]{2,1,0:T(8,128)S(1)}, bf16[16,80,128]{2,1,0:T(8,128)(2,1)S(1)}, f32[1,2048]{1,0:T(1,128)S(1)}) custom-call(s32[16]{0:T(128)S(1)} %fusion.37.order_ref, bf16[2048,512]{1,0:T(8,128)(2,1)S(1)} %bitcast.361, bf16[2048,512]{1,0:T(8,128)(2,1)} %bitcast.16.second_ref, ...), custom_call_target="tpu_custom_call" | custom-call | flops 536870912 | bytes 8388608 | tf_op jit(solution)/shard_map/pallas_call | solution.py:702
  127.5 27.1 %all_to_all.45 = bf16[16,80,128]{2,1,0:T(8,128)(2,1)S(1)} all-to-all(bf16[16,80,128]{2,1,0:T(8,128)(2,1)S(1)} %get-tuple-element.82), channel_id=1, replica_groups=mesh['seq'=16,'tp'=2] {'seq'}, dimensions={0} | all-to-all | bytes 655360 | tf_op jit(solution)/shard_map/all_to_all | solution.py:849
  168.8 10.1 %collective-permute-done.17 = bf16[128,1024]{1,0:T(8,128)(2,1)S(1)} collective-permute-done((bf16[128,1024]{1,0:T(8,128)(2,1)S(1)}, bf16[128,1024]{1,0:T(8,128)(2,1)S(1)}, u32[]{:S(2)}, u32[]{:S(2)}) %collective-permute-start.17) | collective-permute-done | bytes 262176 | tf_op jit(solution)/shard_map/ppermute | solution.py:438
  178.9 11.6 %collective-permute-done.18 = bf16[128,1024]{1,0:T(8,128)(2,1)S(1)} collective-permute-done((bf16[128,1024]{1,0:T(8,128)(2,1)S(1)}, bf16[128,1024]{1,0:T(8,128)(2,1)S(1)}, u32[]{:S(2)}, u32[]{:S(2)}) %collective-permute-start.18) | collective-permute-done | bytes 262176 | tf_op jit(solution)/shard_map/ppermute | solution.py:438
  190.6 14.4 %all-to-all-start.2 = ((bf16[16,128,256]{2,1,0:T(8,128)(2,1)}), bf16[16,128,256]{2,1,0:T(8,128)(2,1)S(1)}, u32[]{:S(2)}, u32[]{:S(2)}) async-start(bf16[16,128,256]{2,1,0:T(8,128)(2,1)} %bitcast.391), calls=%async_computation.2 | async-start | bytes 2097152 | tf_op jit(solution)/shard_map/all_to_all | solution.py:849
  209.0 16.6 %collective-permute-done.21 = bf16[4,128,512]{2,1,0:T(8,128)(2,1)S(1)} collective-permute-done((bf16[4,128,512]{2,1,0:T(8,128)(2,1)S(1)}, bf16[4,128,512]{2,1,0:T(8,128)(2,1)S(1)}, u32[]{:S(2)}, u32[]{:S(2)}) %collective-permute-start.21) | collective-permute-done | bytes 524320 | tf_op jit(solution)/shard_map/ppermute | solution.py:438
  226.7 10.8 %all-to-all-done.2 = bf16[16,128,256]{2,1,0:T(8,128)(2,1)S(1)} async-done(((bf16[16,128,256]{2,1,0:T(8,128)(2,1)}), bf16[16,128,256]{2,1,0:T(8,128)(2,1)S(1)}, u32[]{:S(2)}, u32[]{:S(2)}) %all-to-all-start.2) | async-done | bytes 1048608 | tf_op jit(solution)/shard_map/all_to_all | solution.py:849
  250.2 30.7 %collective-permute-done.23 = bf16[4,2,128,512]{3,2,0,1:T(8,128)(2,1)S(1)} collective-permute-done((bf16[4,2,128,512]{3,2,0,1:T(8,128)(2,1)S(1)}, bf16[4,2,128,512]{3,2,0,1:T(8,128)(2,1)S(1)}, u32[]{:S(2)}, u32[]{:S(2)}) %collective-permute-start.23) | collective-permute-done | bytes 1048608 | tf_op jit(solution)/shard_map/ppermute | solution.py:438
  300.8 8.8 %shard_map.323 = (f32[2048,256]{1,0:T(8,128)S(1)}, f32[2048,256]{1,0:T(8,128)S(1)}, f32[8,2048]{1,0:T(8,128)S(1)}) custom-call(bf16[2048,512]{1,0:T(8,128)(2,1)} %bitcast.375, bf16[2048,512]{1,0:T(8,128)(2,1)} %bitcast.372, bf16[2048,512]{1,0:T(8,128)(2,1)} %collective-permute-done.25.third_ref, bf16[2048,512]{1,0:T(8,128)(2,1)} %collective-permute-done.26.fourth_ref, ...), custom_call_target="tpu_custom_call" | custom-call | flops 2147483648 | bytes 25165824 | tf_op jit(solution)/shard_map/pallas_call | solution.py:813
  326.3 8.9 %shard_map.324 = (bf16[2048,256]{1,0:T(8,128)(2,1)S(1)}, bf16[2048,256]{1,0:T(8,128)(2,1)S(1)}, bf16[2048,512]{1,0:T(8,128)(2,1)}, bf16[2048,512]{1,0:T(8,128)(2,1)}, f32[8,256]{1,0:T(8,128)S(1)}) custom-call(f32[2048,256]{1,0:T(8,128)} %copy-done.4, f32[2048,256]{1,0:T(8,128)} %copy-done.5, f32[2048,256]{1,0:T(8,128)} %bitcast.378, ...), custom_call_target="tpu_custom_call" | custom-call | flops 1073741824 | bytes 12582912 | tf_op jit(solution)/shard_map/pallas_call | solution.py:834
  398.6 17.4 %collective-permute-done.38 = bf16[4,128,512]{2,1,0:T(8,128)(2,1)S(1)} collective-permute-done((bf16[4,128,512]{2,1,0:T(8,128)(2,1)S(1)}, bf16[4,128,512]{2,1,0:T(8,128)(2,1)S(1)}, u32[]{:S(2)}, u32[]{:S(2)}) %collective-permute-start.38) | collective-permute-done | bytes 524320 | tf_op jit(solution)/shard_map/ppermute | solution.py:438
  425.5 7.5 %collective-permute-done.40 = bf16[128,1024]{1,0:T(8,128)(2,1)S(1)} collective-permute-done((bf16[128,1024]{1,0:T(8,128)(2,1)S(1)}, bf16[128,1024]{1,0:T(8,128)(2,1)S(1)}, u32[]{:S(2)}, u32[]{:S(2)}) %collective-permute-start.40) | collective-permute-done | bytes 262176 | tf_op jit(solution)/shard_map/ppermute | solution.py:438
  433.0 19.4 %collective-permute-done.41 = bf16[128,1024]{1,0:T(8,128)(2,1)S(1)} collective-permute-done((bf16[128,1024]{1,0:T(8,128)(2,1)S(1)}, bf16[128,1024]{1,0:T(8,128)(2,1)S(1)}, u32[]{:S(2)}, u32[]{:S(2)}) %collective-permute-start.41) | collective-permute-done | bytes 262176 | tf_op jit(solution)/shard_map/ppermute | solution.py:438
  477.5 14.2 %collective-permute-done.49 = bf16[4,2,128,512]{3,2,0,1:T(8,128)(2,1)} collective-permute-done((bf16[4,2,128,512]{3,2,0,1:T(8,128)(2,1)}, bf16[4,2,128,512]{3,2,0,1:T(8,128)(2,1)}, u32[]{:S(2)}, u32[]{:S(2)}) %collective-permute-start.49) | collective-permute-done | bytes 1048608 | tf_op jit(solution)/shard_map/ppermute | solution.py:438
  531.4 8.6 %shard_map.325 = (bf16[192,2048]{1,0:T(8,128)(2,1)S(1)}, f32[192,1]{1,0:T(8,128)S(1)}) custom-call(s32[16]{0:T(128)S(1)} %fusion.37.order_ref, bf16[192,2048]{1,0:T(8,128)(2,1)S(1)} %copy-done.9, bf16[16,64,128]{2,1,0:T(8,128)(2,1)S(1)} %all-to-all-done.6.pull_ref, f32[16,64,128]{2,1,0:T(8,128)S(1)} %copy-done.11, f32[1,2048]{1,0:T(1,128)S(1)} %get-tuple-element.123.log_ref, ...), custom_call_target="tpu_custom_call" | custom-call | flops 1342177280 | bytes 3145728 | tf_op jit(solution)/shard_map/pallas_call | solution.py:733
  545.8 10.0 %all-to-all-done.7 = bf16[16,128,128]{2,1,0:T(8,128)(2,1)} async-done(((bf16[16,128,128]{2,1,0:T(8,128)(2,1)}), bf16[16,128,128]{2,1,0:T(8,128)(2,1)}, u32[]{:S(2)}, u32[]{:S(2)}) %all-to-all-start.7) | async-done | bytes 524320 | tf_op jit(solution)/shard_map/all_to_all | solution.py:849
  602.1 18.6 %collective-permute-done.57 = bf16[4,2,128,512]{3,2,0,1:T(8,128)(2,1)} collective-permute-done((bf16[4,2,128,512]{3,2,0,1:T(8,128)(2,1)}, bf16[4,2,128,512]{3,2,0,1:T(8,128)(2,1)}, u32[]{:S(2)}, u32[]{:S(2)}) %collective-permute-start.57) | collective-permute-done | bytes 1048608 | tf_op jit(solution)/shard_map/ppermute | solution.py:438
  628.7 8.0 %collective-permute-done.58 = bf16[4,128,512]{2,1,0:T(8,128)(2,1)S(1)} collective-permute-done((bf16[4,128,512]{2,1,0:T(8,128)(2,1)S(1)}, bf16[4,128,512]{2,1,0:T(8,128)(2,1)S(1)}, u32[]{:S(2)}, u32[]{:S(2)}) %collective-permute-start.58) | collective-permute-done | bytes 524320 | tf_op jit(solution)/shard_map/ppermute | solution.py:438
  643.3 18.8 %collective-permute-done.63 = bf16[128,1024]{1,0:T(8,128)(2,1)S(1)} collective-permute-done((bf16[128,1024]{1,0:T(8,128)(2,1)S(1)}, bf16[128,1024]{1,0:T(8,128)(2,1)S(1)}, u32[]{:S(2)}, u32[]{:S(2)}) %collective-permute-start.63) | collective-permute-done | bytes 262176 | tf_op jit(solution)/shard_map/ppermute | solution.py:438
  (519 shorter events, 331.6 us)
Async XLA Ops:
  7.2 149.2 %all-gather.4.cloned.1.call-start = ((), (), s32[]{:S(2)}) async-start(), calls=%async_computation.9 | async-start | bytes 4456448 | tf_op jit(solution)/shard_map/all_gather | solution.py:911
  7.9 229.6 %all-gather.6.cloned.1.call-start = ((), (), s32[]{:S(2)}) async-start(), calls=%async_computation.10 | async-start | bytes 4456448 | tf_op jit(solution)/shard_map/all_gather | solution.py:913
  8.0 37.0 %collective-permute-start.9 = (s32[1,128]{1,0:T(1,128)}, s32[1,128]{1,0:T(1,128)S(1)}, u32[]{:S(2)}, u32[]{:S(2)}) collective-permute-start(s32[1,128]{1,0:T(1,128)} %bitcast.467), channel_id=1, source_target_pairs={{0,8},{2,10},{4,12},{6,14},{8,16},{10,18},{12,20},{14,22},{16,24},... | collective-permute-start | bytes 1544 | tf_op jit(solution)/shard_map/ppermute | solution.py:438
  10.2 34.8 %collective-permute-start.10 = (s32[1,128]{1,0:T(1,128)}, s32[1,128]{1,0:T(1,128)S(1)}, u32[]{:S(2)}, u32[]{:S(2)}) collective-permute-start(s32[1,128]{1,0:T(1,128)} %bitcast.468), channel_id=1, source_target_pairs={{0,16},{2,18},{4,20},{6,22},{8,24},{10,26},{12,28},{14,30},{16,0},... | collective-permute-start | bytes 1544 | tf_op jit(solution)/shard_map/ppermute | solution.py:438
  57.6 36.2 %collective-permute-start.6 = (bf16[4,2,128,512]{3,2,0,1:T(8,128)(2,1)}, bf16[4,2,128,512]{3,2,0,1:T(8,128)(2,1)}, u32[]{:S(2)}, u32[]{:S(2)}) collective-permute-start(bf16[4,2,128,512]{3,2,0,1:T(8,128)(2,1)} %get-tuple-element.261), channel_id=1, source_target_pairs={{0,2},{2,0},{4,6},{6,4},{8,10},{10,8},{12,14},{14,12},{16,18},{18,... | collective-permute-start | bytes 3145736 | tf_op jit(solution)/shard_map/ppermute | solution.py:438
  61.5 45.8 %collective-permute-start.4 = (bf16[4,2,128,512]{3,2,0,1:T(8,128)(2,1)}, bf16[4,2,128,512]{3,2,0,1:T(8,128)(2,1)S(1)}, u32[]{:S(2)}, u32[]{:S(2)}) collective-permute-start(bf16[4,2,128,512]{3,2,0,1:T(8,128)(2,1)} %get-tuple-element.267), channel_id=1, source_target_pairs={{0,4},{2,6},{4,0},{6,2},{8,12},{10,14},{12,8},{14,10},{16,20},{18,... | collective-permute-start | bytes 3145736 | tf_op jit(solution)/shard_map/ppermute | solution.py:438
  62.8 48.3 %all-to-all-start = ((bf16[16,192,128]{2,1,0:T(8,128)(2,1)}), bf16[16,192,128]{2,1,0:T(8,128)(2,1)}, u32[]{:S(2)}, u32[]{:S(2)}) async-start(bf16[16,192,128]{2,1,0:T(8,128)(2,1)} %bitcast.6), calls=%async_computation | async-start | bytes 1572864 | tf_op jit(solution)/shard_map/all_to_all | solution.py:849
  190.6 46.9 %all-to-all-start.2 = ((bf16[16,128,256]{2,1,0:T(8,128)(2,1)}), bf16[16,128,256]{2,1,0:T(8,128)(2,1)S(1)}, u32[]{:S(2)}, u32[]{:S(2)}) async-start(bf16[16,128,256]{2,1,0:T(8,128)(2,1)} %bitcast.391), calls=%async_computation.2 | async-start | bytes 2097152 | tf_op jit(solution)/shard_map/all_to_all | solution.py:849
  237.5 46.7 %collective-permute-start.24 = (bf16[2048,1024]{1,0:T(8,128)(2,1)}, bf16[2048,1024]{1,0:T(8,128)(2,1)}, u32[]{:S(2)}, u32[]{:S(2)}) collective-permute-start(bf16[2048,1024]{1,0:T(8,128)(2,1)} %all-gather.6.cloned.1.call-done), channel_id=1, source_target_pairs={{0,1},{1,0},{2,3},{3,2},{4,5},{5,4},{6,7},{7,6},{8,9},{9,8},{10,11... | collective-permute-start | bytes 12582920 | tf_op jit(solution)/shard_map/ppermute | solution.py:437
  238.4 54.3 %all-to-all-start.3 = ((bf16[16,128,256]{2,1,0:T(8,128)(2,1)}), bf16[16,128,256]{2,1,0:T(8,128)(2,1)}, u32[]{:S(2)}, u32[]{:S(2)}) async-start(bf16[16,128,256]{2,1,0:T(8,128)(2,1)} %bitcast.347), calls=%async_computation.3 | async-start | bytes 2097152 | tf_op jit(solution)/shard_map/all_to_all | solution.py:849
  245.2 255.2 %all-gather.8.cloned.1.call-start = ((), (), s32[]{:S(2)}) async-start(), calls=%async_computation.11 | async-start | bytes 4456448 | tf_op jit(solution)/shard_map/all_gather | solution.py:991
  245.2 35.7 %collective-permute-start.23 = (bf16[4,2,128,512]{3,2,0,1:T(8,128)(2,1)S(1)}, bf16[4,2,128,512]{3,2,0,1:T(8,128)(2,1)S(1)}, u32[]{:S(2)}, u32[]{:S(2)}) collective-permute-start(bf16[4,2,128,512]{3,2,0,1:T(8,128)(2,1)S(1)} %pad_maximum_fusion.9), channel_id=1, source_target_pairs={{0,2},{2,0},{4,6},{6,4},{8,10},{10,8},{12,14},{14,12},{16,18},{18,... | collective-permute-start | bytes 3145736 | tf_op jit(solution)/shard_map/ppermute | solution.py:438
  246.6 34.8 %collective-permute-start.22 = (bf16[4,2,128,512]{3,2,0,1:T(8,128)(2,1)}, bf16[4,2,128,512]{3,2,0,1:T(8,128)(2,1)S(1)}, u32[]{:S(2)}, u32[]{:S(2)}) collective-permute-start(bf16[4,2,128,512]{3,2,0,1:T(8,128)(2,1)} %pad_maximum_fusion.8), channel_id=1, source_target_pairs={{0,4},{2,6},{4,0},{6,2},{8,12},{10,14},{12,8},{14,10},{16,20},{18,... | collective-permute-start | bytes 3145736 | tf_op jit(solution)/shard_map/ppermute | solution.py:438
  350.3 32.1 %collective-permute-start.37 = (bf16[4,2,128,512]{3,2,0,1:T(8,128)(2,1)}, bf16[4,2,128,512]{3,2,0,1:T(8,128)(2,1)}, u32[]{:S(2)}, u32[]{:S(2)}) collective-permute-start(bf16[4,2,128,512]{3,2,0,1:T(8,128)(2,1)} %bitcast.354), channel_id=1, source_target_pairs={{0,2},{2,0},{4,6},{6,4},{8,10},{10,8},{12,14},{14,12},{16,18},{18,... | collective-permute-start | bytes 3145736 | tf_op jit(solution)/shard_map/ppermute | solution.py:438
  352.8 33.3 %collective-permute-start.36 = (bf16[4,2,128,512]{3,2,0,1:T(8,128)(2,1)}, bf16[4,2,128,512]{3,2,0,1:T(8,128)(2,1)}, u32[]{:S(2)}, u32[]{:S(2)}) collective-permute-start(bf16[4,2,128,512]{3,2,0,1:T(8,128)(2,1)} %bitcast.355), channel_id=1, source_target_pairs={{0,4},{2,6},{4,0},{6,2},{8,12},{10,14},{12,8},{14,10},{16,20},{18,... | collective-permute-start | bytes 3145736 | tf_op jit(solution)/shard_map/ppermute | solution.py:438
  363.3 53.1 %all-to-all-start.4 = ((bf16[16,128,256]{2,1,0:T(8,128)(2,1)}), bf16[16,128,256]{2,1,0:T(8,128)(2,1)}, u32[]{:S(2)}, u32[]{:S(2)}) async-start(bf16[16,128,256]{2,1,0:T(8,128)(2,1)} %bitcast.390), calls=%async_computation.4 | async-start | bytes 2097152 | tf_op jit(solution)/shard_map/all_to_all | solution.py:849
  389.8 62.8 %collective-permute-start.44 = (bf16[2048,512]{1,0:T(8,128)(2,1)}, bf16[2048,512]{1,0:T(8,128)(2,1)}, u32[]{:S(2)}, u32[]{:S(2)}) collective-permute-start(bf16[2048,512]{1,0:T(8,128)(2,1)} %convolution_convert_fusion.2), channel_id=1, source_target_pairs={{0,1},{1,0},{2,3},{3,2},{4,5},{5,4},{6,7},{7,6},{8,9},{9,8},{10,11... | collective-permute-start | bytes 6291464 | tf_op jit(solution)/shard_map/ppermute | solution.py:437
  397.0 58.0 %collective-permute-start.43 = (bf16[2048,512]{1,0:T(8,128)(2,1)}, bf16[2048,512]{1,0:T(8,128)(2,1)}, u32[]{:S(2)}, u32[]{:S(2)}) collective-permute-start(bf16[2048,512]{1,0:T(8,128)(2,1)} %convolution_convert_fusion.3), channel_id=1, source_target_pairs={{0,1},{1,0},{2,3},{3,2},{4,5},{5,4},{6,7},{7,6},{8,9},{9,8},{10,11... | collective-permute-start | bytes 6291464 | tf_op jit(solution)/shard_map/ppermute | solution.py:437
  464.1 34.7 %collective-permute-start.48 = (bf16[4,2,128,512]{3,2,0,1:T(8,128)(2,1)}, bf16[4,2,128,512]{3,2,0,1:T(8,128)(2,1)}, u32[]{:S(2)}, u32[]{:S(2)}) collective-permute-start(bf16[4,2,128,512]{3,2,0,1:T(8,128)(2,1)} %bitcast.353), channel_id=1, source_target_pairs={{0,4},{2,6},{4,0},{6,2},{8,12},{10,14},{12,8},{14,10},{16,20},{18,... | collective-permute-start | bytes 3145736 | tf_op jit(solution)/shard_map/ppermute | solution.py:438
  464.1 36.2 %all-to-all-start.5 = ((bf16[16,128,256]{2,1,0:T(8,128)(2,1)}), bf16[16,128,256]{2,1,0:T(8,128)(2,1)}, u32[]{:S(2)}, u32[]{:S(2)}) async-start(bf16[16,128,256]{2,1,0:T(8,128)(2,1)} %bitcast.87), calls=%async_computation.5 | async-start | bytes 2097152 | tf_op jit(solution)/shard_map/all_to_all | solution.py:849
  589.7 31.0 %collective-permute-start.57 = (bf16[4,2,128,512]{3,2,0,1:T(8,128)(2,1)}, bf16[4,2,128,512]{3,2,0,1:T(8,128)(2,1)}, u32[]{:S(2)}, u32[]{:S(2)}) collective-permute-start(bf16[4,2,128,512]{3,2,0,1:T(8,128)(2,1)} %bitcast.351), channel_id=1, source_target_pairs={{0,4},{2,6},{4,0},{6,2},{8,12},{10,14},{12,8},{14,10},{16,20},{18,... | collective-permute-start | bytes 3145736 | tf_op jit(solution)/shard_map/ppermute | solution.py:438
  592.4 31.1 %collective-permute-start.60 = (bf16[4,2,128,512]{3,2,0,1:T(8,128)(2,1)}, bf16[4,2,128,512]{3,2,0,1:T(8,128)(2,1)}, u32[]{:S(2)}, u32[]{:S(2)}) collective-permute-start(bf16[4,2,128,512]{3,2,0,1:T(8,128)(2,1)} %bitcast.350), channel_id=1, source_target_pairs={{0,2},{2,0},{4,6},{6,4},{8,10},{10,8},{12,14},{14,12},{16,18},{18,... | collective-permute-start | bytes 3145736 | tf_op jit(solution)/shard_map/ppermute | solution.py:438
  595.0 45.8 %collective-permute-start.55 = (f32[128,1024]{1,0:T(8,128)S(1)}, f32[128,1024]{1,0:T(8,128)}, u32[]{:S(2)}, u32[]{:S(2)}) collective-permute-start(f32[128,1024]{1,0:T(8,128)S(1)} %fusion.17), channel_id=1, source_target_pairs={{0,1},{1,0},{2,3},{3,2},{4,5},{5,4},{6,7},{7,6},{8,9},{9,8},{10,11... | collective-permute-start | bytes 1572872 | tf_op jit(solution)/shard_map/ppermute | solution.py:437
  596.6 40.6 %all-to-all-start.8 = ((bf16[16,192,128]{2,1,0:T(8,128)(2,1)}), bf16[16,192,128]{2,1,0:T(8,128)(2,1)}, u32[]{:S(2)}, u32[]{:S(2)}) async-start(bf16[16,192,128]{2,1,0:T(8,128)(2,1)} %bitcast_bitcast_fusion.2), calls=%async_computation.8 | async-start | bytes 1572864 | tf_op jit(solution)/shard_map/all_to_all | solution.py:849
  (134 other events, 2292.1 us)
Sparse Core Ops, SparseCore 0:
  10.8 115.3 all-gather.3
  129.6 106.4 all-gather.5
  338.8 113.5 all-gather.7

commit v4 on v3

--- a/solution.py
+++ b/solution.py
@@ -1007,7 +1007,7 @@
     shrink_term = by_row_owner(
         [dot(piece, shrink_far, CONTRACT_FIRST).astype(BF) for piece in low_out], side
     )
-    halves, shrink_in = after(scatter_wide(pair), shrink_in)
+    halves, shrink_in, low_raised = after(scatter_wide(pair), shrink_in, low_raised)
     slabs, shrink_moved = after(scatter_narrow(halves), to_owners(shrink_term))
     shrink_grad = rows_of(shrink_moved)
     second_grad = scatter_column(slabs)

time: 700 us -> 702 us (level)
    unnamed x143 -> x141, local copies, waits for them, and re-layouts: 16.6 us -> 16.7 us
  transfers between devices with their start and end apart: 92 -> 92, of which waited for: 40 -> 43; matrix products, arithmetic and copies ran while one was open for 21% -> 21% of each run, Pallas kernels for 3% -> 3%
where the time goes in v4:
time: 702 us; the launch traced here: 692 us
  waiting for transfers between devices  281 us (40%)
  starting transfers between devices  175 us (25%)
  matrix products  56.1 us (8%)
  local copies, waits for them, and re-layouts  51.3 us (7%)
  other arithmetic  46.9 us (7%)
  Pallas kernels  38.7 us (6%)
  blocking collectives  27.1 us (4%)
  between operations  15.9 us (2%)
    ppermute x58, waiting for transfers between devices, hop(): return lax.ppermute(values, 'seq', HOPS[way])  251 us
    ppermute x58, starting transfers between devices, hop(): return lax.ppermute(values, 'seq', HOPS[way])  68.6 us
    all_to_all x8, starting transfers between devices, to_owners(): lax.all_to_all(values, 'seq', split_axis=0, concat_axis=0, tiled=True)  65.9 us
    dot_general x25, matrix products, dot(): return lax.dot_general(first, second, dims, preferred_element_type=F32)  56.1 us
    ppermute x23, starting transfers between devices, hop(): return lax.ppermute(values, 'tp', [(0, 1), (1, 0)])  40.4 us
    all_to_all x1, blocking collectives, to_owners(): lax.all_to_all(values, 'seq', split_axis=0, concat_axis=0, tiled=True)  27.1 us
    unnamed x141, local copies, waits for them, and re-layouts  16.7 us
    all_to_all x8, waiting for transfers between devices, to_owners(): lax.all_to_all(values, 'seq', split_axis=0, concat_axis=0, tiled=True)  15.3 us
  transfers between devices with their start and end apart: 92, of which 43 were waited for; matrix products, arithmetic and copies ran while one was open for 21% of the time, Pallas kernels for 3%

profile of v4, /device:TPU:1, one launch (start us, length us, event | category | flops | bytes accessed | tf_op | source)
XLA Modules:
  0.0 692.0 jit_solution(7527653744902009654)
XLA Ops:
  25.1 15.9 %collective-permute-done.1 = bf16[128,1024]{1,0:T(8,128)(2,1)S(1)} collective-permute-done((bf16[128,1024]{1,0:T(8,128)(2,1)S(1)}, bf16[128,1024]{1,0:T(8,128)(2,1)S(1)}, u32[]{:S(2)}, u32[]{:S(2)}) %collective-permute-start.1) | collective-permute-done | bytes 262176 | tf_op jit(solution)/shard_map/ppermute | solution.py:438
  45.3 11.2 %collective-permute-done.5 = bf16[4,128,512]{2,1,0:T(8,128)(2,1)S(1)} collective-permute-done((bf16[4,128,512]{2,1,0:T(8,128)(2,1)S(1)}, bf16[4,128,512]{2,1,0:T(8,128)(2,1)S(1)}, u32[]{:S(2)}, u32[]{:S(2)}) %collective-permute-start.5) | collective-permute-done | bytes 524320 | tf_op jit(solution)/shard_map/ppermute | solution.py:438
  62.8 13.3 %all-to-all-start = ((bf16[16,192,128]{2,1,0:T(8,128)(2,1)}), bf16[16,192,128]{2,1,0:T(8,128)(2,1)}, u32[]{:S(2)}, u32[]{:S(2)}) async-start(bf16[16,192,128]{2,1,0:T(8,128)(2,1)} %bitcast.6), calls=%async_computation | async-start | bytes 1572864 | tf_op jit(solution)/shard_map/all_to_all | solution.py:849
  76.1 17.7 %collective-permute-done.6 = bf16[4,2,128,512]{3,2,0,1:T(8,128)(2,1)} collective-permute-done((bf16[4,2,128,512]{3,2,0,1:T(8,128)(2,1)}, bf16[4,2,128,512]{3,2,0,1:T(8,128)(2,1)}, u32[]{:S(2)}, u32[]{:S(2)}) %collective-permute-start.6) | collective-permute-done | bytes 1048608 | tf_op jit(solution)/shard_map/ppermute | solution.py:438
  96.9 10.4 %collective-permute-start.8 = (bf16[2048,512]{1,0:T(8,128)(2,1)}, bf16[2048,512]{1,0:T(8,128)(2,1)}, u32[]{:S(2)}, u32[]{:S(2)}) collective-permute-start(bf16[2048,512]{1,0:T(8,128)(2,1)} %bitcast.16.second_ref), channel_id=1, source_target_pairs={{0,1},{1,0},{2,3},{3,2},{4,5},{5,4},{6,7},{7,6},{8,9},{9,8},{10,11... | collective-permute-start | bytes 6291464 | tf_op jit(solution)/shard_map/ppermute | solution.py:437
  114.2 12.4 %shard_map.322 = (bf16[192,2048]{1,0:T(8,128)(2,1)S(1)}, f32[16,64,128]{2,1,0:T(8,128)S(1)}, bf16[16,80,128]{2,1,0:T(8,128)(2,1)S(1)}, f32[1,2048]{1,0:T(1,128)S(1)}) custom-call(s32[16]{0:T(128)S(1)} %fusion.37.order_ref, bf16[2048,512]{1,0:T(8,128)(2,1)S(1)} %bitcast.361, bf16[2048,512]{1,0:T(8,128)(2,1)} %bitcast.16.second_ref, ...), custom_call_target="tpu_custom_call" | custom-call | flops 536870912 | bytes 8388608 | tf_op jit(solution)/shard_map/pallas_call | solution.py:702
  127.5 27.1 %all_to_all.45 = bf16[16,80,128]{2,1,0:T(8,128)(2,1)S(1)} all-to-all(bf16[16,80,128]{2,1,0:T(8,128)(2,1)S(1)} %get-tuple-element.83), channel_id=1, replica_groups=mesh['seq'=16,'tp'=2] {'seq'}, dimensions={0} | all-to-all | bytes 655360 | tf_op jit(solution)/shard_map/all_to_all | solution.py:849
  168.8 10.2 %collective-permute-done.17 = bf16[128,1024]{1,0:T(8,128)(2,1)S(1)} collective-permute-done((bf16[128,1024]{1,0:T(8,128)(2,1)S(1)}, bf16[128,1024]{1,0:T(8,128)(2,1)S(1)}, u32[]{:S(2)}, u32[]{:S(2)}) %collective-permute-start.17) | collective-permute-done | bytes 262176 | tf_op jit(solution)/shard_map/ppermute | solution.py:438
  179.0 11.5 %collective-permute-done.18 = bf16[128,1024]{1,0:T(8,128)(2,1)S(1)} collective-permute-done((bf16[128,1024]{1,0:T(8,128)(2,1)S(1)}, bf16[128,1024]{1,0:T(8,128)(2,1)S(1)}, u32[]{:S(2)}, u32[]{:S(2)}) %collective-permute-start.18) | collective-permute-done | bytes 262176 | tf_op jit(solution)/shard_map/ppermute | solution.py:438
  190.7 14.0 %all-to-all-start.2 = ((bf16[16,128,256]{2,1,0:T(8,128)(2,1)}), bf16[16,128,256]{2,1,0:T(8,128)(2,1)S(1)}, u32[]{:S(2)}, u32[]{:S(2)}) async-start(bf16[16,128,256]{2,1,0:T(8,128)(2,1)} %bitcast.391), calls=%async_computation.2 | async-start | bytes 2097152 | tf_op jit(solution)/shard_map/all_to_all | solution.py:849
  208.6 16.8 %collective-permute-done.21 = bf16[4,128,512]{2,1,0:T(8,128)(2,1)S(1)} collective-permute-done((bf16[4,128,512]{2,1,0:T(8,128)(2,1)S(1)}, bf16[4,128,512]{2,1,0:T(8,128)(2,1)S(1)}, u32[]{:S(2)}, u32[]{:S(2)}) %collective-permute-start.21) | collective-permute-done | bytes 524320 | tf_op jit(solution)/shard_map/ppermute | solution.py:438
  226.6 11.0 %all-to-all-done.2 = bf16[16,128,256]{2,1,0:T(8,128)(2,1)S(1)} async-done(((bf16[16,128,256]{2,1,0:T(8,128)(2,1)}), bf16[16,128,256]{2,1,0:T(8,128)(2,1)S(1)}, u32[]{:S(2)}, u32[]{:S(2)}) %all-to-all-start.2) | async-done | bytes 1048608 | tf_op jit(solution)/shard_map/all_to_all | solution.py:849
  238.4 6.8 all-to-all-start.3
  250.3 30.7 %collective-permute-done.23 = bf16[4,2,128,512]{3,2,0,1:T(8,128)(2,1)S(1)} collective-permute-done((bf16[4,2,128,512]{3,2,0,1:T(8,128)(2,1)S(1)}, bf16[4,2,128,512]{3,2,0,1:T(8,128)(2,1)S(1)}, u32[]{:S(2)}, u32[]{:S(2)}) %collective-permute-start.23) | collective-permute-done | bytes 1048608 | tf_op jit(solution)/shard_map/ppermute | solution.py:438
  300.8 8.8 %shard_map.323 = (f32[2048,256]{1,0:T(8,128)S(1)}, f32[2048,256]{1,0:T(8,128)S(1)}, f32[8,2048]{1,0:T(8,128)S(1)}) custom-call(bf16[2048,512]{1,0:T(8,128)(2,1)} %bitcast.375, bf16[2048,512]{1,0:T(8,128)(2,1)} %bitcast.372, bf16[2048,512]{1,0:T(8,128)(2,1)} %collective-permute-done.25.third_ref, bf16[2048,512]{1,0:T(8,128)(2,1)} %collective-permute-done.26.fourth_ref, ...), custom_call_target="tpu_custom_call" | custom-call | flops 2147483648 | bytes 25165824 | tf_op jit(solution)/shard_map/pallas_call | solution.py:813
  326.3 8.9 %shard_map.324 = (bf16[2048,256]{1,0:T(8,128)(2,1)S(1)}, bf16[2048,256]{1,0:T(8,128)(2,1)S(1)}, bf16[2048,512]{1,0:T(8,128)(2,1)}, bf16[2048,512]{1,0:T(8,128)(2,1)}, f32[8,256]{1,0:T(8,128)S(1)}) custom-call(f32[2048,256]{1,0:T(8,128)} %copy-done.4, f32[2048,256]{1,0:T(8,128)} %copy-done.5, f32[2048,256]{1,0:T(8,128)} %bitcast.378, ...), custom_call_target="tpu_custom_call" | custom-call | flops 1073741824 | bytes 12582912 | tf_op jit(solution)/shard_map/pallas_call | solution.py:834
  361.5 14.9 %all-to-all-start.4 = ((bf16[16,128,256]{2,1,0:T(8,128)(2,1)}), bf16[16,128,256]{2,1,0:T(8,128)(2,1)}, u32[]{:S(2)}, u32[]{:S(2)}) async-start(bf16[16,128,256]{2,1,0:T(8,128)(2,1)} %bitcast.390), calls=%async_computation.4 | async-start | bytes 2097152 | tf_op jit(solution)/shard_map/all_to_all | solution.py:849
  401.8 18.2 %collective-permute-done.38 = bf16[4,128,512]{2,1,0:T(8,128)(2,1)S(1)} collective-permute-done((bf16[4,128,512]{2,1,0:T(8,128)(2,1)S(1)}, bf16[4,128,512]{2,1,0:T(8,128)(2,1)S(1)}, u32[]{:S(2)}, u32[]{:S(2)}) %collective-permute-start.38) | collective-permute-done | bytes 524320 | tf_op jit(solution)/shard_map/ppermute | solution.py:438
  433.2 21.8 %collective-permute-done.41 = bf16[128,1024]{1,0:T(8,128)(2,1)S(1)} collective-permute-done((bf16[128,1024]{1,0:T(8,128)(2,1)S(1)}, bf16[128,1024]{1,0:T(8,128)(2,1)S(1)}, u32[]{:S(2)}, u32[]{:S(2)}) %collective-permute-start.41) | collective-permute-done | bytes 262176 | tf_op jit(solution)/shard_map/ppermute | solution.py:438
  480.3 16.1 %collective-permute-done.49 = bf16[4,2,128,512]{3,2,0,1:T(8,128)(2,1)} collective-permute-done((bf16[4,2,128,512]{3,2,0,1:T(8,128)(2,1)}, bf16[4,2,128,512]{3,2,0,1:T(8,128)(2,1)}, u32[]{:S(2)}, u32[]{:S(2)}) %collective-permute-start.49) | collective-permute-done | bytes 1048608 | tf_op jit(solution)/shard_map/ppermute | solution.py:438
  533.5 8.6 %shard_map.325 = (bf16[192,2048]{1,0:T(8,128)(2,1)S(1)}, f32[192,1]{1,0:T(8,128)S(1)}) custom-call(s32[16]{0:T(128)S(1)} %fusion.37.order_ref, bf16[192,2048]{1,0:T(8,128)(2,1)S(1)} %copy-done.9, bf16[16,64,128]{2,1,0:T(8,128)(2,1)S(1)} %all-to-all-done.6.pull_ref, f32[16,64,128]{2,1,0:T(8,128)S(1)} %copy-done.11, f32[1,2048]{1,0:T(1,128)S(1)} %get-tuple-element.125.log_ref, ...), custom_call_target="tpu_custom_call" | custom-call | flops 1342177280 | bytes 3145728 | tf_op jit(solution)/shard_map/pallas_call | solution.py:733
  604.3 15.8 %collective-permute-done.57 = bf16[4,2,128,512]{3,2,0,1:T(8,128)(2,1)} collective-permute-done((bf16[4,2,128,512]{3,2,0,1:T(8,128)(2,1)}, bf16[4,2,128,512]{3,2,0,1:T(8,128)(2,1)}, u32[]{:S(2)}, u32[]{:S(2)}) %collective-permute-start.57) | collective-permute-done | bytes 1048608 | tf_op jit(solution)/shard_map/ppermute | solution.py:438
  630.6 8.1 %collective-permute-done.58 = bf16[4,128,512]{2,1,0:T(8,128)(2,1)S(1)} collective-permute-done((bf16[4,128,512]{2,1,0:T(8,128)(2,1)S(1)}, bf16[4,128,512]{2,1,0:T(8,128)(2,1)S(1)}, u32[]{:S(2)}, u32[]{:S(2)}) %collective-permute-start.58) | collective-permute-done | bytes 524320 | tf_op jit(solution)/shard_map/ppermute | solution.py:438
  646.3 18.2 %collective-permute-done.63 = bf16[128,1024]{1,0:T(8,128)(2,1)S(1)} collective-permute-done((bf16[128,1024]{1,0:T(8,128)(2,1)S(1)}, bf16[128,1024]{1,0:T(8,128)(2,1)S(1)}, u32[]{:S(2)}, u32[]{:S(2)}) %collective-permute-start.63) | collective-permute-done | bytes 262176 | tf_op jit(solution)/shard_map/ppermute | solution.py:438
  (517 shorter events, 327.6 us)
Async XLA Ops:
  7.2 149.2 %all-gather.4.cloned.1.call-start = ((), (), s32[]{:S(2)}) async-start(), calls=%async_computation.9 | async-start | bytes 4456448 | tf_op jit(solution)/shard_map/all_gather | solution.py:911
  7.9 229.7 %all-gather.6.cloned.1.call-start = ((), (), s32[]{:S(2)}) async-start(), calls=%async_computation.10 | async-start | bytes 4456448 | tf_op jit(solution)/shard_map/all_gather | solution.py:913
  8.0 37.0 %collective-permute-start.9 = (s32[1,128]{1,0:T(1,128)}, s32[1,128]{1,0:T(1,128)S(1)}, u32[]{:S(2)}, u32[]{:S(2)}) collective-permute-start(s32[1,128]{1,0:T(1,128)} %bitcast.467), channel_id=1, source_target_pairs={{0,8},{2,10},{4,12},{6,14},{8,16},{10,18},{12,20},{14,22},{16,24},... | collective-permute-start | bytes 1544 | tf_op jit(solution)/shard_map/ppermute | solution.py:438
  10.2 34.8 %collective-permute-start.10 = (s32[1,128]{1,0:T(1,128)}, s32[1,128]{1,0:T(1,128)S(1)}, u32[]{:S(2)}, u32[]{:S(2)}) collective-permute-start(s32[1,128]{1,0:T(1,128)} %bitcast.468), channel_id=1, source_target_pairs={{0,16},{2,18},{4,20},{6,22},{8,24},{10,26},{12,28},{14,30},{16,0},... | collective-permute-start | bytes 1544 | tf_op jit(solution)/shard_map/ppermute | solution.py:438
  57.6 36.2 %collective-permute-start.6 = (bf16[4,2,128,512]{3,2,0,1:T(8,128)(2,1)}, bf16[4,2,128,512]{3,2,0,1:T(8,128)(2,1)}, u32[]{:S(2)}, u32[]{:S(2)}) collective-permute-start(bf16[4,2,128,512]{3,2,0,1:T(8,128)(2,1)} %get-tuple-element.263), channel_id=1, source_target_pairs={{0,2},{2,0},{4,6},{6,4},{8,10},{10,8},{12,14},{14,12},{16,18},{18,... | collective-permute-start | bytes 3145736 | tf_op jit(solution)/shard_map/ppermute | solution.py:438
  61.5 45.8 %collective-permute-start.4 = (bf16[4,2,128,512]{3,2,0,1:T(8,128)(2,1)}, bf16[4,2,128,512]{3,2,0,1:T(8,128)(2,1)S(1)}, u32[]{:S(2)}, u32[]{:S(2)}) collective-permute-start(bf16[4,2,128,512]{3,2,0,1:T(8,128)(2,1)} %get-tuple-element.269), channel_id=1, source_target_pairs={{0,4},{2,6},{4,0},{6,2},{8,12},{10,14},{12,8},{14,10},{16,20},{18,... | collective-permute-start | bytes 3145736 | tf_op jit(solution)/shard_map/ppermute | solution.py:438
  62.8 48.3 %all-to-all-start = ((bf16[16,192,128]{2,1,0:T(8,128)(2,1)}), bf16[16,192,128]{2,1,0:T(8,128)(2,1)}, u32[]{:S(2)}, u32[]{:S(2)}) async-start(bf16[16,192,128]{2,1,0:T(8,128)(2,1)} %bitcast.6), calls=%async_computation | async-start | bytes 1572864 | tf_op jit(solution)/shard_map/all_to_all | solution.py:849
  190.7 47.0 %all-to-all-start.2 = ((bf16[16,128,256]{2,1,0:T(8,128)(2,1)}), bf16[16,128,256]{2,1,0:T(8,128)(2,1)S(1)}, u32[]{:S(2)}, u32[]{:S(2)}) async-start(bf16[16,128,256]{2,1,0:T(8,128)(2,1)} %bitcast.391), calls=%async_computation.2 | async-start | bytes 2097152 | tf_op jit(solution)/shard_map/all_to_all | solution.py:849
  237.6 46.7 %collective-permute-start.24 = (bf16[2048,1024]{1,0:T(8,128)(2,1)}, bf16[2048,1024]{1,0:T(8,128)(2,1)}, u32[]{:S(2)}, u32[]{:S(2)}) collective-permute-start(bf16[2048,1024]{1,0:T(8,128)(2,1)} %all-gather.6.cloned.1.call-done), channel_id=1, source_target_pairs={{0,1},{1,0},{2,3},{3,2},{4,5},{5,4},{6,7},{7,6},{8,9},{9,8},{10,11... | collective-permute-start | bytes 12582920 | tf_op jit(solution)/shard_map/ppermute | solution.py:437
  238.4 54.4 %all-to-all-start.3 = ((bf16[16,128,256]{2,1,0:T(8,128)(2,1)}), bf16[16,128,256]{2,1,0:T(8,128)(2,1)}, u32[]{:S(2)}, u32[]{:S(2)}) async-start(bf16[16,128,256]{2,1,0:T(8,128)(2,1)} %bitcast.347), calls=%async_computation.3 | async-start | bytes 2097152 | tf_op jit(solution)/shard_map/all_to_all | solution.py:849
  245.2 259.5 %all-gather.8.cloned.1.call-start = ((), (), s32[]{:S(2)}) async-start(), calls=%async_computation.11 | async-start | bytes 4456448 | tf_op jit(solution)/shard_map/all_gather | solution.py:991
  245.3 35.7 %collective-permute-start.23 = (bf16[4,2,128,512]{3,2,0,1:T(8,128)(2,1)S(1)}, bf16[4,2,128,512]{3,2,0,1:T(8,128)(2,1)S(1)}, u32[]{:S(2)}, u32[]{:S(2)}) collective-permute-start(bf16[4,2,128,512]{3,2,0,1:T(8,128)(2,1)S(1)} %pad_maximum_fusion.9), channel_id=1, source_target_pairs={{0,2},{2,0},{4,6},{6,4},{8,10},{10,8},{12,14},{14,12},{16,18},{18,... | collective-permute-start | bytes 3145736 | tf_op jit(solution)/shard_map/ppermute | solution.py:438
  246.7 34.8 %collective-permute-start.22 = (bf16[4,2,128,512]{3,2,0,1:T(8,128)(2,1)}, bf16[4,2,128,512]{3,2,0,1:T(8,128)(2,1)S(1)}, u32[]{:S(2)}, u32[]{:S(2)}) collective-permute-start(bf16[4,2,128,512]{3,2,0,1:T(8,128)(2,1)} %pad_maximum_fusion.8), channel_id=1, source_target_pairs={{0,4},{2,6},{4,0},{6,2},{8,12},{10,14},{12,8},{14,10},{16,20},{18,... | collective-permute-start | bytes 3145736 | tf_op jit(solution)/shard_map/ppermute | solution.py:438
  350.1 31.9 %collective-permute-start.37 = (bf16[4,2,128,512]{3,2,0,1:T(8,128)(2,1)}, bf16[4,2,128,512]{3,2,0,1:T(8,128)(2,1)}, u32[]{:S(2)}, u32[]{:S(2)}) collective-permute-start(bf16[4,2,128,512]{3,2,0,1:T(8,128)(2,1)} %bitcast.354), channel_id=1, source_target_pairs={{0,2},{2,0},{4,6},{6,4},{8,10},{10,8},{12,14},{14,12},{16,18},{18,... | collective-permute-start | bytes 3145736 | tf_op jit(solution)/shard_map/ppermute | solution.py:438
  361.5 59.0 %all-to-all-start.4 = ((bf16[16,128,256]{2,1,0:T(8,128)(2,1)}), bf16[16,128,256]{2,1,0:T(8,128)(2,1)}, u32[]{:S(2)}, u32[]{:S(2)}) async-start(bf16[16,128,256]{2,1,0:T(8,128)(2,1)} %bitcast.390), calls=%async_computation.4 | async-start | bytes 2097152 | tf_op jit(solution)/shard_map/all_to_all | solution.py:849
  389.7 65.4 %collective-permute-start.44 = (bf16[2048,512]{1,0:T(8,128)(2,1)}, bf16[2048,512]{1,0:T(8,128)(2,1)}, u32[]{:S(2)}, u32[]{:S(2)}) collective-permute-start(bf16[2048,512]{1,0:T(8,128)(2,1)} %convolution_convert_fusion.2), channel_id=1, source_target_pairs={{0,1},{1,0},{2,3},{3,2},{4,5},{5,4},{6,7},{7,6},{8,9},{9,8},{10,11... | collective-permute-start | bytes 6291464 | tf_op jit(solution)/shard_map/ppermute | solution.py:437
  392.8 64.7 %collective-permute-start.43 = (bf16[2048,512]{1,0:T(8,128)(2,1)}, bf16[2048,512]{1,0:T(8,128)(2,1)}, u32[]{:S(2)}, u32[]{:S(2)}) collective-permute-start(bf16[2048,512]{1,0:T(8,128)(2,1)} %convolution_convert_fusion.3), channel_id=1, source_target_pairs={{0,1},{1,0},{2,3},{3,2},{4,5},{5,4},{6,7},{7,6},{8,9},{9,8},{10,11... | collective-permute-start | bytes 6291464 | tf_op jit(solution)/shard_map/ppermute | solution.py:437
  464.6 31.8 %collective-permute-start.49 = (bf16[4,2,128,512]{3,2,0,1:T(8,128)(2,1)}, bf16[4,2,128,512]{3,2,0,1:T(8,128)(2,1)}, u32[]{:S(2)}, u32[]{:S(2)}) collective-permute-start(bf16[4,2,128,512]{3,2,0,1:T(8,128)(2,1)} %bitcast.352), channel_id=1, source_target_pairs={{0,2},{2,0},{4,6},{6,4},{8,10},{10,8},{12,14},{14,12},{16,18},{18,... | collective-permute-start | bytes 3145736 | tf_op jit(solution)/shard_map/ppermute | solution.py:438
  468.4 34.7 %collective-permute-start.48 = (bf16[4,2,128,512]{3,2,0,1:T(8,128)(2,1)}, bf16[4,2,128,512]{3,2,0,1:T(8,128)(2,1)}, u32[]{:S(2)}, u32[]{:S(2)}) collective-permute-start(bf16[4,2,128,512]{3,2,0,1:T(8,128)(2,1)} %bitcast.353), channel_id=1, source_target_pairs={{0,4},{2,6},{4,0},{6,2},{8,12},{10,14},{12,8},{14,10},{16,20},{18,... | collective-permute-start | bytes 3145736 | tf_op jit(solution)/shard_map/ppermute | solution.py:438
  469.5 35.2 %all-to-all-start.5 = ((bf16[16,128,256]{2,1,0:T(8,128)(2,1)}), bf16[16,128,256]{2,1,0:T(8,128)(2,1)}, u32[]{:S(2)}, u32[]{:S(2)}) async-start(bf16[16,128,256]{2,1,0:T(8,128)(2,1)} %bitcast.87), calls=%async_computation.5 | async-start | bytes 2097152 | tf_op jit(solution)/shard_map/all_to_all | solution.py:849
  555.3 31.7 %collective-permute-start.56 = (bf16[2048,512]{1,0:T(8,128)(2,1)}, bf16[2048,512]{1,0:T(8,128)(2,1)}, u32[]{:S(2)}, u32[]{:S(2)}) collective-permute-start(bf16[2048,512]{1,0:T(8,128)(2,1)} %convolution_convert_fusion.1), channel_id=1, source_target_pairs={{0,1},{1,0},{2,3},{3,2},{4,5},{5,4},{6,7},{7,6},{8,9},{9,8},{10,11... | collective-permute-start | bytes 6291464 | tf_op jit(solution)/shard_map/ppermute | solution.py:437
  594.0 31.5 %collective-permute-start.60 = (bf16[4,2,128,512]{3,2,0,1:T(8,128)(2,1)}, bf16[4,2,128,512]{3,2,0,1:T(8,128)(2,1)}, u32[]{:S(2)}, u32[]{:S(2)}) collective-permute-start(bf16[4,2,128,512]{3,2,0,1:T(8,128)(2,1)} %bitcast.350), channel_id=1, source_target_pairs={{0,2},{2,0},{4,6},{6,4},{8,10},{10,8},{12,14},{14,12},{16,18},{18,... | collective-permute-start | bytes 3145736 | tf_op jit(solution)/shard_map/ppermute | solution.py:438
  598.1 45.1 %collective-permute-start.55 = (f32[128,1024]{1,0:T(8,128)S(1)}, f32[128,1024]{1,0:T(8,128)}, u32[]{:S(2)}, u32[]{:S(2)}) collective-permute-start(f32[128,1024]{1,0:T(8,128)S(1)} %fusion.17), channel_id=1, source_target_pairs={{0,1},{1,0},{2,3},{3,2},{4,5},{5,4},{6,7},{7,6},{8,9},{9,8},{10,11... | collective-permute-start | bytes 1572872 | tf_op jit(solution)/shard_map/ppermute | solution.py:437
  599.7 39.8 %all-to-all-start.8 = ((bf16[16,192,128]{2,1,0:T(8,128)(2,1)}), bf16[16,192,128]{2,1,0:T(8,128)(2,1)}, u32[]{:S(2)}, u32[]{:S(2)}) async-start(bf16[16,192,128]{2,1,0:T(8,128)(2,1)} %bitcast_bitcast_fusion.2), calls=%async_computation.8 | async-start | bytes 1572864 | tf_op jit(solution)/shard_map/all_to_all | solution.py:849
  (133 other events, 2286.7 us)
Sparse Core Ops, SparseCore 0:
  10.8 115.3 all-gather.3
  129.6 106.6 all-gather.5
  338.6 115.9 all-gather.7
